TPU v7x, 32 devices: a whole 2x2x4 slice. The times are simulated.
32 devices in a mesh: seq: 8 (over y, x, core), dp: 4 (over z).
Axes of the slice: x: 2, y: 2, z: 4, core: 2. Of those that a mesh axis runs over, the one named last changes fastest.
Arguments:
- layer_input: bfloat16 [4, 2048, 4096], P('dp', None, 'seq'), may hold values from -6 to 6
- query_proj: bfloat16 [4, 2048, 512], P('dp', 'seq'), may hold values from -6 to 6
- key_proj: bfloat16 [4, 2048, 128], P('dp', 'seq'), may hold values from -6 to 6
- value_proj: bfloat16 [4, 2048, 128], P('dp', 'seq'), may hold values from -6 to 6
- out_grad: bfloat16 [4, 2048, 512], P('dp', 'seq'), may hold values from -1 to 1
- block_pos: int32 [4, 16], P('dp'), may hold values from 0 to 15, each once within a row
- doc_ids: int32 [4, 16], P('dp'), may hold values from 0 to 7, never falling along the last dimension, each value on 1 to 4 neighbouring positions
Outputs:
- weight_grad: float32 [4096, 768], P(('seq', 'dp'))
Inputs may be any that keep to these rules, and one draw needn't show every extreme that they name: Each row is a permutation: storage block j of a sequence holds the tokens of position block block_pos[j] in order. `doc_ids`: along a row the document numbers never fall; each document covers 1 to 4 whole position blocks, and one covers exactly 4.
All inputs are finite; a program needn't handle non-finite values.
Results may differ from a plain program's by a relative error of at most 0.0062.
Values may be sent and summed in bfloat16 or wider, within the bound.
No kernel may reach another device: no remote copies, remote signals or barrier semaphores. Data moves between devices by JAX's collectives and lax.ppermute only.
A program may use at most 64 MiB of HBM per device.

v0:
```python
import jax
import jax.numpy as jnp
from jax import lax
from jax.sharding import PartitionSpec as P

masked_fill = -1e30


def token_labels(pos_row, doc_row, length):
    blocks = pos_row.shape[0]
    block_span = length // blocks
    indices = jnp.arange(blocks, dtype=jnp.int32)
    block_doc = jnp.sum(
        jnp.where(pos_row[:, None] == indices[None, :], doc_row[None, :], 0), axis=1
    )
    offsets = jnp.arange(length, dtype=jnp.int32) % block_span
    token_pos = jnp.repeat(pos_row, block_span) * block_span + offsets
    token_doc = jnp.repeat(block_doc, block_span)
    return (token_pos, token_doc)


def block_terms(
    queries,
    grad_heads,
    key_rows,
    value_rows,
    query_pos,
    query_doc,
    key_pos,
    key_doc,
    scaling,
    block_span,
):
    tok_count, head_count, head_dim = queries.shape
    blocks = key_rows.shape[0] // block_span

    def block_parts(block_id):
        first = block_id * block_span
        key_block = lax.dynamic_slice_in_dim(key_rows, first, block_span)
        value_block = lax.dynamic_slice_in_dim(value_rows, first, block_span)
        block_doc = lax.dynamic_slice_in_dim(key_doc, first, block_span)
        block_pos = lax.dynamic_slice_in_dim(key_pos, first, block_span)
        live_mask = (query_doc[:, None] == block_doc[None, :]) & (
            query_pos[:, None] >= block_pos[None, :]
        )
        return (key_block, value_block, live_mask)

    def guarded(block_id, update, state_in):
        alive = jnp.any(block_parts(block_id)[2])
        return lax.cond(alive, update, lambda unchanged: unchanged, state_in)

    def block_scores(key_block, live_mask):
        scores = (
            jnp.einsum("ihc,jc->hij", queries, key_block, preferred_element_type=jnp.float32)
            * scaling
        )
        return jnp.where(live_mask[None], scores, masked_fill)

    def first_pass(block_id, state_in):

        def update(state_now):
            row_peak, row_total = state_now
            key_block, value_block, live_mask = block_parts(block_id)
            masked = block_scores(key_block, live_mask)
            new_peak = jnp.maximum(row_peak, jnp.max(masked, axis=2, keepdims=True))
            added = jnp.sum(
                jnp.where(live_mask[None], jnp.exp(masked - new_peak), 0.0), axis=2, keepdims=True
            )
            return (new_peak, row_total * jnp.exp(row_peak - new_peak) + added)

        return guarded(block_id, update, state_in)

    start_peak = jnp.full((head_count, tok_count, 1), masked_fill, jnp.float32)
    start_total = jnp.zeros((head_count, tok_count, 1), jnp.float32)
    row_peak, row_total = lax.fori_loop(0, blocks, first_pass, (start_peak, start_total))

    def block_probs(key_block, live_mask):
        masked = block_scores(key_block, live_mask)
        return jnp.where(live_mask[None], jnp.exp(masked - row_peak), 0.0) / row_total

    def second_pass(block_id, attended):

        def update(acc_now):
            key_block, value_block, live_mask = block_parts(block_id)
            probs_b = block_probs(key_block, live_mask).astype(jnp.bfloat16)
            return acc_now + jnp.einsum(
                "hij,jc->hic", probs_b, value_block, preferred_element_type=jnp.float32
            )

        return guarded(block_id, update, attended)

    attended = lax.fori_loop(
        0, blocks, second_pass, jnp.zeros((head_count, tok_count, head_dim), jnp.float32)
    )
    row_delta = jnp.sum(jnp.transpose(grad_heads.astype(jnp.float32), (1, 0, 2)) * attended, axis=2)

    def third_pass(block_id, state_in):

        def update(state_now):
            query_acc, key_part, value_part = state_now
            key_block, value_block, live_mask = block_parts(block_id)
            probs = block_probs(key_block, live_mask)
            probs_b = probs.astype(jnp.bfloat16)
            dprobs = jnp.einsum(
                "ihc,jc->hij", grad_heads, value_block, preferred_element_type=jnp.float32
            )
            dscores = (probs * (dprobs - row_delta[..., None])).astype(jnp.bfloat16)
            query_acc = query_acc + jnp.einsum(
                "hij,jc->ihc", dscores, key_block, preferred_element_type=jnp.float32
            )
            key_new = (
                jnp.einsum("hij,ihc->jc", dscores, queries, preferred_element_type=jnp.float32)
                * scaling
            )
            value_new = jnp.einsum(
                "hij,ihc->jc", probs_b, grad_heads, preferred_element_type=jnp.float32
            )
            first = block_id * block_span
            key_part = lax.dynamic_update_slice_in_dim(key_part, key_new, first, 0)
            value_part = lax.dynamic_update_slice_in_dim(value_part, value_new, first, 0)
            return (query_acc, key_part, value_part)

        return guarded(block_id, update, state_in)

    start_query = jnp.zeros((tok_count, head_count, head_dim), jnp.float32)
    start_keys = jnp.zeros(key_rows.shape, jnp.float32)
    start_values = jnp.zeros(value_rows.shape, jnp.float32)
    query_acc, key_part, value_part = lax.fori_loop(
        0, blocks, third_pass, (start_query, start_keys, start_values)
    )
    query_grad = (query_acc * scaling).astype(jnp.bfloat16).reshape(tok_count, -1)
    return (query_grad, key_part, value_part)


def body(layer_input, query_proj, key_proj, value_proj, out_grad, block_pos, doc_ids):
    shards = lax.axis_size("seq")
    my_index = lax.axis_index("seq")
    tok_count = query_proj.shape[1]
    head_dim = key_proj.shape[2]
    head_count = query_proj.shape[2] // head_dim
    length = tok_count * shards
    scaling = head_dim ** (-0.5)
    key_all, value_all = (
        lax.all_gather(key_proj, "seq", axis=1, tiled=True),
        lax.all_gather(value_proj, "seq", axis=1, tiled=True),
    )
    key_rows = key_all[0]
    value_rows = value_all[0]
    key_pos, key_doc = token_labels(block_pos[0], doc_ids[0], length)
    query_pos = lax.dynamic_slice_in_dim(key_pos, my_index * tok_count, tok_count)
    query_doc = lax.dynamic_slice_in_dim(key_doc, my_index * tok_count, tok_count)
    queries = query_proj[0].reshape(tok_count, head_count, head_dim)
    grad_heads = out_grad[0].reshape(tok_count, head_count, head_dim)
    block_span = length // block_pos.shape[1]
    query_grad, key_part, value_part = block_terms(
        queries,
        grad_heads,
        key_rows,
        value_rows,
        query_pos,
        query_doc,
        key_pos,
        key_doc,
        scaling,
        block_span,
    )
    kv_part = jnp.concatenate([key_part, value_part], axis=1)
    kv_summed = lax.psum(kv_part, "seq").astype(jnp.bfloat16)
    query_all = lax.all_gather(query_grad[None], "seq", axis=1, tiled=True)
    grad_rows = jnp.concatenate([query_all[0], kv_summed], axis=1)
    feature_slab = layer_input[0]
    return lax.psum_scatter(
        lax.dot_general(
            feature_slab, grad_rows, (((0,), (0,)), ((), ())), preferred_element_type=jnp.float32
        ),
        "dp",
        scatter_dimension=0,
        tiled=True,
    )


def solution(mesh):
    placed = (
        P("dp", None, "seq"),
        P("dp", "seq", None),
        P("dp", "seq", None),
        P("dp", "seq", None),
        P("dp", "seq", None),
        P("dp", None),
        P("dp", None),
    )
    return jax.shard_map(
        body, mesh=mesh, in_specs=placed, out_specs=P(("seq", "dp"), None), check_vma=False
    )
```

profile of v0, /device:TPU:0, one launch (start us, length us, event | category | flops | bytes accessed | tf_op | source)
XLA Modules:
  0.0 275.5 jit_solution(9238335968574466974)
XLA Ops:
  6.5 0.8 broadcast_multiply_fusion
  7.4 0.9 select_reduce_fusion.1
  8.5 1.1 copy.27
  9.8 1.1 copy.29
  11.1 11.3 %all_gather.9 = bf16[1,2048,128]{2,1,0:T(8,128)(2,1)S(1)} all-gather(bf16[1,256,128]{2,1,0:T(8,128)(2,1)S(1)} %copy-done.2), channel_id=1, replica_groups=mesh['seq'=8,'dp'=4] {'seq'}, dimensions={1}, use_global_device_ids=true | all-gather | bytes 589824 | tf_op jit(solution)/shard_map/all_gather | solution.py:144
  22.4 27.5 %while.48 = (s32[]{:T(128)}, f32[4,256,1]{1,0,2:T(4,128)S(1)}, f32[4,256,1]{1,0,2:T(4,128)S(1)}, s32[256]{0:T(256)S(1)}, s32[2048]{0:T(1024)S(1)}, /*index=5*/s3...) while((s32[]{:T(128)}, f32[4,256,1]{1,0,2:T(4,128)S(1)}, ...), condition=%wide.region_7.8_spmd, body=%wide.region_1.7_spmd.sunk | while | flops 34572296 | bytes 1505643 | solution.py:75
  28.8 0.8 and_reduce_fusion.6
  32.1 0.8 and_reduce_fusion.6
  33.7 0.8 and_reduce_fusion.6
  37.0 0.8 and_reduce_fusion.6
  40.2 0.8 and_reduce_fusion.6
  45.1 0.8 and_reduce_fusion.6
  48.4 0.8 and_reduce_fusion.6
  49.9 12.2 %all_gather.10 = bf16[1,2048,128]{2,1,0:T(8,128)(2,1)} all-gather(bf16[1,256,128]{2,1,0:T(8,128)(2,1)S(1)} %copy-done.3), channel_id=1, replica_groups=mesh['seq'=8,'dp'=4] {'seq'}, dimensions={1}, use_global_device_ids=true | all-gather | bytes 589824 | tf_op jit(solution)/shard_map/all_gather | solution.py:145
  62.1 29.8 %while.49 = (s32[]{:T(128)}, f32[4,256,128]{2,1,0:T(8,128)S(1)}, s32[256]{0:T(256)S(1)}, s32[2048]{0:T(1024)S(1)}, s32[256]{0:T(256)S(1)}, /*index=5*/s32[2048]{...) while((s32[]{:T(128)}, f32[4,256,128]{2,1,0:T(8,128)S(1)}, ...), condition=%wide.region_12.13_spmd, body=%wide.region_8.12_spmd.sunk | while | flops 68255752 | bytes 1461607 | solution.py:92
  62.3 0.8 and_reduce_fusion.7
  63.7 1.6 conditional.7
  64.0 1.3 convolution_add_fusion
  65.5 0.8 and_reduce_fusion.7
  67.0 1.6 conditional.7
  67.3 1.3 convolution_add_fusion
  68.8 0.8 and_reduce_fusion.7
  70.4 0.8 and_reduce_fusion.7
  72.1 0.8 and_reduce_fusion.7
  73.7 0.8 and_reduce_fusion.7
  75.4 0.8 and_reduce_fusion.7
  77.1 0.8 and_reduce_fusion.7
  78.7 0.8 and_reduce_fusion.7
  80.4 0.8 and_reduce_fusion.7
  82.1 0.8 and_reduce_fusion.7
  83.7 0.8 and_reduce_fusion.7
  85.4 0.8 and_reduce_fusion.7
  87.0 0.8 and_reduce_fusion.7
  88.7 0.8 and_reduce_fusion.7
  90.4 0.8 and_reduce_fusion.7
  91.9 1.0 copy.31
  92.9 1.1 fusion.62
  94.0 1.1 broadcast.157.clone
  95.1 1.0 broadcast.157
  96.2 36.2 %while.50 = (s32[]{:T(128)}, f32[256,4,128]{0,2,1:T(8,128)S(1)}, f32[2048,128]{1,0:T(8,128)}, f32[2048,128]{1,0:T(8,128)}, s32[256]{0:T(256)S(1)}, /*index=5*/s3...) while((s32[]{:T(128)}, f32[256,4,128]{0,2,1:T(8,128)S(1)}, ...), condition=%wide.region_18.19_spmd, body=%wide.region_14.18_spmd.sunk | while | flops 169328640 | bytes 4774379 | solution.py:128
  97.7 5.1 %conditional.8 = ((f32[256,4,128]{0,2,1:T(8,128)S(1)}, f32[2048,128]{1,0:T(8,128)}, f32[2048,128]{1,0:T(8,128)})) conditional(s32[]{:T(128)} %convert_element_type.51, (f32[256,4,128]{0,2,1:T(8,128)S(1)}, f32[2048,128]{1,0:T(8,128)}, f32[2048,128]{1,0:T(8,128)}) %tuple.114, (s32[]{:T(128)}, bf16[2048,128]{1,0:T(8,128)(2,1)}, s32[256]{0:T(256)S(1)}, ...), branch_computations={%region_16.16_spmd, %region_17.17_spmd} | conditional | flops 169197568 | bytes 4768874 | solution.py:50
  98.0 1.1 fusion.36
  99.1 1.0 fusion.38
  100.1 1.0 fusion.29
  101.1 0.9 fusion.39
  102.0 0.9 fusion.41
  104.4 5.1 %conditional.8 = ((f32[256,4,128]{0,2,1:T(8,128)S(1)}, f32[2048,128]{1,0:T(8,128)}, f32[2048,128]{1,0:T(8,128)})) conditional(s32[]{:T(128)} %convert_element_type.51, (f32[256,4,128]{0,2,1:T(8,128)S(1)}, f32[2048,128]{1,0:T(8,128)}, f32[2048,128]{1,0:T(8,128)}) %tuple.114, (s32[]{:T(128)}, bf16[2048,128]{1,0:T(8,128)(2,1)}, s32[256]{0:T(256)S(1)}, ...), branch_computations={%region_16.16_spmd, %region_17.17_spmd} | conditional | flops 169197568 | bytes 4768874 | solution.py:50
  104.7 1.1 fusion.36
  105.8 1.0 fusion.38
  106.8 1.0 fusion.29
  107.8 0.8 fusion.39
  108.7 0.8 fusion.41
  114.6 0.8 and_reduce_fusion.8
  116.2 0.8 and_reduce_fusion.8
  121.1 0.8 and_reduce_fusion.8
  122.7 0.8 and_reduce_fusion.8
  127.6 0.8 and_reduce_fusion.8
  129.2 0.8 and_reduce_fusion.8
  133.2 3.0 %pad_maximum_fusion = f32[2048,256]{1,0:T(8,128)} fusion(f32[2048,128]{1,0:T(8,128)} %get-tuple-element.733, f32[2048,128]{1,0:T(8,128)} %get-tuple-element.732), kind=kLoop, calls=%fused_computation.70 | loop fusion | flops 524288 | bytes 4194304 | tf_op jit(solution)/shard_map/concatenate | solution.py:167
  136.1 82.0 %all-reduce.1 = bf16[2048,256]{1,0:T(8,128)(2,1)} all-reduce(f32[2048,256]{1,0:T(8,128)} %pad_maximum_fusion), channel_id=1, replica_groups=mesh['seq'=8,'dp'=4] {'seq'}, use_global_device_ids=true, to_apply=%region_19.20 | all-reduce | flops 524288 | bytes 3145728 | tf_op jit(solution)/shard_map/psum | solution.py:168
  218.1 2.3 copy.34
  220.4 4.9 %fusion.57 = f32[512,768]{0,1:T(8,128)} fusion(bf16[1,2048,512]{2,1,0:T(8,128)(2,1)S(1)} %copy-done, bf16[2048,256]{0,1:T(8,128)(2,1)} %copy.34, bf16[2048,512]{0,1:T(8,128)(2,1)} %bitcast.127), kind=kOutput, calls=%fused_computation.72 | convolution fusion | flops 1616904192 | bytes 6815744 | tf_op jit(solution)/shard_map/dot_general | solution.py:173
  225.3 41.5 %reduce-scatter.2.cloned.1.call-done = f32[128,768]{0,1:T(8,128)} async-done(((f32[512,768]{0,1:T(8,128)}), f32[128,768]{0,1:T(8,128)}) %reduce-scatter.2.cloned.1.call-update) | async-done | bytes 393232 | tf_op jit(solution)/shard_map/reduce_scatter | solution.py:172
  266.8 1.9 copy.35
  (211 shorter events, 28.2 us)
Async XLA Ops:
  6.5 213.9 %copy-start = (bf16[1,2048,512]{2,1,0:T(8,128)(2,1)S(1)}, bf16[1,2048,512]{2,1,0:T(8,128)(2,1)}, u32[]{:S(2)}) copy-start(bf16[1,2048,512]{2,1,0:T(8,128)(2,1)} %param.19) | copy-start | bytes 6291460
  6.5 4.5 %copy-start.2 = (bf16[1,256,128]{2,1,0:T(8,128)(2,1)S(1)}, bf16[1,256,128]{2,1,0:T(8,128)(2,1)}, u32[]{:S(2)}) copy-start(bf16[1,256,128]{2,1,0:T(8,128)(2,1)} %param.21) | copy-start | bytes 196612
  6.5 213.8 %all-gather.2.cloned.1.call-start = ((), (), s32[]{:S(2)}) async-start(), calls=%async_computation.1 | async-start | bytes 2359296 | tf_op jit(solution)/shard_map/all_gather | solution.py:169
  22.4 27.5 %copy-start.3 = (bf16[1,256,128]{2,1,0:T(8,128)(2,1)S(1)}, bf16[1,256,128]{2,1,0:T(8,128)(2,1)}, u32[]{:S(2)}) copy-start(bf16[1,256,128]{2,1,0:T(8,128)(2,1)} %param.22) | copy-start | bytes 196612
  49.9 12.2 %copy-start.1 = (bf16[2048,128]{1,0:T(8,128)(2,1)}, bf16[2048,128]{1,0:T(8,128)(2,1)S(1)}, u32[]{:S(2)}) copy-start(bf16[2048,128]{1,0:T(8,128)(2,1)S(1)} %get-tuple-element.1273) | copy-start | bytes 1572868
  133.1 133.7 %reduce-scatter.2.cloned.1.call-start = ((), (), s32[]{:S(2)}) async-start(), calls=%async_computation.2 | async-start | bytes 1966080 | tf_op jit(solution)/shard_map/reduce_scatter | solution.py:172
Sparse Core Ops, SparseCore 0:
  133.2 59.2 all-gather.1
  225.4 41.3 reduce-scatter.1
where the time goes:
time: 277 us; the launch traced here: 276 us
  blocking collectives  105 us (38%)
  other arithmetic  46.2 us (17%)
  waiting for transfers between devices  41.5 us (15%)
  loops' own time  32.9 us (12%)
  local copies, waits for them, and re-layouts  18.3 us (7%)
  matrix products  17.5 us (6%)
  between operations  13.5 us (5%)
    psum x1, blocking collectives, body(): kv_summed = lax.psum(kv_part, 'seq').astype(jnp.bfloat16)  82 us
    reduce_scatter x1, waiting for transfers between devices, body(): lax.psum_scatter(lax.dot_general(feature_slab, grad_rows, (((0,), (0,)),...  41.5 us
    reduce_or x48, other arithmetic, guarded(): alive = jnp.any(block_parts(block_id)[2])  38.7 us
    all_gather x1, blocking collectives, body(): lax.all_gather(value_proj, 'seq', axis=1, tiled=True)  12.2 us
    all_gather x1, blocking collectives, body(): lax.all_gather(key_proj, 'seq', axis=1, tiled=True)  11.3 us
    another operation x1, loops' own time, block_terms(): lax.fori_loop(0, blocks, first_pass, (start_peak, start_total))  10.7 us
    another operation x1, loops' own time, block_terms(): lax.fori_loop(0, blocks, second_pass, jnp.zeros((head_count, tok_count, h...  10.7 us
    another operation x1, loops' own time, block_terms(): lax.fori_loop(0, blocks, third_pass, (start_query, start_keys, start_valu...  10.6 us
  transfers between devices with their start and end apart: 2, of which 1 were waited for; matrix products, arithmetic and copies ran while one was open for 2% of the time, Pallas kernels for 0%

commit v1 on v0

v1 whole, which is shorter than its diff:
```python
import functools

import jax
import jax.numpy as jnp
from jax import lax
from jax.experimental import pallas as pl
from jax.experimental.pallas import tpu as pltpu
from jax.sharding import PartitionSpec as P

masked_fill = -1e30
MOST_DOC = 4
VMEM_LIMIT = 56 * 1024 * 1024

NT = (((1,), (1,)), ((), ()))
NN = (((1,), (0,)), ((), ()))
TN = (((0,), (0,)), ((), ()))


def dot(a, b, dims):
    return lax.dot_general(a, b, dims, preferred_element_type=jnp.float32)


def smem():
    return pl.BlockSpec(memory_space=pltpu.SMEM)


def vmem():
    return pl.BlockSpec(memory_space=pltpu.VMEM)


def kernel_params():
    return pltpu.CompilerParams(vmem_limit_bytes=VMEM_LIMIT)


def attention_kernel(shards, blocks, heads, hd, scaling, *refs):
    me_ref, pos_ref, doc_ref = refs[:3]
    kv_refs = refs[3 : 3 + shards]
    q_refs = refs[3 + shards : 5 + shards]
    g_refs = refs[5 + shards : 7 + shards]
    dq_ref, own_ref = refs[7 + shards : 9 + shards]
    sends = refs[9 + shards : 9 + shards + (shards // 2 - 1)]
    keys, values, dk_acc, dv_acc, inverse = refs[9 + shards + (shards // 2 - 1) :]
    me = me_ref[0]
    per_dev = blocks // shards
    span = keys.shape[0] // blocks

    for rel in range(shards):
        for b in range(per_dev):
            storage = (me ^ rel) * per_dev + b
            place = pos_ref[0, storage]
            inverse[place] = storage
            rows = pl.ds(pl.multiple_of(place * span, span), span)
            keys[rows, :] = kv_refs[rel][b * span : (b + 1) * span, :hd]
            values[rows, :] = kv_refs[rel][b * span : (b + 1) * span, hd:]
    dk_acc[...] = jnp.zeros_like(dk_acc)
    dv_acc[...] = jnp.zeros_like(dv_acc)

    def block_step(which, b, count, first):
        window = pl.ds(pl.multiple_of(first * span, span), count * span)
        key_win = keys[window, :]
        value_win = values[window, :]
        rows = slice(b * span, (b + 1) * span)
        q_cat = jnp.concatenate(
            [q_refs[which][rows, h * hd : (h + 1) * hd] for h in range(heads)], axis=0
        )
        g_cat = jnp.concatenate(
            [g_refs[which][rows, h * hd : (h + 1) * hd] for h in range(heads)], axis=0
        )
        scores = dot(key_win, q_cat, NT)
        dprobs = dot(value_win, g_cat, NT)
        key_at = lax.broadcasted_iota(jnp.int32, (span, heads * span), 0)
        query_at = lax.rem(lax.broadcasted_iota(jnp.int32, (span, heads * span), 1), span)
        last = jnp.where(key_at <= query_at, scores[(count - 1) * span :], masked_fill)
        if count > 1:
            scores = jnp.concatenate([scores[: (count - 1) * span], last], axis=0)
        else:
            scores = last
        peak = jnp.max(scores, axis=0, keepdims=True)
        weights = jnp.exp((scores - peak) * scaling)
        probs = weights * (1.0 / jnp.sum(weights, axis=0, keepdims=True))
        probs_b = probs.astype(jnp.bfloat16)
        delta = jnp.sum(probs_b.astype(jnp.float32) * dprobs, axis=0, keepdims=True)
        dscores = (probs * (dprobs - delta)).astype(jnp.bfloat16)
        dk_new = dot(dscores, q_cat, NN) * scaling
        dv_new = dot(probs_b, g_cat, NN)
        for j in range(count):
            at = pl.ds(pl.multiple_of(inverse[first + j] * span, span), span)
            dk_acc[at, :] += dk_new[j * span : (j + 1) * span]
            dv_acc[at, :] += dv_new[j * span : (j + 1) * span]
        if which == 0:
            dq_new = (dot(dscores, key_win, TN) * scaling).astype(jnp.bfloat16)
            for h in range(heads):
                dq_ref[rows, h * hd : (h + 1) * hd] = dq_new[h * span : (h + 1) * span]

    for which in range(2):
        for b in range(per_dev):
            place = pos_ref[0, (me ^ which) * per_dev + b]
            doc = doc_ref[0, place]
            count = jnp.int32(1)
            for back in range(1, MOST_DOC):
                at = jnp.maximum(place - back, 0)
                same = (place >= back) & (doc_ref[0, at] == doc)
                count = count + same.astype(jnp.int32)
            for n in range(1, MOST_DOC + 1):

                @pl.when(count == n)
                def _():
                    block_step(which, b, n, place - (n - 1))

    tok = per_dev * span

    def shard_rows(rel):
        return pl.ds(pl.multiple_of((me ^ rel) * tok, tok), tok)

    own_ref[:, :hd] = dk_acc[shard_rows(0), :]
    own_ref[:, hd:] = dv_acc[shard_rows(0), :]
    for i, send in enumerate(sends):
        send[:, :hd] = dk_acc[shard_rows(2 * i + 2), :].astype(jnp.bfloat16)
        send[:, hd:] = dv_acc[shard_rows(2 * i + 2), :].astype(jnp.bfloat16)


def attention(me, block_pos, doc_ids, kv_chunks, queries, grads, hd):
    shards = len(kv_chunks)
    tok, qw = queries[0].shape
    blocks = block_pos.shape[1]
    heads = qw // hd
    length = tok * shards
    sends = shards // 2 - 1
    part = jax.ShapeDtypeStruct((tok, 2 * hd), jnp.bfloat16)
    return pl.pallas_call(
        functools.partial(attention_kernel, shards, blocks, heads, hd, hd**-0.5),
        out_shape=(
            jax.ShapeDtypeStruct((tok, qw), jnp.bfloat16),
            jax.ShapeDtypeStruct((tok, 2 * hd), jnp.float32),
        )
        + (part,) * sends,
        in_specs=[smem()] * 3 + [vmem()] * (shards + 4),
        out_specs=(vmem(),) * (2 + sends),
        scratch_shapes=[
            pltpu.VMEM((length, hd), jnp.bfloat16),
            pltpu.VMEM((length, hd), jnp.bfloat16),
            pltpu.VMEM((length, hd), jnp.float32),
            pltpu.VMEM((length, hd), jnp.float32),
            pltpu.SMEM((blocks,), jnp.int32),
        ],
        compiler_params=kernel_params(),
        name="attention",
    )(me, block_pos, doc_ids, *kv_chunks, *queries, *grads)


def sum_kernel(own_ref, *refs):
    total = own_ref[...]
    for ref in refs[:-1]:
        total = total + ref[...].astype(jnp.float32)
    refs[-1][...] = total.astype(refs[-1].dtype)


def sum_parts(own, parts, dtype):
    return pl.pallas_call(
        sum_kernel,
        out_shape=jax.ShapeDtypeStruct(own.shape, dtype),
        in_specs=[vmem()] * (1 + len(parts)),
        out_specs=vmem(),
        compiler_params=kernel_params(),
        name="sum_parts",
    )(own, *parts)


def transpose_kernel(x_ref, out_ref):
    out_ref[...] = x_ref[...].T


def transposed(slab):
    rows, columns = slab.shape
    step = min(rows, 512)
    return pl.pallas_call(
        transpose_kernel,
        grid=(rows // step,),
        out_shape=jax.ShapeDtypeStruct((columns, rows), slab.dtype),
        in_specs=[pl.BlockSpec((step, columns), lambda i: (i, 0))],
        out_specs=pl.BlockSpec((columns, step), lambda i: (0, i)),
        compiler_params=kernel_params(),
        name="slab_transpose",
    )(slab)


def weight_kernel(shards, owners, me_ref, x_ref, *refs):
    chunks = refs[:shards]
    own_ref = refs[shards]
    sends = refs[shards + 1 : shards + owners]
    total = refs[-1]
    me, my_dp = me_ref[0], me_ref[1]
    tok = chunks[0].shape[0]
    for rel in range(shards):
        columns = pl.ds(pl.multiple_of((me ^ rel) * tok, tok), tok)
        term = dot(x_ref[:, columns], chunks[rel][...], NN)
        if rel == 0:
            total[...] = term
        else:
            total[...] += term
    piece = total.shape[0] // owners
    for rel in range(owners):
        rows = pl.ds(pl.multiple_of((my_dp ^ rel) * piece, piece), piece)
        if rel == 0:
            own_ref[...] = total[rows, :]
        else:
            sends[rel - 1][...] = total[rows, :].astype(jnp.bfloat16)


def weight_part(me, x_t, chunks, owners):
    shards = len(chunks)
    features = x_t.shape[0]
    columns = chunks[0].shape[1]
    piece = features // owners
    return pl.pallas_call(
        functools.partial(weight_kernel, shards, owners),
        out_shape=(jax.ShapeDtypeStruct((piece, columns), jnp.float32),)
        + (jax.ShapeDtypeStruct((piece, columns), jnp.bfloat16),) * (owners - 1),
        in_specs=[smem()] + [vmem()] * (1 + shards),
        out_specs=(vmem(),) * owners,
        scratch_shapes=[pltpu.VMEM((features, columns), jnp.float32)],
        compiler_params=kernel_params(),
        name="weight_part",
    )(me, x_t, *chunks)


def final_kernel(groups, owners, *refs):
    out_ref = refs[-1]
    first = 0
    for g in range(groups):
        own = refs[g * owners]
        total = own[...]
        for rel in range(1, owners):
            total = total + refs[g * owners + rel][...].astype(jnp.float32)
        out_ref[:, first : first + own.shape[1]] = total
        first += own.shape[1]


def final_sum(parts):
    groups, owners = len(parts), len(parts[0])
    flat = [array for group in parts for array in group]
    columns = sum(group[0].shape[1] for group in parts)
    return pl.pallas_call(
        functools.partial(final_kernel, groups, owners),
        out_shape=jax.ShapeDtypeStruct((flat[0].shape[0], columns), jnp.float32),
        in_specs=[vmem()] * len(flat),
        out_specs=vmem(),
        compiler_params=kernel_params(),
        name="final_sum",
    )(*flat)


def swap(x, axis, rel):
    return lax.ppermute(x, axis, [(i, i ^ rel) for i in range(lax.axis_size(axis))])


def gather(x):
    shards = lax.axis_size("seq")
    chunks = [None] * shards
    chunks[0] = x
    for rel in range(2, shards, 2):
        chunks[rel] = swap(x, "seq", rel)
    for rel in range(0, shards, 2):
        chunks[rel + 1] = swap(chunks[rel], "seq", 1)
    return chunks


def body(layer_input, query_proj, key_proj, value_proj, out_grad, block_pos, doc_ids):
    shards = lax.axis_size("seq")
    dp = lax.axis_size("dp")
    hd = key_proj.shape[2]
    me = jnp.stack([lax.axis_index("seq"), lax.axis_index("dp")]).astype(jnp.int32)
    kv = jnp.concatenate([key_proj[0], value_proj[0]], axis=1)
    kv_chunks = gather(kv)
    queries = (query_proj[0], swap(query_proj[0], "seq", 1))
    grads = (out_grad[0], swap(out_grad[0], "seq", 1))
    x_t = transposed(layer_input[0])

    dq, own, *sends = attention(me, block_pos, doc_ids, kv_chunks, queries, grads, hd)
    half = dq.shape[1] // 2
    exchanged = [swap(send, "seq", 2 * i + 2) for i, send in enumerate(sends)]
    dkv = sum_parts(own, exchanged, jnp.bfloat16)
    groups = [gather(dq[:, :half]), gather(dq[:, half:]), gather(dkv)]

    if dp <= 8 and dp & (dp - 1) == 0:
        parts = []
        for chunks in groups:
            own_rows, *others = weight_part(me, x_t, chunks, dp)
            parts.append(
                [own_rows] + [swap(other, "dp", i + 1) for i, other in enumerate(others)]
            )
        return final_sum(parts)
    terms = [weight_part(me, x_t, chunks, 1)[0] for chunks in groups]
    return lax.psum_scatter(
        jnp.concatenate(terms, axis=1), "dp", scatter_dimension=0, tiled=True
    )


def solution(mesh):
    placed = (
        P("dp", None, "seq"),
        P("dp", "seq", None),
        P("dp", "seq", None),
        P("dp", "seq", None),
        P("dp", "seq", None),
        P("dp", None),
        P("dp", None),
    )
    return jax.shard_map(
        body, mesh=mesh, in_specs=placed, out_specs=P(("seq", "dp"), None), check_vma=False
    )
```

time: 277 us -> 89.4 us (0.32)
  blocking collectives: 105 us -> 0 us
  other arithmetic: 46.2 us -> 1.5 us
  starting transfers between devices: 0.04 us -> 38.8 us
  loops' own time: 32.9 us -> 0 us
  Pallas kernels: 0 us -> 24.3 us
  waiting for transfers between devices: 41.5 us -> 21.1 us
  matrix products: 17.5 us -> 0 us
  local copies, waits for them, and re-layouts: 18.3 us -> 3.12 us
  between operations: 13.5 us -> 0.45 us
    psum x1 -> x0, blocking collectives: 82 us -> none  [body(): kv_summed = lax.psum(kv_part, 'seq').astype(jnp.bfloat16)]
    reduce_scatter x1 -> x0, waiting for transfers between devices: 41.5 us -> none  [body(): lax.psum_scatter(lax.dot_general(feature_slab, grad_rows, (((0,), (0,)),...]
    ppermute x0 -> x42, starting transfers between devices: none -> 38.8 us  [swap(): lax.ppermute(x, axis, [(i, i ^ rel) for i in range(lax.axis_size(axis))])]
    reduce_or x48 -> x0, other arithmetic: 38.7 us -> none  [guarded(): alive = jnp.any(block_parts(block_id)[2])]
    another operation x51 -> x0, loops' own time: 32.9 us -> none  [the longest x1 10.7 us: block_terms(): lax.fori_loop(0, blocks, first_pass, (start_peak, start_total))]
    pallas_call x0 -> x7, Pallas kernels: none -> 24.3 us  [the longest x3 10.2 us: weight_part(): pl.pallas_call(functools.partial(weight_kernel, shards, owners), out_shap...]
    all_gather x2 -> x0, blocking collectives: 23.5 us -> none  [the longest x1 12.2 us: body(): lax.all_gather(value_proj, 'seq', axis=1, tiled=True)]
    ppermute x0 -> x42, waiting for transfers between devices: none -> 21.1 us  [swap(): lax.ppermute(x, axis, [(i, i ^ rel) for i in range(lax.axis_size(axis))])]
  transfers between devices with their start and end apart: 2 -> 42, of which waited for: 1 -> 13; matrix products, arithmetic and copies ran while one was open for 2% -> 2% of each run, Pallas kernels for 0% -> 18%
where the time goes in v1:
time: 89.4 us; the launch traced here: 89.2 us
  starting transfers between devices  38.8 us (43%)
  Pallas kernels  24.3 us (27%)
  waiting for transfers between devices  21.1 us (24%)
  local copies, waits for them, and re-layouts  3.12 us (3%)
  other arithmetic  1.5 us (2%)
    ppermute x42, starting transfers between devices, swap(): lax.ppermute(x, axis, [(i, i ^ rel) for i in range(lax.axis_size(axis))])  38.8 us
    ppermute x42, waiting for transfers between devices, swap(): lax.ppermute(x, axis, [(i, i ^ rel) for i in range(lax.axis_size(axis))])  21.1 us
    pallas_call x3, Pallas kernels, weight_part(): pl.pallas_call(functools.partial(weight_kernel, shards, owners), out_shap...  10.2 us
    pallas_call x1, Pallas kernels, attention(): pl.pallas_call(functools.partial(attention_kernel, shards, blocks, heads,...  6.08 us
    pallas_call x1, Pallas kernels, transposed(): pl.pallas_call(transpose_kernel, grid=(rows // step,), out_shape=jax.Shap...  4.14 us
    unnamed x96, local copies, waits for them, and re-layouts  2.13 us
    pallas_call x1, Pallas kernels, final_sum(): pl.pallas_call(functools.partial(final_kernel, groups, owners), out_shape...  2.06 us
    pallas_call x1, Pallas kernels, sum_parts(): pl.pallas_call(sum_kernel, out_shape=jax.ShapeDtypeStruct(own.shape, dtyp...  1.85 us
  transfers between devices with their start and end apart: 42, of which 13 were waited for; matrix products, arithmetic and copies ran while one was open for 2% of the time, Pallas kernels for 18%

profile of v1, /device:TPU:0, one launch (start us, length us, event | category | flops | bytes accessed | tf_op | source)
XLA Modules:
  0.0 89.2 jit_solution(6786484177893114256)
XLA Ops:
  0.0 0.9 pad_maximum_fusion.refs_3_
  0.9 3.0 %collective-permute-start.1 = (bf16[256,256]{1,0:T(8,128)(2,1)S(1)}, bf16[256,256]{1,0:T(8,128)(2,1)S(1)}, u32[]{:S(2)}, u32[]{:S(2)}) collective-permute-start(bf16[256,256]{1,0:T(8,128)(2,1)S(1)} %pad_maximum_fusion.refs_3_), channel_id=1, source_target_pairs={{0,8},{4,12},{8,0},{12,4},{16,24},{20,28},{24,16},{28,20},{1,9},{5... | collective-permute-start | bytes 393224 | tf_op jit(solution)/shard_map/ppermute | solution.py:254
  3.9 1.5 %collective-permute-start.3 = (bf16[256,256]{1,0:T(8,128)(2,1)S(1)}, bf16[256,256]{1,0:T(8,128)(2,1)S(1)}, u32[]{:S(2)}, u32[]{:S(2)}) collective-permute-start(bf16[256,256]{1,0:T(8,128)(2,1)S(1)} %pad_maximum_fusion.refs_3_), channel_id=1, source_target_pairs={{0,16},{4,20},{8,24},{12,28},{16,0},{20,4},{24,8},{28,12},{1,17},{... | collective-permute-start | bytes 393224 | tf_op jit(solution)/shard_map/ppermute | solution.py:254
  5.4 0.0 collective-permute-start.5
  5.4 0.5 collective-permute-start.7
  6.0 1.8 %collective-permute-done.1.refs_5_ = bf16[256,256]{1,0:T(8,128)(2,1)S(1)} collective-permute-done((bf16[256,256]{1,0:T(8,128)(2,1)S(1)}, bf16[256,256]{1,0:T(8,128)(2,1)S(1)}, u32[]{:S(2)}, u32[]{:S(2)}) %collective-permute-start.1) | collective-permute-done | bytes 131104 | tf_op jit(solution)/shard_map/ppermute | solution.py:254
  7.8 3.9 %collective-permute-done.3.refs_7_ = bf16[256,256]{1,0:T(8,128)(2,1)S(1)} collective-permute-done((bf16[256,256]{1,0:T(8,128)(2,1)S(1)}, bf16[256,256]{1,0:T(8,128)(2,1)S(1)}, u32[]{:S(2)}, u32[]{:S(2)}) %collective-permute-start.3) | collective-permute-done | bytes 131104 | tf_op jit(solution)/shard_map/ppermute | solution.py:254
  11.7 0.5 collective-permute-start.4
  12.2 0.1 collective-permute-start.6
  12.3 0.6 pad_add_fusion.refs_0_.me_ref
  12.9 0.1 collective-permute-done.2.refs_6_
  13.0 0.2 collective-permute-done.4.refs_8_
  13.2 0.3 collective-permute-done.6.refs_10_
  13.6 0.1 copy-done.9
  13.7 0.2 copy-done.10
  13.9 0.3 copy-done.11
  14.2 0.1 copy-done.3
  14.3 0.7 copy-done.4
  15.0 6.1 %attention.1 = (bf16[256,512]{1,0:T(8,128)(2,1)}, f32[256,256]{1,0:T(8,128)}, bf16[256,256]{1,0:T(8,128)(2,1)}, bf16[256,256]{1,0:T(8,128)(2,1)}, bf16[256,256]{1,0:T(8,128)(2,1)}) custom-call(s32[2]{0:T(128)} %pad_add_fusion.refs_0_.me_ref, s32[1,16]{1,0:T(1,128)} %refs_1_.1, s32[1,16]{1,0:T(1,128)} %refs_2_.1, bf16[256,256]{1,0:T(8,128)(2,1)} %copy-done, ...), custom_call_target="tpu_custom_call" | custom-call | tf_op jit(solution)/shard_map/attention/pallas_call | solution.py:130
  21.1 1.1 %collective-permute-start.29 = (bf16[256,256]{1,0:T(8,128)(2,1)}, bf16[256,256]{1,0:T(8,128)(2,1)S(1)}, u32[]{:S(2)}, u32[]{:S(2)}) collective-permute-start(bf16[256,256]{1,0:T(8,128)(2,1)} %get-tuple-element.32), channel_id=1, source_target_pairs={{0,8},{4,12},{8,0},{12,4},{16,24},{20,28},{24,16},{28,20},{1,9},{5... | collective-permute-start | bytes 393224 | tf_op jit(solution)/shard_map/ppermute | solution.py:254
  22.2 0.7 collective-permute-start.30
  22.9 1.7 %collective-permute-start.31 = (bf16[256,256]{1,0:T(8,128)(2,1)}, bf16[256,256]{1,0:T(8,128)(2,1)S(1)}, u32[]{:S(2)}, u32[]{:S(2)}) collective-permute-start(bf16[256,256]{1,0:T(8,128)(2,1)} %get-tuple-element.34), channel_id=1, source_target_pairs={{0,24},{4,28},{8,16},{12,20},{16,8},{20,12},{24,0},{28,4},{1,25},{... | collective-permute-start | bytes 393224 | tf_op jit(solution)/shard_map/ppermute | solution.py:254
  24.6 1.0 %fusion = (bf16[256,256]{1,0:T(8,128)(2,1)S(1)}, bf16[256,256]{1,0:T(8,128)(2,1)S(1)}) fusion(bf16[256,512]{1,0:T(8,128)(2,1)} %get-tuple-element.22), kind=kLoop, calls=%fused_computation.2 | loop fusion | bytes 524288 | tf_op jit(solution)/shard_map/slice | solution.py:283
  25.6 0.0 copy-start.1
  25.6 1.2 %collective-permute-start.20 = (bf16[256,256]{1,0:T(8,128)(2,1)S(1)}, bf16[256,256]{1,0:T(8,128)(2,1)S(1)}, u32[]{:S(2)}, u32[]{:S(2)}) collective-permute-start(bf16[256,256]{1,0:T(8,128)(2,1)S(1)} %get-tuple-element.39.refs_0_), channel_id=1, source_target_pairs={{0,8},{4,12},{8,0},{12,4},{16,24},{20,28},{24,16},{28,20},{1,9},{5... | collective-permute-start | bytes 393224 | tf_op jit(solution)/shard_map/ppermute | solution.py:254
  26.8 0.7 collective-permute-start.22
  27.5 1.7 %collective-permute-start.24 = (bf16[256,256]{1,0:T(8,128)(2,1)S(1)}, bf16[256,256]{1,0:T(8,128)(2,1)S(1)}, u32[]{:S(2)}, u32[]{:S(2)}) collective-permute-start(bf16[256,256]{1,0:T(8,128)(2,1)S(1)} %get-tuple-element.39.refs_0_), channel_id=1, source_target_pairs={{0,24},{4,28},{8,16},{12,20},{16,8},{20,12},{24,0},{28,4},{1,25},{... | collective-permute-start | bytes 393224 | tf_op jit(solution)/shard_map/ppermute | solution.py:254
  29.2 2.5 %collective-permute-done.31.refs_2_ = bf16[256,256]{1,0:T(8,128)(2,1)S(1)} collective-permute-done((bf16[256,256]{1,0:T(8,128)(2,1)}, bf16[256,256]{1,0:T(8,128)(2,1)S(1)}, u32[]{:S(2)}, u32[]{:S(2)}) %collective-permute-start.31) | collective-permute-done | bytes 131104 | tf_op jit(solution)/shard_map/ppermute | solution.py:254
  31.7 0.7 collective-permute-start.10
  32.4 0.7 collective-permute-done.20.refs_2_
  33.2 1.9 %collective-permute-start.12 = (bf16[256,256]{1,0:T(8,128)(2,1)S(1)}, bf16[256,256]{1,0:T(8,128)(2,1)S(1)}, u32[]{:S(2)}, u32[]{:S(2)}) collective-permute-start(bf16[256,256]{1,0:T(8,128)(2,1)S(1)} %get-tuple-element.40.refs_0_), channel_id=1, source_target_pairs={{0,16},{4,20},{8,24},{12,28},{16,0},{20,4},{24,8},{28,12},{1,17},{... | collective-permute-start | bytes 393224 | tf_op jit(solution)/shard_map/ppermute | solution.py:254
  35.1 3.7 %collective-permute-start.14 = (bf16[256,256]{1,0:T(8,128)(2,1)S(1)}, bf16[256,256]{1,0:T(8,128)(2,1)S(1)}, u32[]{:S(2)}, u32[]{:S(2)}) collective-permute-start(bf16[256,256]{1,0:T(8,128)(2,1)S(1)} %get-tuple-element.40.refs_0_), channel_id=1, source_target_pairs={{0,24},{4,28},{8,16},{12,20},{16,8},{20,12},{24,0},{28,4},{1,25},{... | collective-permute-start | bytes 393224 | tf_op jit(solution)/shard_map/ppermute | solution.py:254
  38.8 1.8 %sum_parts.1.refs_0_ = bf16[256,256]{1,0:T(8,128)(2,1)} custom-call(f32[256,256]{1,0:T(8,128)} %get-tuple-element.31.own_ref, bf16[256,256]{1,0:T(8,128)(2,1)} %copy-done.12, bf16[256,256]{1,0:T(8,128)(2,1)} %copy-done.13, bf16[256,256]{1,0:T(8,128)(2,1)} %copy-done.14), custom_call_target="tpu_custom_call" | custom-call | tf_op jit(solution)/shard_map/sum_parts/pallas_call | solution.py:159
  40.7 0.6 collective-permute-start.35
  41.3 2.9 %collective-permute-start.37 = (bf16[256,256]{1,0:T(8,128)(2,1)}, bf16[256,256]{1,0:T(8,128)(2,1)S(1)}, u32[]{:S(2)}, u32[]{:S(2)}) collective-permute-start(bf16[256,256]{1,0:T(8,128)(2,1)} %sum_parts.1.refs_0_), channel_id=1, source_target_pairs={{0,24},{4,28},{8,16},{12,20},{16,8},{20,12},{24,0},{28,4},{1,25},{... | collective-permute-start | bytes 393224 | tf_op jit(solution)/shard_map/ppermute | solution.py:254
  44.2 0.5 collective-permute-start.23
  44.7 2.5 %collective-permute-done.33.refs_2_ = bf16[256,256]{1,0:T(8,128)(2,1)S(1)} collective-permute-done((bf16[256,256]{1,0:T(8,128)(2,1)}, bf16[256,256]{1,0:T(8,128)(2,1)S(1)}, u32[]{:S(2)}, u32[]{:S(2)}) %collective-permute-start.33) | collective-permute-done | bytes 131104 | tf_op jit(solution)/shard_map/ppermute | solution.py:254
  47.2 2.5 %collective-permute-done.35.refs_4_ = bf16[256,256]{1,0:T(8,128)(2,1)S(1)} collective-permute-done((bf16[256,256]{1,0:T(8,128)(2,1)}, bf16[256,256]{1,0:T(8,128)(2,1)S(1)}, u32[]{:S(2)}, u32[]{:S(2)}) %collective-permute-start.35) | collective-permute-done | bytes 131104 | tf_op jit(solution)/shard_map/ppermute | solution.py:254
  49.7 0.5 collective-permute-start.13
  50.2 0.1 collective-permute-start.15
  50.3 0.4 collective-permute-start.32
  50.7 0.1 collective-permute-start.34
  50.8 0.2 collective-permute-done.11.refs_3_
  51.0 0.2 collective-permute-start.36
  51.2 0.3 collective-permute-start.38
  51.5 4.1 %slab_transpose.1.x_ref = bf16[512,2048]{1,0:T(8,128)(2,1)} custom-call(bf16[2048,512]{1,0:T(8,128)(2,1)} %bitcast.7), custom_call_target="tpu_custom_call" | custom-call | tf_op jit(solution)/shard_map/slab_transpose/pallas_call | solution.py:176
  55.9 3.4 %weight_part.4 = (f32[128,256]{1,0:T(8,128)}, bf16[128,256]{1,0:T(8,128)(2,1)}, bf16[128,256]{1,0:T(8,128)(2,1)}, bf16[128,256]{1,0:T(8,128)(2,1)}) custom-call(s32[2]{0:T(128)} %pad_add_fusion.refs_0_.me_ref, bf16[512,2048]{1,0:T(8,128)(2,1)} %slab_transpose.1.x_ref, bf16[256,256]{1,0:T(8,128)(2,1)} %copy-done.2, bf16[256,256]{1,0:T(8,128)(2,1)} %copy-done.23, ...), custom_call_target="tpu_custom_call" | custom-call | tf_op jit(solution)/shard_map/weight_part/pallas_call | solution.py:215
  59.3 1.4 %collective-permute-start.26 = (bf16[128,256]{1,0:T(8,128)(2,1)}, bf16[128,256]{1,0:T(8,128)(2,1)S(1)}, u32[]{:S(2)}, u32[]{:S(2)}) collective-permute-start(bf16[128,256]{1,0:T(8,128)(2,1)} %get-tuple-element.28), channel_id=1, source_target_pairs={{0,1},{1,0},{2,3},{3,2},{4,5},{5,4},{6,7},{7,6},{8,9},{9,8},{10,11... | collective-permute-start | bytes 196616 | tf_op jit(solution)/shard_map/ppermute | solution.py:254
  60.7 3.4 %weight_part.3 = (f32[128,256]{1,0:T(8,128)}, bf16[128,256]{1,0:T(8,128)(2,1)}, bf16[128,256]{1,0:T(8,128)(2,1)}, bf16[128,256]{1,0:T(8,128)(2,1)}) custom-call(s32[2]{0:T(128)} %pad_add_fusion.refs_0_.me_ref, bf16[512,2048]{1,0:T(8,128)(2,1)} %slab_transpose.1.x_ref, bf16[256,256]{1,0:T(8,128)(2,1)} %copy-done.1, bf16[256,256]{1,0:T(8,128)(2,1)} %copy-done.25, ...), custom_call_target="tpu_custom_call" | custom-call | tf_op jit(solution)/shard_map/weight_part/pallas_call | solution.py:215
  64.1 0.0 copy-start.26
  64.2 3.6 %collective-permute-start.27 = (bf16[128,256]{1,0:T(8,128)(2,1)S(1)}, bf16[128,256]{1,0:T(8,128)(2,1)S(1)}, u32[]{:S(2)}, u32[]{:S(2)}) collective-permute-start(bf16[128,256]{1,0:T(8,128)(2,1)S(1)} %copy-done.47), channel_id=1, source_target_pairs={{0,2},{1,3},{2,0},{3,1},{4,6},{5,7},{6,4},{7,5},{8,10},{9,11},{10,... | collective-permute-start | bytes 196616 | tf_op jit(solution)/shard_map/ppermute | solution.py:254
  67.8 0.1 collective-permute-start.28
  67.9 0.6 collective-permute-start.16
  68.5 3.7 %collective-permute-start.17 = (bf16[128,256]{1,0:T(8,128)(2,1)}, bf16[128,256]{1,0:T(8,128)(2,1)S(1)}, u32[]{:S(2)}, u32[]{:S(2)}) collective-permute-start(bf16[128,256]{1,0:T(8,128)(2,1)} %get-tuple-element.25), channel_id=1, source_target_pairs={{0,2},{1,3},{2,0},{3,1},{4,6},{5,7},{6,4},{7,5},{8,10},{9,11},{10,... | collective-permute-start | bytes 196616 | tf_op jit(solution)/shard_map/ppermute | solution.py:254
  72.3 3.4 %weight_part.5 = (f32[128,256]{1,0:T(8,128)}, bf16[128,256]{1,0:T(8,128)(2,1)}, bf16[128,256]{1,0:T(8,128)(2,1)}, bf16[128,256]{1,0:T(8,128)(2,1)}) custom-call(s32[2]{0:T(128)} %pad_add_fusion.refs_0_.me_ref, bf16[512,2048]{1,0:T(8,128)(2,1)} %slab_transpose.1.x_ref, bf16[256,256]{1,0:T(8,128)(2,1)} %sum_parts.1.refs_0_, bf16[256,256]{1,0:T(8,128)(2,1)} %copy-done.26, ...), custom_call_target="tpu_custom_call" | custom-call | tf_op jit(solution)/shard_map/weight_part/pallas_call | solution.py:215
  75.7 0.2 collective-permute-start.18
  75.9 1.1 %collective-permute-start.39 = (bf16[128,256]{1,0:T(8,128)(2,1)}, bf16[128,256]{1,0:T(8,128)(2,1)S(1)}, u32[]{:S(2)}, u32[]{:S(2)}) collective-permute-start(bf16[128,256]{1,0:T(8,128)(2,1)} %get-tuple-element.36), channel_id=1, source_target_pairs={{0,1},{1,0},{2,3},{3,2},{4,5},{5,4},{6,7},{7,6},{8,9},{9,8},{10,11... | collective-permute-start | bytes 196616 | tf_op jit(solution)/shard_map/ppermute | solution.py:254
  76.9 3.2 %collective-permute-start.40 = (bf16[128,256]{1,0:T(8,128)(2,1)}, bf16[128,256]{1,0:T(8,128)(2,1)S(1)}, u32[]{:S(2)}, u32[]{:S(2)}) collective-permute-start(bf16[128,256]{1,0:T(8,128)(2,1)} %get-tuple-element.37), channel_id=1, source_target_pairs={{0,2},{1,3},{2,0},{3,1},{4,6},{5,7},{6,4},{7,5},{8,10},{9,11},{10,... | collective-permute-start | bytes 196616 | tf_op jit(solution)/shard_map/ppermute | solution.py:254
  80.1 0.1 collective-permute-start.41
  80.3 1.6 %collective-permute-done.18.refs_3_ = bf16[128,256]{1,0:T(8,128)(2,1)S(1)} collective-permute-done((bf16[128,256]{1,0:T(8,128)(2,1)S(1)}, bf16[128,256]{1,0:T(8,128)(2,1)S(1)}, u32[]{:S(2)}, u32[]{:S(2)}) %collective-permute-start.18) | collective-permute-done | bytes 65568 | tf_op jit(solution)/shard_map/ppermute | solution.py:254
  81.8 3.1 %collective-permute-done.40.refs_10_ = bf16[128,256]{1,0:T(8,128)(2,1)S(1)} collective-permute-done((bf16[128,256]{1,0:T(8,128)(2,1)}, bf16[128,256]{1,0:T(8,128)(2,1)S(1)}, u32[]{:S(2)}, u32[]{:S(2)}) %collective-permute-start.40) | collective-permute-done | bytes 65568 | tf_op jit(solution)/shard_map/ppermute | solution.py:254
  84.9 1.6 %collective-permute-done.41.refs_11_ = bf16[128,256]{1,0:T(8,128)(2,1)S(1)} collective-permute-done((bf16[128,256]{1,0:T(8,128)(2,1)}, bf16[128,256]{1,0:T(8,128)(2,1)S(1)}, u32[]{:S(2)}, u32[]{:S(2)}) %collective-permute-start.41) | collective-permute-done | bytes 65568 | tf_op jit(solution)/shard_map/ppermute | solution.py:254
  86.6 0.6 copy-done.44
  87.1 2.1 %final_sum.1 = f32[128,768]{1,0:T(8,128)} custom-call(f32[128,256]{1,0:T(8,128)} %get-tuple-element.23.refs_0_, bf16[128,256]{1,0:T(8,128)(2,1)} %copy-done.39, bf16[128,256]{1,0:T(8,128)(2,1)} %copy-done.40, bf16[128,256]{1,0:T(8,128)(2,1)} %copy-done.41, f32[128,256]{1,0:T(8,128)} %get-tuple-element.27.refs_4_, bf16[128,256]{1,0:T(8,128)(2,1)} %copy-done.36, ...), custom_call_target="tpu_custom_call" | custom-call | tf_op jit(solution)/shard_map/final_sum/pallas_call | solution.py:243
  (126 shorter events, 0.3 us)
Async XLA Ops:
  0.9 12.7 %copy-start = (bf16[256,256]{1,0:T(8,128)(2,1)}, bf16[256,256]{1,0:T(8,128)(2,1)S(1)}, u32[]{:S(2)}) copy-start(bf16[256,256]{1,0:T(8,128)(2,1)S(1)} %pad_maximum_fusion.refs_3_) | copy-start | bytes 393220
  0.9 6.9 %collective-permute-start.1 = (bf16[256,256]{1,0:T(8,128)(2,1)S(1)}, bf16[256,256]{1,0:T(8,128)(2,1)S(1)}, u32[]{:S(2)}, u32[]{:S(2)}) collective-permute-start(bf16[256,256]{1,0:T(8,128)(2,1)S(1)} %pad_maximum_fusion.refs_3_), channel_id=1, source_target_pairs={{0,8},{4,12},{8,0},{12,4},{16,24},{20,28},{24,16},{28,20},{1,9},{5... | collective-permute-start | bytes 393224 | tf_op jit(solution)/shard_map/ppermute | solution.py:254
  3.9 7.8 %collective-permute-start.3 = (bf16[256,256]{1,0:T(8,128)(2,1)S(1)}, bf16[256,256]{1,0:T(8,128)(2,1)S(1)}, u32[]{:S(2)}, u32[]{:S(2)}) collective-permute-start(bf16[256,256]{1,0:T(8,128)(2,1)S(1)} %pad_maximum_fusion.refs_3_), channel_id=1, source_target_pairs={{0,16},{4,20},{8,24},{12,28},{16,0},{20,4},{24,8},{28,12},{1,17},{... | collective-permute-start | bytes 393224 | tf_op jit(solution)/shard_map/ppermute | solution.py:254
  5.4 6.3 %collective-permute-start.5 = (bf16[256,256]{1,0:T(8,128)(2,1)S(1)}, bf16[256,256]{1,0:T(8,128)(2,1)S(1)}, u32[]{:S(2)}, u32[]{:S(2)}) collective-permute-start(bf16[256,256]{1,0:T(8,128)(2,1)S(1)} %pad_maximum_fusion.refs_3_), channel_id=1, source_target_pairs={{0,24},{4,28},{8,16},{12,20},{16,8},{20,12},{24,0},{28,4},{1,25},{... | collective-permute-start | bytes 393224 | tf_op jit(solution)/shard_map/ppermute | solution.py:254
  5.4 6.8 %collective-permute-start = (bf16[256,256]{1,0:T(8,128)(2,1)S(1)}, bf16[256,256]{1,0:T(8,128)(2,1)S(1)}, u32[]{:S(2)}, u32[]{:S(2)}) collective-permute-start(bf16[256,256]{1,0:T(8,128)(2,1)S(1)} %pad_maximum_fusion.refs_3_), channel_id=1, source_target_pairs={{0,4},{4,0},{8,12},{12,8},{16,20},{20,16},{24,28},{28,24},{1,5},{5... | collective-permute-start | bytes 393224 | tf_op jit(solution)/shard_map/ppermute | solution.py:254
  5.4 8.1 %collective-permute-start.7 = (bf16[256,512]{1,0:T(8,128)(2,1)}, bf16[256,512]{1,0:T(8,128)(2,1)S(1)}, u32[]{:S(2)}, u32[]{:S(2)}) collective-permute-start(bf16[256,512]{1,0:T(8,128)(2,1)} %bitcast.8), channel_id=1, source_target_pairs={{0,4},{4,0},{8,12},{12,8},{16,20},{20,16},{24,28},{28,24},{1,5},{5... | collective-permute-start | bytes 786440 | tf_op jit(solution)/shard_map/ppermute | solution.py:254
  7.8 5.8 %collective-permute-start.8 = (bf16[256,512]{1,0:T(8,128)(2,1)}, bf16[256,512]{1,0:T(8,128)(2,1)S(1)}, u32[]{:S(2)}, u32[]{:S(2)}) collective-permute-start(bf16[256,512]{1,0:T(8,128)(2,1)} %bitcast.10), channel_id=1, source_target_pairs={{0,4},{4,0},{8,12},{12,8},{16,20},{20,16},{24,28},{28,24},{1,5},{5... | collective-permute-start | bytes 786440 | tf_op jit(solution)/shard_map/ppermute | solution.py:254
  11.7 1.3 %collective-permute-start.2 = (bf16[256,256]{1,0:T(8,128)(2,1)S(1)}, bf16[256,256]{1,0:T(8,128)(2,1)S(1)}, u32[]{:S(2)}, u32[]{:S(2)}) collective-permute-start(bf16[256,256]{1,0:T(8,128)(2,1)S(1)} %collective-permute-done.1.refs_5_), channel_id=1, source_target_pairs={{0,4},{4,0},{8,12},{12,8},{16,20},{20,16},{24,28},{28,24},{1,5},{5... | collective-permute-start | bytes 393224 | tf_op jit(solution)/shard_map/ppermute | solution.py:254
  11.7 1.5 %collective-permute-start.4 = (bf16[256,256]{1,0:T(8,128)(2,1)S(1)}, bf16[256,256]{1,0:T(8,128)(2,1)S(1)}, u32[]{:S(2)}, u32[]{:S(2)}) collective-permute-start(bf16[256,256]{1,0:T(8,128)(2,1)S(1)} %collective-permute-done.3.refs_7_), channel_id=1, source_target_pairs={{0,4},{4,0},{8,12},{12,8},{16,20},{20,16},{24,28},{28,24},{1,5},{5... | collective-permute-start | bytes 393224 | tf_op jit(solution)/shard_map/ppermute | solution.py:254
  12.2 1.3 %collective-permute-start.6 = (bf16[256,256]{1,0:T(8,128)(2,1)S(1)}, bf16[256,256]{1,0:T(8,128)(2,1)S(1)}, u32[]{:S(2)}, u32[]{:S(2)}) collective-permute-start(bf16[256,256]{1,0:T(8,128)(2,1)S(1)} %collective-permute-done.5.refs_9_), channel_id=1, source_target_pairs={{0,4},{4,0},{8,12},{12,8},{16,20},{20,16},{24,28},{28,24},{1,5},{5... | collective-permute-start | bytes 393224 | tf_op jit(solution)/shard_map/ppermute | solution.py:254
  21.1 6.4 %collective-permute-start.29 = (bf16[256,256]{1,0:T(8,128)(2,1)}, bf16[256,256]{1,0:T(8,128)(2,1)S(1)}, u32[]{:S(2)}, u32[]{:S(2)}) collective-permute-start(bf16[256,256]{1,0:T(8,128)(2,1)} %get-tuple-element.32), channel_id=1, source_target_pairs={{0,8},{4,12},{8,0},{12,4},{16,24},{20,28},{24,16},{28,20},{1,9},{5... | collective-permute-start | bytes 393224 | tf_op jit(solution)/shard_map/ppermute | solution.py:254
  22.2 7.0 %collective-permute-start.30 = (bf16[256,256]{1,0:T(8,128)(2,1)}, bf16[256,256]{1,0:T(8,128)(2,1)S(1)}, u32[]{:S(2)}, u32[]{:S(2)}) collective-permute-start(bf16[256,256]{1,0:T(8,128)(2,1)} %get-tuple-element.33), channel_id=1, source_target_pairs={{0,16},{4,20},{8,24},{12,28},{16,0},{20,4},{24,8},{28,12},{1,17},{... | collective-permute-start | bytes 393224 | tf_op jit(solution)/shard_map/ppermute | solution.py:254
  22.9 8.8 %collective-permute-start.31 = (bf16[256,256]{1,0:T(8,128)(2,1)}, bf16[256,256]{1,0:T(8,128)(2,1)S(1)}, u32[]{:S(2)}, u32[]{:S(2)}) collective-permute-start(bf16[256,256]{1,0:T(8,128)(2,1)} %get-tuple-element.34), channel_id=1, source_target_pairs={{0,24},{4,28},{8,16},{12,20},{16,8},{20,12},{24,0},{28,4},{1,25},{... | collective-permute-start | bytes 393224 | tf_op jit(solution)/shard_map/ppermute | solution.py:254
  25.6 30.1 %copy-start.1 = (bf16[256,256]{1,0:T(8,128)(2,1)}, bf16[256,256]{1,0:T(8,128)(2,1)S(1)}, u32[]{:S(2)}) copy-start(bf16[256,256]{1,0:T(8,128)(2,1)S(1)} %get-tuple-element.40.refs_0_) | copy-start | bytes 393220
  25.6 30.1 %copy-start.2 = (bf16[256,256]{1,0:T(8,128)(2,1)}, bf16[256,256]{1,0:T(8,128)(2,1)S(1)}, u32[]{:S(2)}) copy-start(bf16[256,256]{1,0:T(8,128)(2,1)S(1)} %get-tuple-element.39.refs_0_) | copy-start | bytes 393220
  25.6 7.5 %collective-permute-start.20 = (bf16[256,256]{1,0:T(8,128)(2,1)S(1)}, bf16[256,256]{1,0:T(8,128)(2,1)S(1)}, u32[]{:S(2)}, u32[]{:S(2)}) collective-permute-start(bf16[256,256]{1,0:T(8,128)(2,1)S(1)} %get-tuple-element.39.refs_0_), channel_id=1, source_target_pairs={{0,8},{4,12},{8,0},{12,4},{16,24},{20,28},{24,16},{28,20},{1,9},{5... | collective-permute-start | bytes 393224 | tf_op jit(solution)/shard_map/ppermute | solution.py:254
  26.8 8.3 %collective-permute-start.22 = (bf16[256,256]{1,0:T(8,128)(2,1)S(1)}, bf16[256,256]{1,0:T(8,128)(2,1)S(1)}, u32[]{:S(2)}, u32[]{:S(2)}) collective-permute-start(bf16[256,256]{1,0:T(8,128)(2,1)S(1)} %get-tuple-element.39.refs_0_), channel_id=1, source_target_pairs={{0,16},{4,20},{8,24},{12,28},{16,0},{20,4},{24,8},{28,12},{1,17},{... | collective-permute-start | bytes 393224 | tf_op jit(solution)/shard_map/ppermute | solution.py:254
  27.5 11.3 %copy-start.12 = (bf16[256,256]{1,0:T(8,128)(2,1)}, bf16[256,256]{1,0:T(8,128)(2,1)S(1)}, u32[]{:S(2)}) copy-start(bf16[256,256]{1,0:T(8,128)(2,1)S(1)} %collective-permute-done.29.refs_0_) | copy-start | bytes 393220
  27.5 11.3 %collective-permute-start.24 = (bf16[256,256]{1,0:T(8,128)(2,1)S(1)}, bf16[256,256]{1,0:T(8,128)(2,1)S(1)}, u32[]{:S(2)}, u32[]{:S(2)}) collective-permute-start(bf16[256,256]{1,0:T(8,128)(2,1)S(1)} %get-tuple-element.39.refs_0_), channel_id=1, source_target_pairs={{0,24},{4,28},{8,16},{12,20},{16,8},{20,12},{24,0},{28,4},{1,25},{... | collective-permute-start | bytes 393224 | tf_op jit(solution)/shard_map/ppermute | solution.py:254
  29.2 9.6 %copy-start.13 = (bf16[256,256]{1,0:T(8,128)(2,1)}, bf16[256,256]{1,0:T(8,128)(2,1)S(1)}, u32[]{:S(2)}) copy-start(bf16[256,256]{1,0:T(8,128)(2,1)S(1)} %collective-permute-done.30.refs_1_) | copy-start | bytes 393220
  29.2 11.5 %collective-permute-start.19 = (bf16[256,256]{1,0:T(8,128)(2,1)S(1)}, bf16[256,256]{1,0:T(8,128)(2,1)S(1)}, u32[]{:S(2)}, u32[]{:S(2)}) collective-permute-start(bf16[256,256]{1,0:T(8,128)(2,1)S(1)} %get-tuple-element.39.refs_0_), channel_id=1, source_target_pairs={{0,4},{4,0},{8,12},{12,8},{16,20},{20,16},{24,28},{28,24},{1,5},{5... | collective-permute-start | bytes 393224 | tf_op jit(solution)/shard_map/ppermute | solution.py:254
  31.7 7.1 %copy-start.14 = (bf16[256,256]{1,0:T(8,128)(2,1)}, bf16[256,256]{1,0:T(8,128)(2,1)S(1)}, u32[]{:S(2)}) copy-start(bf16[256,256]{1,0:T(8,128)(2,1)S(1)} %collective-permute-done.31.refs_2_) | copy-start | bytes 393220
  31.7 9.0 %collective-permute-start.10 = (bf16[256,256]{1,0:T(8,128)(2,1)S(1)}, bf16[256,256]{1,0:T(8,128)(2,1)S(1)}, u32[]{:S(2)}, u32[]{:S(2)}) collective-permute-start(bf16[256,256]{1,0:T(8,128)(2,1)S(1)} %get-tuple-element.40.refs_0_), channel_id=1, source_target_pairs={{0,8},{4,12},{8,0},{12,4},{16,24},{20,28},{24,16},{28,20},{1,9},{5... | collective-permute-start | bytes 393224 | tf_op jit(solution)/shard_map/ppermute | solution.py:254
  33.2 22.5 %copy-start.15 = (bf16[256,256]{1,0:T(8,128)(2,1)}, bf16[256,256]{1,0:T(8,128)(2,1)S(1)}, u32[]{:S(2)}) copy-start(bf16[256,256]{1,0:T(8,128)(2,1)S(1)} %collective-permute-done.20.refs_2_) | copy-start | bytes 393220
  33.2 8.2 %collective-permute-start.12 = (bf16[256,256]{1,0:T(8,128)(2,1)S(1)}, bf16[256,256]{1,0:T(8,128)(2,1)S(1)}, u32[]{:S(2)}, u32[]{:S(2)}) collective-permute-start(bf16[256,256]{1,0:T(8,128)(2,1)S(1)} %get-tuple-element.40.refs_0_), channel_id=1, source_target_pairs={{0,16},{4,20},{8,24},{12,28},{16,0},{20,4},{24,8},{28,12},{1,17},{... | collective-permute-start | bytes 393224 | tf_op jit(solution)/shard_map/ppermute | solution.py:254
  35.1 20.6 %copy-start.17 = (bf16[256,256]{1,0:T(8,128)(2,1)}, bf16[256,256]{1,0:T(8,128)(2,1)S(1)}, u32[]{:S(2)}) copy-start(bf16[256,256]{1,0:T(8,128)(2,1)S(1)} %collective-permute-done.22.refs_4_) | copy-start | bytes 393220
  35.1 9.1 %collective-permute-start.14 = (bf16[256,256]{1,0:T(8,128)(2,1)S(1)}, bf16[256,256]{1,0:T(8,128)(2,1)S(1)}, u32[]{:S(2)}, u32[]{:S(2)}) collective-permute-start(bf16[256,256]{1,0:T(8,128)(2,1)S(1)} %get-tuple-element.40.refs_0_), channel_id=1, source_target_pairs={{0,24},{4,28},{8,16},{12,20},{16,8},{20,12},{24,0},{28,4},{1,25},{... | collective-permute-start | bytes 393224 | tf_op jit(solution)/shard_map/ppermute | solution.py:254
  38.8 16.9 %copy-start.20 = (bf16[256,256]{1,0:T(8,128)(2,1)}, bf16[256,256]{1,0:T(8,128)(2,1)S(1)}, u32[]{:S(2)}) copy-start(bf16[256,256]{1,0:T(8,128)(2,1)S(1)} %collective-permute-done.24.refs_6_) | copy-start | bytes 393220
  38.8 5.4 %collective-permute-start.9 = (bf16[256,256]{1,0:T(8,128)(2,1)S(1)}, bf16[256,256]{1,0:T(8,128)(2,1)S(1)}, u32[]{:S(2)}, u32[]{:S(2)}) collective-permute-start(bf16[256,256]{1,0:T(8,128)(2,1)S(1)} %get-tuple-element.40.refs_0_), channel_id=1, source_target_pairs={{0,4},{4,0},{8,12},{12,8},{16,20},{20,16},{24,28},{28,24},{1,5},{5... | collective-permute-start | bytes 393224 | tf_op jit(solution)/shard_map/ppermute | solution.py:254
  40.7 15.0 %copy-start.23 = (bf16[256,256]{1,0:T(8,128)(2,1)}, bf16[256,256]{1,0:T(8,128)(2,1)S(1)}, u32[]{:S(2)}) copy-start(bf16[256,256]{1,0:T(8,128)(2,1)S(1)} %collective-permute-done.19.refs_1_) | copy-start | bytes 393220
  40.7 6.5 %collective-permute-start.33 = (bf16[256,256]{1,0:T(8,128)(2,1)}, bf16[256,256]{1,0:T(8,128)(2,1)S(1)}, u32[]{:S(2)}, u32[]{:S(2)}) collective-permute-start(bf16[256,256]{1,0:T(8,128)(2,1)} %sum_parts.1.refs_0_), channel_id=1, source_target_pairs={{0,8},{4,12},{8,0},{12,4},{16,24},{20,28},{24,16},{28,20},{1,9},{5... | collective-permute-start | bytes 393224 | tf_op jit(solution)/shard_map/ppermute | solution.py:254
  40.7 15.0 %copy-start.19 = (bf16[256,256]{1,0:T(8,128)(2,1)}, bf16[256,256]{1,0:T(8,128)(2,1)S(1)}, u32[]{:S(2)}) copy-start(bf16[256,256]{1,0:T(8,128)(2,1)S(1)} %collective-permute-done.10.refs_2_) | copy-start | bytes 393220
  40.7 8.9 %collective-permute-start.35 = (bf16[256,256]{1,0:T(8,128)(2,1)}, bf16[256,256]{1,0:T(8,128)(2,1)S(1)}, u32[]{:S(2)}, u32[]{:S(2)}) collective-permute-start(bf16[256,256]{1,0:T(8,128)(2,1)} %sum_parts.1.refs_0_), channel_id=1, source_target_pairs={{0,16},{4,20},{8,24},{12,28},{16,0},{20,4},{24,8},{28,12},{1,17},{... | collective-permute-start | bytes 393224 | tf_op jit(solution)/shard_map/ppermute | solution.py:254
  41.3 14.4 %copy-start.22 = (bf16[256,256]{1,0:T(8,128)(2,1)}, bf16[256,256]{1,0:T(8,128)(2,1)S(1)}, u32[]{:S(2)}) copy-start(bf16[256,256]{1,0:T(8,128)(2,1)S(1)} %collective-permute-done.12.refs_4_) | copy-start | bytes 393220
  41.3 8.3 %collective-permute-start.37 = (bf16[256,256]{1,0:T(8,128)(2,1)}, bf16[256,256]{1,0:T(8,128)(2,1)S(1)}, u32[]{:S(2)}, u32[]{:S(2)}) collective-permute-start(bf16[256,256]{1,0:T(8,128)(2,1)} %sum_parts.1.refs_0_), channel_id=1, source_target_pairs={{0,24},{4,28},{8,16},{12,20},{16,8},{20,12},{24,0},{28,4},{1,25},{... | collective-permute-start | bytes 393224 | tf_op jit(solution)/shard_map/ppermute | solution.py:254
  44.2 11.6 %copy-start.24 = (bf16[256,256]{1,0:T(8,128)(2,1)}, bf16[256,256]{1,0:T(8,128)(2,1)S(1)}, u32[]{:S(2)}) copy-start(bf16[256,256]{1,0:T(8,128)(2,1)S(1)} %collective-permute-done.14.refs_6_) | copy-start | bytes 393220
  44.2 6.0 %collective-permute-start.21 = (bf16[256,256]{1,0:T(8,128)(2,1)S(1)}, bf16[256,256]{1,0:T(8,128)(2,1)S(1)}, u32[]{:S(2)}, u32[]{:S(2)}) collective-permute-start(bf16[256,256]{1,0:T(8,128)(2,1)S(1)} %collective-permute-done.20.refs_2_), channel_id=1, source_target_pairs={{0,4},{4,0},{8,12},{12,8},{16,20},{20,16},{24,28},{28,24},{1,5},{5... | collective-permute-start | bytes 393224 | tf_op jit(solution)/shard_map/ppermute | solution.py:254
  44.2 11.5 %copy-start.25 = (bf16[256,256]{1,0:T(8,128)(2,1)}, bf16[256,256]{1,0:T(8,128)(2,1)S(1)}, u32[]{:S(2)}) copy-start(bf16[256,256]{1,0:T(8,128)(2,1)S(1)} %collective-permute-done.9.refs_1_) | copy-start | bytes 393220
  44.2 6.1 %collective-permute-start.23 = (bf16[256,256]{1,0:T(8,128)(2,1)S(1)}, bf16[256,256]{1,0:T(8,128)(2,1)S(1)}, u32[]{:S(2)}, u32[]{:S(2)}) collective-permute-start(bf16[256,256]{1,0:T(8,128)(2,1)S(1)} %collective-permute-done.22.refs_4_), channel_id=1, source_target_pairs={{0,4},{4,0},{8,12},{12,8},{16,20},{20,16},{24,28},{28,24},{1,5},{5... | collective-permute-start | bytes 393224 | tf_op jit(solution)/shard_map/ppermute | solution.py:254
  47.2 8.6 %copy-start.16 = (bf16[256,256]{1,0:T(8,128)(2,1)}, bf16[256,256]{1,0:T(8,128)(2,1)S(1)}, u32[]{:S(2)}) copy-start(bf16[256,256]{1,0:T(8,128)(2,1)S(1)} %collective-permute-done.33.refs_2_) | copy-start | bytes 393220
  47.2 3.5 %collective-permute-start.25 = (bf16[256,256]{1,0:T(8,128)(2,1)S(1)}, bf16[256,256]{1,0:T(8,128)(2,1)S(1)}, u32[]{:S(2)}, u32[]{:S(2)}) collective-permute-start(bf16[256,256]{1,0:T(8,128)(2,1)S(1)} %collective-permute-done.24.refs_6_), channel_id=1, source_target_pairs={{0,4},{4,0},{8,12},{12,8},{16,20},{20,16},{24,28},{28,24},{1,5},{5... | collective-permute-start | bytes 393224 | tf_op jit(solution)/shard_map/ppermute | solution.py:254
  49.7 1.3 %collective-permute-start.11 = (bf16[256,256]{1,0:T(8,128)(2,1)S(1)}, bf16[256,256]{1,0:T(8,128)(2,1)S(1)}, u32[]{:S(2)}, u32[]{:S(2)}) collective-permute-start(bf16[256,256]{1,0:T(8,128)(2,1)S(1)} %collective-permute-done.10.refs_2_), channel_id=1, source_target_pairs={{0,4},{4,0},{8,12},{12,8},{16,20},{20,16},{24,28},{28,24},{1,5},{5... | collective-permute-start | bytes 393224 | tf_op jit(solution)/shard_map/ppermute | solution.py:254
  49.7 1.5 %collective-permute-start.13 = (bf16[256,256]{1,0:T(8,128)(2,1)S(1)}, bf16[256,256]{1,0:T(8,128)(2,1)S(1)}, u32[]{:S(2)}, u32[]{:S(2)}) collective-permute-start(bf16[256,256]{1,0:T(8,128)(2,1)S(1)} %collective-permute-done.12.refs_4_), channel_id=1, source_target_pairs={{0,4},{4,0},{8,12},{12,8},{16,20},{20,16},{24,28},{28,24},{1,5},{5... | collective-permute-start | bytes 393224 | tf_op jit(solution)/shard_map/ppermute | solution.py:254
  50.2 9.1 %collective-permute-start.15 = (bf16[256,256]{1,0:T(8,128)(2,1)S(1)}, bf16[256,256]{1,0:T(8,128)(2,1)S(1)}, u32[]{:S(2)}, u32[]{:S(2)}) collective-permute-start(bf16[256,256]{1,0:T(8,128)(2,1)S(1)} %collective-permute-done.14.refs_6_), channel_id=1, source_target_pairs={{0,4},{4,0},{8,12},{12,8},{16,20},{20,16},{24,28},{28,24},{1,5},{5... | collective-permute-start | bytes 393224 | tf_op jit(solution)/shard_map/ppermute | solution.py:254
  50.3 13.8 %collective-permute-start.32 = (bf16[256,256]{1,0:T(8,128)(2,1)}, bf16[256,256]{1,0:T(8,128)(2,1)S(1)}, u32[]{:S(2)}, u32[]{:S(2)}) collective-permute-start(bf16[256,256]{1,0:T(8,128)(2,1)} %sum_parts.1.refs_0_), channel_id=1, source_target_pairs={{0,4},{4,0},{8,12},{12,8},{16,20},{20,16},{24,28},{28,24},{1,5},{5... | collective-permute-start | bytes 393224 | tf_op jit(solution)/shard_map/ppermute | solution.py:254
  50.7 17.1 %collective-permute-start.34 = (bf16[256,256]{1,0:T(8,128)(2,1)S(1)}, bf16[256,256]{1,0:T(8,128)(2,1)S(1)}, u32[]{:S(2)}, u32[]{:S(2)}) collective-permute-start(bf16[256,256]{1,0:T(8,128)(2,1)S(1)} %collective-permute-done.33.refs_2_), channel_id=1, source_target_pairs={{0,4},{4,0},{8,12},{12,8},{16,20},{20,16},{24,28},{28,24},{1,5},{5... | collective-permute-start | bytes 393224 | tf_op jit(solution)/shard_map/ppermute | solution.py:254
  51.0 16.9 %collective-permute-start.36 = (bf16[256,256]{1,0:T(8,128)(2,1)S(1)}, bf16[256,256]{1,0:T(8,128)(2,1)S(1)}, u32[]{:S(2)}, u32[]{:S(2)}) collective-permute-start(bf16[256,256]{1,0:T(8,128)(2,1)S(1)} %collective-permute-done.35.refs_4_), channel_id=1, source_target_pairs={{0,4},{4,0},{8,12},{12,8},{16,20},{20,16},{24,28},{28,24},{1,5},{5... | collective-permute-start | bytes 393224 | tf_op jit(solution)/shard_map/ppermute | solution.py:254
  51.2 17.3 %collective-permute-start.38 = (bf16[256,256]{1,0:T(8,128)(2,1)S(1)}, bf16[256,256]{1,0:T(8,128)(2,1)S(1)}, u32[]{:S(2)}, u32[]{:S(2)}) collective-permute-start(bf16[256,256]{1,0:T(8,128)(2,1)S(1)} %collective-permute-done.37.refs_6_), channel_id=1, source_target_pairs={{0,4},{4,0},{8,12},{12,8},{16,20},{20,16},{24,28},{28,24},{1,5},{5... | collective-permute-start | bytes 393224 | tf_op jit(solution)/shard_map/ppermute | solution.py:254
  59.2 8.5 %copy-start.45 = (bf16[128,256]{1,0:T(8,128)(2,1)S(1)}, bf16[128,256]{1,0:T(8,128)(2,1)}, u32[]{:S(2)}) copy-start(bf16[128,256]{1,0:T(8,128)(2,1)} %get-tuple-element.30) | copy-start | bytes 196612
  59.3 16.4 %collective-permute-start.26 = (bf16[128,256]{1,0:T(8,128)(2,1)}, bf16[128,256]{1,0:T(8,128)(2,1)S(1)}, u32[]{:S(2)}, u32[]{:S(2)}) collective-permute-start(bf16[128,256]{1,0:T(8,128)(2,1)} %get-tuple-element.28), channel_id=1, source_target_pairs={{0,1},{1,0},{2,3},{3,2},{4,5},{5,4},{6,7},{7,6},{8,9},{9,8},{10,11... | collective-permute-start | bytes 196616 | tf_op jit(solution)/shard_map/ppermute | solution.py:254
  64.1 11.5 %copy-start.46 = (bf16[128,256]{1,0:T(8,128)(2,1)S(1)}, bf16[128,256]{1,0:T(8,128)(2,1)}, u32[]{:S(2)}) copy-start(bf16[128,256]{1,0:T(8,128)(2,1)} %get-tuple-element.26) | copy-start | bytes 196612
  64.1 8.1 %copy-start.26 = (bf16[256,256]{1,0:T(8,128)(2,1)}, bf16[256,256]{1,0:T(8,128)(2,1)S(1)}, u32[]{:S(2)}) copy-start(bf16[256,256]{1,0:T(8,128)(2,1)S(1)} %collective-permute-done.32.refs_1_) | copy-start | bytes 393220
  64.2 11.7 %collective-permute-start.27 = (bf16[128,256]{1,0:T(8,128)(2,1)S(1)}, bf16[128,256]{1,0:T(8,128)(2,1)S(1)}, u32[]{:S(2)}, u32[]{:S(2)}) collective-permute-start(bf16[128,256]{1,0:T(8,128)(2,1)S(1)} %copy-done.47), channel_id=1, source_target_pairs={{0,2},{1,3},{2,0},{3,1},{4,6},{5,7},{6,4},{7,5},{8,10},{9,11},{10,... | collective-permute-start | bytes 196616 | tf_op jit(solution)/shard_map/ppermute | solution.py:254
  67.8 9.1 %collective-permute-start.28 = (bf16[128,256]{1,0:T(8,128)(2,1)S(1)}, bf16[128,256]{1,0:T(8,128)(2,1)S(1)}, u32[]{:S(2)}, u32[]{:S(2)}) collective-permute-start(bf16[128,256]{1,0:T(8,128)(2,1)S(1)} %copy-done.45), channel_id=1, source_target_pairs={{0,3},{1,2},{2,1},{3,0},{4,7},{5,6},{6,5},{7,4},{8,11},{9,10},{10,... | collective-permute-start | bytes 196616 | tf_op jit(solution)/shard_map/ppermute | solution.py:254
  67.9 12.2 %collective-permute-start.16 = (bf16[128,256]{1,0:T(8,128)(2,1)}, bf16[128,256]{1,0:T(8,128)(2,1)S(1)}, u32[]{:S(2)}, u32[]{:S(2)}) collective-permute-start(bf16[128,256]{1,0:T(8,128)(2,1)} %get-tuple-element.24), channel_id=1, source_target_pairs={{0,1},{1,0},{2,3},{3,2},{4,5},{5,4},{6,7},{7,6},{8,9},{9,8},{10,11... | collective-permute-start | bytes 196616 | tf_op jit(solution)/shard_map/ppermute | solution.py:254
  68.5 11.7 %collective-permute-start.17 = (bf16[128,256]{1,0:T(8,128)(2,1)}, bf16[128,256]{1,0:T(8,128)(2,1)S(1)}, u32[]{:S(2)}, u32[]{:S(2)}) collective-permute-start(bf16[128,256]{1,0:T(8,128)(2,1)} %get-tuple-element.25), channel_id=1, source_target_pairs={{0,2},{1,3},{2,0},{3,1},{4,6},{5,7},{6,4},{7,5},{8,10},{9,11},{10,... | collective-permute-start | bytes 196616 | tf_op jit(solution)/shard_map/ppermute | solution.py:254
  75.6 10.9 %copy-start.36 = (bf16[128,256]{1,0:T(8,128)(2,1)}, bf16[128,256]{1,0:T(8,128)(2,1)S(1)}, u32[]{:S(2)}) copy-start(bf16[128,256]{1,0:T(8,128)(2,1)S(1)} %collective-permute-done.26.refs_5_) | copy-start | bytes 196612
  75.7 6.2 %collective-permute-start.18 = (bf16[128,256]{1,0:T(8,128)(2,1)S(1)}, bf16[128,256]{1,0:T(8,128)(2,1)S(1)}, u32[]{:S(2)}, u32[]{:S(2)}) collective-permute-start(bf16[128,256]{1,0:T(8,128)(2,1)S(1)} %copy-done.46), channel_id=1, source_target_pairs={{0,3},{1,2},{2,1},{3,0},{4,7},{5,6},{6,5},{7,4},{8,11},{9,10},{10,... | collective-permute-start | bytes 196616 | tf_op jit(solution)/shard_map/ppermute | solution.py:254
  75.9 10.7 %copy-start.37 = (bf16[128,256]{1,0:T(8,128)(2,1)}, bf16[128,256]{1,0:T(8,128)(2,1)S(1)}, u32[]{:S(2)}) copy-start(bf16[128,256]{1,0:T(8,128)(2,1)S(1)} %collective-permute-done.27.refs_6_) | copy-start | bytes 196612
  75.9 6.0 %collective-permute-start.39 = (bf16[128,256]{1,0:T(8,128)(2,1)}, bf16[128,256]{1,0:T(8,128)(2,1)S(1)}, u32[]{:S(2)}, u32[]{:S(2)}) collective-permute-start(bf16[128,256]{1,0:T(8,128)(2,1)} %get-tuple-element.36), channel_id=1, source_target_pairs={{0,1},{1,0},{2,3},{3,2},{4,5},{5,4},{6,7},{7,6},{8,9},{9,8},{10,11... | collective-permute-start | bytes 196616 | tf_op jit(solution)/shard_map/ppermute | solution.py:254
  76.9 9.6 %copy-start.38 = (bf16[128,256]{1,0:T(8,128)(2,1)}, bf16[128,256]{1,0:T(8,128)(2,1)S(1)}, u32[]{:S(2)}) copy-start(bf16[128,256]{1,0:T(8,128)(2,1)S(1)} %collective-permute-done.28.refs_7_) | copy-start | bytes 196612
  76.9 8.0 %collective-permute-start.40 = (bf16[128,256]{1,0:T(8,128)(2,1)}, bf16[128,256]{1,0:T(8,128)(2,1)S(1)}, u32[]{:S(2)}, u32[]{:S(2)}) collective-permute-start(bf16[128,256]{1,0:T(8,128)(2,1)} %get-tuple-element.37), channel_id=1, source_target_pairs={{0,2},{1,3},{2,0},{3,1},{4,6},{5,7},{6,4},{7,5},{8,10},{9,11},{10,... | collective-permute-start | bytes 196616 | tf_op jit(solution)/shard_map/ppermute | solution.py:254
  80.1 6.4 %copy-start.39 = (bf16[128,256]{1,0:T(8,128)(2,1)}, bf16[128,256]{1,0:T(8,128)(2,1)S(1)}, u32[]{:S(2)}) copy-start(bf16[128,256]{1,0:T(8,128)(2,1)S(1)} %collective-permute-done.16.refs_1_) | copy-start | bytes 196612
  80.1 6.4 %collective-permute-start.41 = (bf16[128,256]{1,0:T(8,128)(2,1)}, bf16[128,256]{1,0:T(8,128)(2,1)S(1)}, u32[]{:S(2)}, u32[]{:S(2)}) collective-permute-start(bf16[128,256]{1,0:T(8,128)(2,1)} %get-tuple-element.38), channel_id=1, source_target_pairs={{0,3},{1,2},{2,1},{3,0},{4,7},{5,6},{6,5},{7,4},{8,11},{9,10},{10,... | collective-permute-start | bytes 196616 | tf_op jit(solution)/shard_map/ppermute | solution.py:254
  (26 other events, 89.1 us)

commit v2 on v1

--- a/solution.py
+++ b/solution.py
@@ -9,7 +9,7 @@
 
 masked_fill = -1e30
 MOST_DOC = 4
-VMEM_LIMIT = 56 * 1024 * 1024
+VMEM_LIMIT = 20 * 1024 * 1024
 
 NT = (((1,), (1,)), ((), ()))
 NN = (((1,), (0,)), ((), ()))
@@ -166,38 +166,16 @@
     )(own, *parts)
 
 
-def transpose_kernel(x_ref, out_ref):
-    out_ref[...] = x_ref[...].T
-
-
-def transposed(slab):
-    rows, columns = slab.shape
-    step = min(rows, 512)
-    return pl.pallas_call(
-        transpose_kernel,
-        grid=(rows // step,),
-        out_shape=jax.ShapeDtypeStruct((columns, rows), slab.dtype),
-        in_specs=[pl.BlockSpec((step, columns), lambda i: (i, 0))],
-        out_specs=pl.BlockSpec((columns, step), lambda i: (0, i)),
-        compiler_params=kernel_params(),
-        name="slab_transpose",
-    )(slab)
-
-
 def weight_kernel(shards, owners, me_ref, x_ref, *refs):
     chunks = refs[:shards]
     own_ref = refs[shards]
     sends = refs[shards + 1 : shards + owners]
-    total = refs[-1]
+    rows_all, total = refs[-2:]
     me, my_dp = me_ref[0], me_ref[1]
     tok = chunks[0].shape[0]
     for rel in range(shards):
-        columns = pl.ds(pl.multiple_of((me ^ rel) * tok, tok), tok)
-        term = dot(x_ref[:, columns], chunks[rel][...], NN)
-        if rel == 0:
-            total[...] = term
-        else:
-            total[...] += term
+        rows_all[pl.ds(pl.multiple_of((me ^ rel) * tok, tok), tok), :] = chunks[rel][...]
+    total[...] = dot(x_ref[...], rows_all[...], TN)
     piece = total.shape[0] // owners
     for rel in range(owners):
         rows = pl.ds(pl.multiple_of((my_dp ^ rel) * piece, piece), piece)
@@ -207,9 +185,9 @@
             sends[rel - 1][...] = total[rows, :].astype(jnp.bfloat16)
 
 
-def weight_part(me, x_t, chunks, owners):
+def weight_part(me, slab, chunks, owners):
     shards = len(chunks)
-    features = x_t.shape[0]
+    length, features = slab.shape
     columns = chunks[0].shape[1]
     piece = features // owners
     return pl.pallas_call(
@@ -218,10 +196,18 @@
         + (jax.ShapeDtypeStruct((piece, columns), jnp.bfloat16),) * (owners - 1),
         in_specs=[smem()] + [vmem()] * (1 + shards),
         out_specs=(vmem(),) * owners,
-        scratch_shapes=[pltpu.VMEM((features, columns), jnp.float32)],
-        compiler_params=kernel_params(),
+        scratch_shapes=[
+            pltpu.VMEM((length, columns), jnp.bfloat16),
+            pltpu.VMEM((features, columns), jnp.float32),
+        ],
+        compiler_params=kernel_params(),
+        cost_estimate=pl.CostEstimate(
+            flops=2 * length * features * columns,
+            bytes_accessed=2 * length * (features + columns),
+            transcendentals=0,
+        ),
         name="weight_part",
-    )(me, x_t, *chunks)
+    )(me, slab, *chunks)
 
 
 def final_kernel(groups, owners, *refs):
@@ -274,8 +260,7 @@
     kv_chunks = gather(kv)
     queries = (query_proj[0], swap(query_proj[0], "seq", 1))
     grads = (out_grad[0], swap(out_grad[0], "seq", 1))
-    x_t = transposed(layer_input[0])
-
+    slab = layer_input[0]
     dq, own, *sends = attention(me, block_pos, doc_ids, kv_chunks, queries, grads, hd)
     half = dq.shape[1] // 2
     exchanged = [swap(send, "seq", 2 * i + 2) for i, send in enumerate(sends)]
@@ -285,12 +270,12 @@
     if dp <= 8 and dp & (dp - 1) == 0:
         parts = []
         for chunks in groups:
-            own_rows, *others = weight_part(me, x_t, chunks, dp)
+            own_rows, *others = weight_part(me, slab, chunks, dp)
             parts.append(
                 [own_rows] + [swap(other, "dp", i + 1) for i, other in enumerate(others)]
             )
         return final_sum(parts)
-    terms = [weight_part(me, x_t, chunks, 1)[0] for chunks in groups]
+    terms = [weight_part(me, slab, chunks, 1)[0] for chunks in groups]
     return lax.psum_scatter(
         jnp.concatenate(terms, axis=1), "dp", scatter_dimension=0, tiled=True
     )

time: 89.4 us -> 78.9 us (0.88)
  Pallas kernels: 24.3 us -> 9.48 us
  waiting for transfers between devices: 21.1 us -> 27.1 us
    pallas_call x3, Pallas kernels: 10.2 us -> 4.11 us  [weight_part(): pl.pallas_call(functools.partial(weight_kernel, shards, owners), out_shap...]
    ppermute x42, waiting for transfers between devices: 21.1 us -> 27.1 us  [swap(): lax.ppermute(x, axis, [(i, i ^ rel) for i in range(lax.axis_size(axis))])]
    pallas_call x1 -> x0, Pallas kernels: 4.14 us -> none  [transposed(): pl.pallas_call(transpose_kernel, grid=(rows // step,), out_shape=jax.Shap...]
    pallas_call x1, Pallas kernels: 1.85 us -> 0.07 us  [sum_parts(): pl.pallas_call(sum_kernel, out_shape=jax.ShapeDtypeStruct(own.shape, dtyp...]
    pallas_call x1, Pallas kernels: 6.08 us -> 4.47 us  [attention(): pl.pallas_call(functools.partial(attention_kernel, shards, blocks, heads,...]
    pallas_call x1, Pallas kernels: 2.06 us -> 0.83 us  [final_sum(): pl.pallas_call(functools.partial(final_kernel, groups, owners), out_shape...]
    unnamed x96 -> x10, local copies, waits for them, and re-layouts: 2.13 us -> 3.21 us
    slice x1, local copies, waits for them, and re-layouts: 0.98 us -> 0.02 us  [body(): groups = [gather(dq[:, :half]), gather(dq[:, half:]), gather(dkv)]]
  transfers between devices with their start and end apart: 42 -> 42, of which waited for: 13 -> 18; matrix products, arithmetic and copies ran while one was open for 2% -> 0% of each run, Pallas kernels for 18% -> 5%
where the time goes in v2:
time: 78.9 us; the launch traced here: 79.1 us
  starting transfers between devices  38 us (48%)
  waiting for transfers between devices  27.1 us (34%)
  Pallas kernels  9.48 us (12%)
  local copies, waits for them, and re-layouts  3.23 us (4%)
  other arithmetic  1.11 us (1%)
    ppermute x42, starting transfers between devices, swap(): lax.ppermute(x, axis, [(i, i ^ rel) for i in range(lax.axis_size(axis))])  38 us
    ppermute x42, waiting for transfers between devices, swap(): lax.ppermute(x, axis, [(i, i ^ rel) for i in range(lax.axis_size(axis))])  27.1 us
    pallas_call x1, Pallas kernels, attention(): pl.pallas_call(functools.partial(attention_kernel, shards, blocks, heads,...  4.47 us
    pallas_call x3, Pallas kernels, weight_part(): pl.pallas_call(functools.partial(weight_kernel, shards, owners), out_shap...  4.11 us
    unnamed x10, local copies, waits for them, and re-layouts  3.21 us
  transfers between devices with their start and end apart: 42, of which 18 were waited for; matrix products, arithmetic and copies ran while one was open for 0% of the time, Pallas kernels for 5%

profile of v2, /device:TPU:0, one launch (start us, length us, event | category | flops | bytes accessed | tf_op | source)
XLA Modules:
  0.0 79.1 jit_solution(10958419097050463612)
XLA Ops:
  0.0 1.0 %pad_maximum_fusion.refs_3_ = bf16[256,256]{1,0:T(8,128)(2,1)S(1)} fusion(bf16[256,128]{1,0:T(8,128)(2,1)} %bitcast.14, bf16[256,128]{1,0:T(8,128)(2,1)} %bitcast.15), kind=kLoop, calls=%fused_computation | loop fusion | flops 262144 | bytes 262144 | tf_op jit(solution)/shard_map/concatenate | solution.py:259
  1.0 4.0 %collective-permute-start.5 = (bf16[256,256]{1,0:T(8,128)(2,1)S(1)}, bf16[256,256]{1,0:T(8,128)(2,1)S(1)}, u32[]{:S(2)}, u32[]{:S(2)}) collective-permute-start(bf16[256,256]{1,0:T(8,128)(2,1)S(1)} %pad_maximum_fusion.refs_3_), channel_id=1, source_target_pairs={{0,24},{4,28},{8,16},{12,20},{16,8},{20,12},{24,0},{28,4},{1,25},{... | collective-permute-start | bytes 393224 | tf_op jit(solution)/shard_map/ppermute | solution.py:240
  5.0 0.5 collective-permute-start.3
  5.5 0.1 collective-permute-start.1
  5.6 0.5 collective-permute-start.7
  6.2 2.8 %collective-permute-done.5.refs_9_ = bf16[256,256]{1,0:T(8,128)(2,1)S(1)} collective-permute-done((bf16[256,256]{1,0:T(8,128)(2,1)S(1)}, bf16[256,256]{1,0:T(8,128)(2,1)S(1)}, u32[]{:S(2)}, u32[]{:S(2)}) %collective-permute-start.5) | collective-permute-done | bytes 131104 | tf_op jit(solution)/shard_map/ppermute | solution.py:240
  8.9 0.0 collective-permute-start.8
  8.9 2.4 %collective-permute-done.3.refs_7_ = bf16[256,256]{1,0:T(8,128)(2,1)S(1)} collective-permute-done((bf16[256,256]{1,0:T(8,128)(2,1)S(1)}, bf16[256,256]{1,0:T(8,128)(2,1)S(1)}, u32[]{:S(2)}, u32[]{:S(2)}) %collective-permute-start.3) | collective-permute-done | bytes 131104 | tf_op jit(solution)/shard_map/ppermute | solution.py:240
  11.3 0.0 collective-permute-start.6
  11.3 0.2 collective-permute-done.1.refs_5_
  11.6 0.3 collective-permute-start.4
  11.8 0.0 collective-permute-done.refs_4_
  11.8 0.2 collective-permute-start.2
  12.1 0.1 pad_add_fusion.refs_0_.me_ref
  12.1 0.5 collective-permute-done.6.refs_10_
  12.7 0.2 collective-permute-done.4.refs_8_
  12.9 0.4 collective-permute-done.2.refs_6_
  13.3 0.9 %copy-done.1 = bf16[1,256,512]{2,1,0:T(8,128)(2,1)S(1)} copy-done((bf16[1,256,512]{2,1,0:T(8,128)(2,1)S(1)}, bf16[1,256,512]{2,1,0:T(8,128)(2,1)}, u32[]{:S(2)}) %copy-start.1) | copy-done | bytes 262168
  14.3 0.9 %copy-done.2 = bf16[1,256,512]{2,1,0:T(8,128)(2,1)S(1)} copy-done((bf16[1,256,512]{2,1,0:T(8,128)(2,1)S(1)}, bf16[1,256,512]{2,1,0:T(8,128)(2,1)}, u32[]{:S(2)}) %copy-start.2) | copy-done | bytes 262168
  15.2 0.7 copy-done.3
  15.9 0.7 copy-done.4
  16.5 4.5 %attention.1 = (bf16[256,512]{1,0:T(8,128)(2,1)S(1)}, f32[256,256]{1,0:T(8,128)S(1)}, bf16[256,256]{1,0:T(8,128)(2,1)S(1)}, bf16[256,256]{1,0:T(8,128)(2,1)S(1)}, bf16[256,256]{1,0:T(8,128)(2,1)S(1)}) custom-call(s32[2]{0:T(128)S(1)} %pad_add_fusion.refs_0_.me_ref, s32[1,16]{1,0:T(1,128)S(1)} %copy-done.3, s32[1,16]{1,0:T(1,128)S(1)} %copy-done.4, ...), custom_call_target="tpu_custom_call" | custom-call | tf_op jit(solution)/shard_map/attention/pallas_call | solution.py:130
  21.0 1.8 %collective-permute-start.24 = (bf16[256,256]{1,0:T(8,128)(2,1)S(1)}, bf16[256,256]{1,0:T(8,128)(2,1)S(1)}, u32[]{:S(2)}, u32[]{:S(2)}) collective-permute-start(bf16[256,256]{1,0:T(8,128)(2,1)S(1)} %get-tuple-element.39.refs_0_), channel_id=1, source_target_pairs={{0,24},{4,28},{8,16},{12,20},{16,8},{20,12},{24,0},{28,4},{1,25},{... | collective-permute-start | bytes 393224 | tf_op jit(solution)/shard_map/ppermute | solution.py:240
  22.9 1.4 %collective-permute-start.22 = (bf16[256,256]{1,0:T(8,128)(2,1)S(1)}, bf16[256,256]{1,0:T(8,128)(2,1)S(1)}, u32[]{:S(2)}, u32[]{:S(2)}) collective-permute-start(bf16[256,256]{1,0:T(8,128)(2,1)S(1)} %get-tuple-element.39.refs_0_), channel_id=1, source_target_pairs={{0,16},{4,20},{8,24},{12,28},{16,0},{20,4},{24,8},{28,12},{1,17},{... | collective-permute-start | bytes 393224 | tf_op jit(solution)/shard_map/ppermute | solution.py:240
  24.2 0.4 collective-permute-start.20
  24.6 1.8 %collective-permute-start.14 = (bf16[256,256]{1,0:T(8,128)(2,1)S(1)}, bf16[256,256]{1,0:T(8,128)(2,1)S(1)}, u32[]{:S(2)}, u32[]{:S(2)}) collective-permute-start(bf16[256,256]{1,0:T(8,128)(2,1)S(1)} %get-tuple-element.40.refs_0_), channel_id=1, source_target_pairs={{0,24},{4,28},{8,16},{12,20},{16,8},{20,12},{24,0},{28,4},{1,25},{... | collective-permute-start | bytes 393224 | tf_op jit(solution)/shard_map/ppermute | solution.py:240
  26.4 2.0 %collective-permute-done.24.refs_6_ = bf16[256,256]{1,0:T(8,128)(2,1)S(1)} collective-permute-done((bf16[256,256]{1,0:T(8,128)(2,1)S(1)}, bf16[256,256]{1,0:T(8,128)(2,1)S(1)}, u32[]{:S(2)}, u32[]{:S(2)}) %collective-permute-start.24) | collective-permute-done | bytes 131104 | tf_op jit(solution)/shard_map/ppermute | solution.py:240
  28.3 1.8 %collective-permute-start.12 = (bf16[256,256]{1,0:T(8,128)(2,1)S(1)}, bf16[256,256]{1,0:T(8,128)(2,1)S(1)}, u32[]{:S(2)}, u32[]{:S(2)}) collective-permute-start(bf16[256,256]{1,0:T(8,128)(2,1)S(1)} %get-tuple-element.40.refs_0_), channel_id=1, source_target_pairs={{0,16},{4,20},{8,24},{12,28},{16,0},{20,4},{24,8},{28,12},{1,17},{... | collective-permute-start | bytes 393224 | tf_op jit(solution)/shard_map/ppermute | solution.py:240
  30.1 1.1 %collective-permute-done.22.refs_4_ = bf16[256,256]{1,0:T(8,128)(2,1)S(1)} collective-permute-done((bf16[256,256]{1,0:T(8,128)(2,1)S(1)}, bf16[256,256]{1,0:T(8,128)(2,1)S(1)}, u32[]{:S(2)}, u32[]{:S(2)}) %collective-permute-start.22) | collective-permute-done | bytes 131104 | tf_op jit(solution)/shard_map/ppermute | solution.py:240
  31.2 1.7 %collective-permute-start.10 = (bf16[256,256]{1,0:T(8,128)(2,1)S(1)}, bf16[256,256]{1,0:T(8,128)(2,1)S(1)}, u32[]{:S(2)}, u32[]{:S(2)}) collective-permute-start(bf16[256,256]{1,0:T(8,128)(2,1)S(1)} %get-tuple-element.40.refs_0_), channel_id=1, source_target_pairs={{0,8},{4,12},{8,0},{12,4},{16,24},{20,28},{24,16},{28,20},{1,9},{5... | collective-permute-start | bytes 393224 | tf_op jit(solution)/shard_map/ppermute | solution.py:240
  32.9 0.4 collective-permute-start.29
  33.3 0.1 collective-permute-done.14.refs_6_
  33.4 1.7 %collective-permute-start.30 = (bf16[256,256]{1,0:T(8,128)(2,1)S(1)}, bf16[256,256]{1,0:T(8,128)(2,1)S(1)}, u32[]{:S(2)}, u32[]{:S(2)}) collective-permute-start(bf16[256,256]{1,0:T(8,128)(2,1)S(1)} %get-tuple-element.33), channel_id=1, source_target_pairs={{0,16},{4,20},{8,24},{12,28},{16,0},{20,4},{24,8},{28,12},{1,17},{... | collective-permute-start | bytes 393224 | tf_op jit(solution)/shard_map/ppermute | solution.py:240
  35.1 1.0 %collective-permute-done.12.refs_4_ = bf16[256,256]{1,0:T(8,128)(2,1)S(1)} collective-permute-done((bf16[256,256]{1,0:T(8,128)(2,1)S(1)}, bf16[256,256]{1,0:T(8,128)(2,1)S(1)}, u32[]{:S(2)}, u32[]{:S(2)}) %collective-permute-start.12) | collective-permute-done | bytes 131104 | tf_op jit(solution)/shard_map/ppermute | solution.py:240
  36.1 1.7 %collective-permute-start.31 = (bf16[256,256]{1,0:T(8,128)(2,1)S(1)}, bf16[256,256]{1,0:T(8,128)(2,1)S(1)}, u32[]{:S(2)}, u32[]{:S(2)}) collective-permute-start(bf16[256,256]{1,0:T(8,128)(2,1)S(1)} %get-tuple-element.34), channel_id=1, source_target_pairs={{0,24},{4,28},{8,16},{12,20},{16,8},{20,12},{24,0},{28,4},{1,25},{... | collective-permute-start | bytes 393224 | tf_op jit(solution)/shard_map/ppermute | solution.py:240
  37.8 0.5 collective-permute-start.23
  38.4 0.9 %collective-permute-done.29.refs_0_ = bf16[256,256]{1,0:T(8,128)(2,1)S(1)} collective-permute-done((bf16[256,256]{1,0:T(8,128)(2,1)S(1)}, bf16[256,256]{1,0:T(8,128)(2,1)S(1)}, u32[]{:S(2)}, u32[]{:S(2)}) %collective-permute-start.29) | collective-permute-done | bytes 131104 | tf_op jit(solution)/shard_map/ppermute | solution.py:240
  39.3 0.5 collective-permute-start.15
  39.8 3.4 %collective-permute-done.31.refs_2_ = bf16[256,256]{1,0:T(8,128)(2,1)S(1)} collective-permute-done((bf16[256,256]{1,0:T(8,128)(2,1)S(1)}, bf16[256,256]{1,0:T(8,128)(2,1)S(1)}, u32[]{:S(2)}, u32[]{:S(2)}) %collective-permute-start.31) | collective-permute-done | bytes 131104 | tf_op jit(solution)/shard_map/ppermute | solution.py:240
  43.2 0.1 sum_parts.1.refs_0_
  43.3 1.4 %collective-permute-start.37 = (bf16[256,256]{1,0:T(8,128)(2,1)S(1)}, bf16[256,256]{1,0:T(8,128)(2,1)S(1)}, u32[]{:S(2)}, u32[]{:S(2)}) collective-permute-start(bf16[256,256]{1,0:T(8,128)(2,1)S(1)} %sum_parts.1.refs_0_), channel_id=1, source_target_pairs={{0,24},{4,28},{8,16},{12,20},{16,8},{20,12},{24,0},{28,4},{1,25},{... | collective-permute-start | bytes 393224 | tf_op jit(solution)/shard_map/ppermute | solution.py:240
  44.8 0.8 collective-permute-start.35
  45.5 1.3 %collective-permute-start.33 = (bf16[256,256]{1,0:T(8,128)(2,1)S(1)}, bf16[256,256]{1,0:T(8,128)(2,1)S(1)}, u32[]{:S(2)}, u32[]{:S(2)}) collective-permute-start(bf16[256,256]{1,0:T(8,128)(2,1)S(1)} %sum_parts.1.refs_0_), channel_id=1, source_target_pairs={{0,8},{4,12},{8,0},{12,4},{16,24},{20,28},{24,16},{28,20},{1,9},{5... | collective-permute-start | bytes 393224 | tf_op jit(solution)/shard_map/ppermute | solution.py:240
  46.9 0.5 collective-permute-start.32
  47.4 3.2 %collective-permute-done.37.refs_6_ = bf16[256,256]{1,0:T(8,128)(2,1)S(1)} collective-permute-done((bf16[256,256]{1,0:T(8,128)(2,1)S(1)}, bf16[256,256]{1,0:T(8,128)(2,1)S(1)}, u32[]{:S(2)}, u32[]{:S(2)}) %collective-permute-start.37) | collective-permute-done | bytes 131104 | tf_op jit(solution)/shard_map/ppermute | solution.py:240
  50.6 2.4 %collective-permute-done.35.refs_4_ = bf16[256,256]{1,0:T(8,128)(2,1)S(1)} collective-permute-done((bf16[256,256]{1,0:T(8,128)(2,1)S(1)}, bf16[256,256]{1,0:T(8,128)(2,1)S(1)}, u32[]{:S(2)}, u32[]{:S(2)}) %collective-permute-start.35) | collective-permute-done | bytes 131104 | tf_op jit(solution)/shard_map/ppermute | solution.py:240
  53.0 0.0 collective-permute-start.36
  53.1 0.5 collective-permute-start.34
  53.5 1.4 %weight_part.4 = (f32[128,256]{1,0:T(8,128)S(1)}, bf16[128,256]{1,0:T(8,128)(2,1)S(1)}, bf16[128,256]{1,0:T(8,128)(2,1)S(1)}, bf16[128,256]{1,0:T(8,128)(2,1)S(1)}) custom-call(s32[2]{0:T(128)S(1)} %pad_add_fusion.refs_0_.me_ref, bf16[2048,512]{1,0:T(8,128)(2,1)S(1)} %bitcast.7, bf16[256,256]{1,0:T(8,128)(2,1)S(1)} %get-tuple-element.39.refs_0_, ...), custom_call_target="tpu_custom_call" | custom-call | flops 536870912 | bytes 3145728 | tf_op jit(solution)/shard_map/weight_part/pallas_call | solution.py:193
  54.9 1.2 %collective-permute-start.26 = (bf16[128,256]{1,0:T(8,128)(2,1)S(1)}, bf16[128,256]{1,0:T(8,128)(2,1)S(1)}, u32[]{:S(2)}, u32[]{:S(2)}) collective-permute-start(bf16[128,256]{1,0:T(8,128)(2,1)S(1)} %get-tuple-element.28), channel_id=1, source_target_pairs={{0,1},{1,0},{2,3},{3,2},{4,5},{5,4},{6,7},{7,6},{8,9},{9,8},{10,11... | collective-permute-start | bytes 196616 | tf_op jit(solution)/shard_map/ppermute | solution.py:240
  56.1 1.4 %weight_part.3 = (f32[128,256]{1,0:T(8,128)S(1)}, bf16[128,256]{1,0:T(8,128)(2,1)S(1)}, bf16[128,256]{1,0:T(8,128)(2,1)S(1)}, bf16[128,256]{1,0:T(8,128)(2,1)S(1)}) custom-call(s32[2]{0:T(128)S(1)} %pad_add_fusion.refs_0_.me_ref, bf16[2048,512]{1,0:T(8,128)(2,1)S(1)} %bitcast.8, bf16[256,256]{1,0:T(8,128)(2,1)S(1)} %get-tuple-element.40.refs_0_, ...), custom_call_target="tpu_custom_call" | custom-call | flops 536870912 | bytes 3145728 | tf_op jit(solution)/shard_map/weight_part/pallas_call | solution.py:193
  57.5 3.3 %collective-permute-start.27 = (bf16[128,256]{1,0:T(8,128)(2,1)S(1)}, bf16[128,256]{1,0:T(8,128)(2,1)S(1)}, u32[]{:S(2)}, u32[]{:S(2)}) collective-permute-start(bf16[128,256]{1,0:T(8,128)(2,1)S(1)} %get-tuple-element.29), channel_id=1, source_target_pairs={{0,2},{1,3},{2,0},{3,1},{4,6},{5,7},{6,4},{7,5},{8,10},{9,11},{10,... | collective-permute-start | bytes 196616 | tf_op jit(solution)/shard_map/ppermute | solution.py:240
  60.7 0.1 collective-permute-start.28
  60.8 0.6 collective-permute-start.16
  61.4 3.7 %collective-permute-start.17 = (bf16[128,256]{1,0:T(8,128)(2,1)S(1)}, bf16[128,256]{1,0:T(8,128)(2,1)S(1)}, u32[]{:S(2)}, u32[]{:S(2)}) collective-permute-start(bf16[128,256]{1,0:T(8,128)(2,1)S(1)} %get-tuple-element.25), channel_id=1, source_target_pairs={{0,2},{1,3},{2,0},{3,1},{4,6},{5,7},{6,4},{7,5},{8,10},{9,11},{10,... | collective-permute-start | bytes 196616 | tf_op jit(solution)/shard_map/ppermute | solution.py:240
  65.1 1.4 %weight_part.5 = (f32[128,256]{1,0:T(8,128)S(1)}, bf16[128,256]{1,0:T(8,128)(2,1)S(1)}, bf16[128,256]{1,0:T(8,128)(2,1)S(1)}, bf16[128,256]{1,0:T(8,128)(2,1)S(1)}) custom-call(s32[2]{0:T(128)S(1)} %pad_add_fusion.refs_0_.me_ref, bf16[2048,512]{1,0:T(8,128)(2,1)S(1)} %bitcast.9, bf16[256,256]{1,0:T(8,128)(2,1)S(1)} %sum_parts.1.refs_0_, ...), custom_call_target="tpu_custom_call" | custom-call | flops 536870912 | bytes 3145728 | tf_op jit(solution)/shard_map/weight_part/pallas_call | solution.py:193
  66.5 0.1 collective-permute-start.18
  66.7 0.5 collective-permute-start.39
  67.2 0.4 collective-permute-done.28.refs_7_
  67.5 4.6 %collective-permute-start.40 = (bf16[128,256]{1,0:T(8,128)(2,1)S(1)}, bf16[128,256]{1,0:T(8,128)(2,1)S(1)}, u32[]{:S(2)}, u32[]{:S(2)}) collective-permute-start(bf16[128,256]{1,0:T(8,128)(2,1)S(1)} %get-tuple-element.37), channel_id=1, source_target_pairs={{0,2},{1,3},{2,0},{3,1},{4,6},{5,7},{6,4},{7,5},{8,10},{9,11},{10,... | collective-permute-start | bytes 196616 | tf_op jit(solution)/shard_map/ppermute | solution.py:240
  72.2 0.5 collective-permute-done.18.refs_3_
  72.7 3.6 %collective-permute-done.40.refs_10_ = bf16[128,256]{1,0:T(8,128)(2,1)S(1)} collective-permute-done((bf16[128,256]{1,0:T(8,128)(2,1)S(1)}, bf16[128,256]{1,0:T(8,128)(2,1)S(1)}, u32[]{:S(2)}, u32[]{:S(2)}) %collective-permute-start.40) | collective-permute-done | bytes 65568 | tf_op jit(solution)/shard_map/ppermute | solution.py:240
  76.3 1.9 %collective-permute-done.41.refs_11_ = bf16[128,256]{1,0:T(8,128)(2,1)S(1)} collective-permute-done((bf16[128,256]{1,0:T(8,128)(2,1)S(1)}, bf16[128,256]{1,0:T(8,128)(2,1)S(1)}, u32[]{:S(2)}, u32[]{:S(2)}) %collective-permute-start.41) | collective-permute-done | bytes 65568 | tf_op jit(solution)/shard_map/ppermute | solution.py:240
  78.2 0.8 %final_sum.1 = f32[128,768]{1,0:T(8,128)} custom-call(f32[128,256]{1,0:T(8,128)S(1)} %get-tuple-element.23.refs_0_, bf16[128,256]{1,0:T(8,128)(2,1)S(1)} %collective-permute-done.16.refs_1_, bf16[128,256]{1,0:T(8,128)(2,1)S(1)} %collective-permute-done.17.refs_2_, bf16[128,256]{1,0:T(8,128)(2,1)S(1)} %collective-permute-done.18.refs_3_, ...), custom_call_target="tpu_custom_call" | custom-call | tf_op jit(solution)/shard_map/final_sum/pallas_call | solution.py:229
  (39 shorter events, 0.1 us)
Async XLA Ops:
  0.0 53.5 %copy-start = (bf16[1,2048,512]{2,1,0:T(8,128)(2,1)S(1)}, bf16[1,2048,512]{2,1,0:T(8,128)(2,1)}, u32[]{:S(2)}) copy-start(bf16[1,2048,512]{2,1,0:T(8,128)(2,1)} %param.7) | copy-start | bytes 6291460
  1.0 7.9 %collective-permute-start.5 = (bf16[256,256]{1,0:T(8,128)(2,1)S(1)}, bf16[256,256]{1,0:T(8,128)(2,1)S(1)}, u32[]{:S(2)}, u32[]{:S(2)}) collective-permute-start(bf16[256,256]{1,0:T(8,128)(2,1)S(1)} %pad_maximum_fusion.refs_3_), channel_id=1, source_target_pairs={{0,24},{4,28},{8,16},{12,20},{16,8},{20,12},{24,0},{28,4},{1,25},{... | collective-permute-start | bytes 393224 | tf_op jit(solution)/shard_map/ppermute | solution.py:240
  5.0 6.3 %collective-permute-start.3 = (bf16[256,256]{1,0:T(8,128)(2,1)S(1)}, bf16[256,256]{1,0:T(8,128)(2,1)S(1)}, u32[]{:S(2)}, u32[]{:S(2)}) collective-permute-start(bf16[256,256]{1,0:T(8,128)(2,1)S(1)} %pad_maximum_fusion.refs_3_), channel_id=1, source_target_pairs={{0,16},{4,20},{8,24},{12,28},{16,0},{20,4},{24,8},{28,12},{1,17},{... | collective-permute-start | bytes 393224 | tf_op jit(solution)/shard_map/ppermute | solution.py:240
  5.5 6.0 %collective-permute-start.1 = (bf16[256,256]{1,0:T(8,128)(2,1)S(1)}, bf16[256,256]{1,0:T(8,128)(2,1)S(1)}, u32[]{:S(2)}, u32[]{:S(2)}) collective-permute-start(bf16[256,256]{1,0:T(8,128)(2,1)S(1)} %pad_maximum_fusion.refs_3_), channel_id=1, source_target_pairs={{0,8},{4,12},{8,0},{12,4},{16,24},{20,28},{24,16},{28,20},{1,9},{5... | collective-permute-start | bytes 393224 | tf_op jit(solution)/shard_map/ppermute | solution.py:240
  5.6 6.2 %collective-permute-start = (bf16[256,256]{1,0:T(8,128)(2,1)S(1)}, bf16[256,256]{1,0:T(8,128)(2,1)S(1)}, u32[]{:S(2)}, u32[]{:S(2)}) collective-permute-start(bf16[256,256]{1,0:T(8,128)(2,1)S(1)} %pad_maximum_fusion.refs_3_), channel_id=1, source_target_pairs={{0,4},{4,0},{8,12},{12,8},{16,20},{20,16},{24,28},{28,24},{1,5},{5... | collective-permute-start | bytes 393224 | tf_op jit(solution)/shard_map/ppermute | solution.py:240
  5.6 7.7 %collective-permute-start.7 = (bf16[256,512]{1,0:T(8,128)(2,1)}, bf16[256,512]{1,0:T(8,128)(2,1)S(1)}, u32[]{:S(2)}, u32[]{:S(2)}) collective-permute-start(bf16[256,512]{1,0:T(8,128)(2,1)} %bitcast.10), channel_id=1, source_target_pairs={{0,4},{4,0},{8,12},{12,8},{16,20},{20,16},{24,28},{28,24},{1,5},{5... | collective-permute-start | bytes 786440 | tf_op jit(solution)/shard_map/ppermute | solution.py:240
  8.9 4.4 %collective-permute-start.8 = (bf16[256,512]{1,0:T(8,128)(2,1)}, bf16[256,512]{1,0:T(8,128)(2,1)S(1)}, u32[]{:S(2)}, u32[]{:S(2)}) collective-permute-start(bf16[256,512]{1,0:T(8,128)(2,1)} %bitcast.12), channel_id=1, source_target_pairs={{0,4},{4,0},{8,12},{12,8},{16,20},{20,16},{24,28},{28,24},{1,5},{5... | collective-permute-start | bytes 786440 | tf_op jit(solution)/shard_map/ppermute | solution.py:240
  11.3 1.3 %collective-permute-start.6 = (bf16[256,256]{1,0:T(8,128)(2,1)S(1)}, bf16[256,256]{1,0:T(8,128)(2,1)S(1)}, u32[]{:S(2)}, u32[]{:S(2)}) collective-permute-start(bf16[256,256]{1,0:T(8,128)(2,1)S(1)} %collective-permute-done.5.refs_9_), channel_id=1, source_target_pairs={{0,4},{4,0},{8,12},{12,8},{16,20},{20,16},{24,28},{28,24},{1,5},{5... | collective-permute-start | bytes 393224 | tf_op jit(solution)/shard_map/ppermute | solution.py:240
  11.6 1.3 %collective-permute-start.4 = (bf16[256,256]{1,0:T(8,128)(2,1)S(1)}, bf16[256,256]{1,0:T(8,128)(2,1)S(1)}, u32[]{:S(2)}, u32[]{:S(2)}) collective-permute-start(bf16[256,256]{1,0:T(8,128)(2,1)S(1)} %collective-permute-done.3.refs_7_), channel_id=1, source_target_pairs={{0,4},{4,0},{8,12},{12,8},{16,20},{20,16},{24,28},{28,24},{1,5},{5... | collective-permute-start | bytes 393224 | tf_op jit(solution)/shard_map/ppermute | solution.py:240
  11.8 1.5 %collective-permute-start.2 = (bf16[256,256]{1,0:T(8,128)(2,1)S(1)}, bf16[256,256]{1,0:T(8,128)(2,1)}, u32[]{:S(2)}, u32[]{:S(2)}) collective-permute-start(bf16[256,256]{1,0:T(8,128)(2,1)S(1)} %collective-permute-done.1.refs_5_), channel_id=1, source_target_pairs={{0,4},{4,0},{8,12},{12,8},{16,20},{20,16},{24,28},{28,24},{1,5},{5... | collective-permute-start | bytes 393224 | tf_op jit(solution)/shard_map/ppermute | solution.py:240
  13.3 1.0 %copy-start.1 = (bf16[1,256,512]{2,1,0:T(8,128)(2,1)S(1)}, bf16[1,256,512]{2,1,0:T(8,128)(2,1)}, u32[]{:S(2)}) copy-start(bf16[1,256,512]{2,1,0:T(8,128)(2,1)} %param.8) | copy-start | bytes 786436
  14.3 0.9 %copy-start.2 = (bf16[1,256,512]{2,1,0:T(8,128)(2,1)S(1)}, bf16[1,256,512]{2,1,0:T(8,128)(2,1)}, u32[]{:S(2)}) copy-start(bf16[1,256,512]{2,1,0:T(8,128)(2,1)} %param.11) | copy-start | bytes 786436
  15.2 0.7 copy-start.3
  15.9 0.7 copy-start.4
  21.0 7.3 %collective-permute-start.24 = (bf16[256,256]{1,0:T(8,128)(2,1)S(1)}, bf16[256,256]{1,0:T(8,128)(2,1)S(1)}, u32[]{:S(2)}, u32[]{:S(2)}) collective-permute-start(bf16[256,256]{1,0:T(8,128)(2,1)S(1)} %get-tuple-element.39.refs_0_), channel_id=1, source_target_pairs={{0,24},{4,28},{8,16},{12,20},{16,8},{20,12},{24,0},{28,4},{1,25},{... | collective-permute-start | bytes 393224 | tf_op jit(solution)/shard_map/ppermute | solution.py:240
  22.9 8.4 %collective-permute-start.22 = (bf16[256,256]{1,0:T(8,128)(2,1)S(1)}, bf16[256,256]{1,0:T(8,128)(2,1)S(1)}, u32[]{:S(2)}, u32[]{:S(2)}) collective-permute-start(bf16[256,256]{1,0:T(8,128)(2,1)S(1)} %get-tuple-element.39.refs_0_), channel_id=1, source_target_pairs={{0,16},{4,20},{8,24},{12,28},{16,0},{20,4},{24,8},{28,12},{1,17},{... | collective-permute-start | bytes 393224 | tf_op jit(solution)/shard_map/ppermute | solution.py:240
  24.2 8.7 %collective-permute-start.20 = (bf16[256,256]{1,0:T(8,128)(2,1)S(1)}, bf16[256,256]{1,0:T(8,128)(2,1)S(1)}, u32[]{:S(2)}, u32[]{:S(2)}) collective-permute-start(bf16[256,256]{1,0:T(8,128)(2,1)S(1)} %get-tuple-element.39.refs_0_), channel_id=1, source_target_pairs={{0,8},{4,12},{8,0},{12,4},{16,24},{20,28},{24,16},{28,20},{1,9},{5... | collective-permute-start | bytes 393224 | tf_op jit(solution)/shard_map/ppermute | solution.py:240
  24.6 8.3 %collective-permute-start.19 = (bf16[256,256]{1,0:T(8,128)(2,1)S(1)}, bf16[256,256]{1,0:T(8,128)(2,1)S(1)}, u32[]{:S(2)}, u32[]{:S(2)}) collective-permute-start(bf16[256,256]{1,0:T(8,128)(2,1)S(1)} %get-tuple-element.39.refs_0_), channel_id=1, source_target_pairs={{0,4},{4,0},{8,12},{12,8},{16,20},{20,16},{24,28},{28,24},{1,5},{5... | collective-permute-start | bytes 393224 | tf_op jit(solution)/shard_map/ppermute | solution.py:240
  24.6 8.8 %collective-permute-start.14 = (bf16[256,256]{1,0:T(8,128)(2,1)S(1)}, bf16[256,256]{1,0:T(8,128)(2,1)S(1)}, u32[]{:S(2)}, u32[]{:S(2)}) collective-permute-start(bf16[256,256]{1,0:T(8,128)(2,1)S(1)} %get-tuple-element.40.refs_0_), channel_id=1, source_target_pairs={{0,24},{4,28},{8,16},{12,20},{16,8},{20,12},{24,0},{28,4},{1,25},{... | collective-permute-start | bytes 393224 | tf_op jit(solution)/shard_map/ppermute | solution.py:240
  28.3 7.8 %collective-permute-start.12 = (bf16[256,256]{1,0:T(8,128)(2,1)S(1)}, bf16[256,256]{1,0:T(8,128)(2,1)S(1)}, u32[]{:S(2)}, u32[]{:S(2)}) collective-permute-start(bf16[256,256]{1,0:T(8,128)(2,1)S(1)} %get-tuple-element.40.refs_0_), channel_id=1, source_target_pairs={{0,16},{4,20},{8,24},{12,28},{16,0},{20,4},{24,8},{28,12},{1,17},{... | collective-permute-start | bytes 393224 | tf_op jit(solution)/shard_map/ppermute | solution.py:240
  31.2 6.6 %collective-permute-start.10 = (bf16[256,256]{1,0:T(8,128)(2,1)S(1)}, bf16[256,256]{1,0:T(8,128)(2,1)S(1)}, u32[]{:S(2)}, u32[]{:S(2)}) collective-permute-start(bf16[256,256]{1,0:T(8,128)(2,1)S(1)} %get-tuple-element.40.refs_0_), channel_id=1, source_target_pairs={{0,8},{4,12},{8,0},{12,4},{16,24},{20,28},{24,16},{28,20},{1,9},{5... | collective-permute-start | bytes 393224 | tf_op jit(solution)/shard_map/ppermute | solution.py:240
  32.9 4.9 %collective-permute-start.9 = (bf16[256,256]{1,0:T(8,128)(2,1)S(1)}, bf16[256,256]{1,0:T(8,128)(2,1)S(1)}, u32[]{:S(2)}, u32[]{:S(2)}) collective-permute-start(bf16[256,256]{1,0:T(8,128)(2,1)S(1)} %get-tuple-element.40.refs_0_), channel_id=1, source_target_pairs={{0,4},{4,0},{8,12},{12,8},{16,20},{20,16},{24,28},{28,24},{1,5},{5... | collective-permute-start | bytes 393224 | tf_op jit(solution)/shard_map/ppermute | solution.py:240
  32.9 6.4 %collective-permute-start.29 = (bf16[256,256]{1,0:T(8,128)(2,1)S(1)}, bf16[256,256]{1,0:T(8,128)(2,1)S(1)}, u32[]{:S(2)}, u32[]{:S(2)}) collective-permute-start(bf16[256,256]{1,0:T(8,128)(2,1)S(1)} %get-tuple-element.32), channel_id=1, source_target_pairs={{0,8},{4,12},{8,0},{12,4},{16,24},{20,28},{24,16},{28,20},{1,9},{5... | collective-permute-start | bytes 393224 | tf_op jit(solution)/shard_map/ppermute | solution.py:240
  33.4 5.9 %collective-permute-start.30 = (bf16[256,256]{1,0:T(8,128)(2,1)S(1)}, bf16[256,256]{1,0:T(8,128)(2,1)S(1)}, u32[]{:S(2)}, u32[]{:S(2)}) collective-permute-start(bf16[256,256]{1,0:T(8,128)(2,1)S(1)} %get-tuple-element.33), channel_id=1, source_target_pairs={{0,16},{4,20},{8,24},{12,28},{16,0},{20,4},{24,8},{28,12},{1,17},{... | collective-permute-start | bytes 393224 | tf_op jit(solution)/shard_map/ppermute | solution.py:240
  36.1 7.2 %collective-permute-start.31 = (bf16[256,256]{1,0:T(8,128)(2,1)S(1)}, bf16[256,256]{1,0:T(8,128)(2,1)S(1)}, u32[]{:S(2)}, u32[]{:S(2)}) collective-permute-start(bf16[256,256]{1,0:T(8,128)(2,1)S(1)} %get-tuple-element.34), channel_id=1, source_target_pairs={{0,24},{4,28},{8,16},{12,20},{16,8},{20,12},{24,0},{28,4},{1,25},{... | collective-permute-start | bytes 393224 | tf_op jit(solution)/shard_map/ppermute | solution.py:240
  37.8 5.5 %collective-permute-start.25 = (bf16[256,256]{1,0:T(8,128)(2,1)S(1)}, bf16[256,256]{1,0:T(8,128)(2,1)S(1)}, u32[]{:S(2)}, u32[]{:S(2)}) collective-permute-start(bf16[256,256]{1,0:T(8,128)(2,1)S(1)} %collective-permute-done.24.refs_6_), channel_id=1, source_target_pairs={{0,4},{4,0},{8,12},{12,8},{16,20},{20,16},{24,28},{28,24},{1,5},{5... | collective-permute-start | bytes 393224 | tf_op jit(solution)/shard_map/ppermute | solution.py:240
  37.8 6.9 %collective-permute-start.23 = (bf16[256,256]{1,0:T(8,128)(2,1)S(1)}, bf16[256,256]{1,0:T(8,128)(2,1)S(1)}, u32[]{:S(2)}, u32[]{:S(2)}) collective-permute-start(bf16[256,256]{1,0:T(8,128)(2,1)S(1)} %collective-permute-done.22.refs_4_), channel_id=1, source_target_pairs={{0,4},{4,0},{8,12},{12,8},{16,20},{20,16},{24,28},{28,24},{1,5},{5... | collective-permute-start | bytes 393224 | tf_op jit(solution)/shard_map/ppermute | solution.py:240
  39.3 6.3 %collective-permute-start.21 = (bf16[256,256]{1,0:T(8,128)(2,1)S(1)}, bf16[256,256]{1,0:T(8,128)(2,1)S(1)}, u32[]{:S(2)}, u32[]{:S(2)}) collective-permute-start(bf16[256,256]{1,0:T(8,128)(2,1)S(1)} %collective-permute-done.20.refs_2_), channel_id=1, source_target_pairs={{0,4},{4,0},{8,12},{12,8},{16,20},{20,16},{24,28},{28,24},{1,5},{5... | collective-permute-start | bytes 393224 | tf_op jit(solution)/shard_map/ppermute | solution.py:240
  39.3 7.6 %collective-permute-start.15 = (bf16[256,256]{1,0:T(8,128)(2,1)S(1)}, bf16[256,256]{1,0:T(8,128)(2,1)S(1)}, u32[]{:S(2)}, u32[]{:S(2)}) collective-permute-start(bf16[256,256]{1,0:T(8,128)(2,1)S(1)} %collective-permute-done.14.refs_6_), channel_id=1, source_target_pairs={{0,4},{4,0},{8,12},{12,8},{16,20},{20,16},{24,28},{28,24},{1,5},{5... | collective-permute-start | bytes 393224 | tf_op jit(solution)/shard_map/ppermute | solution.py:240
  43.2 3.7 %collective-permute-start.13 = (bf16[256,256]{1,0:T(8,128)(2,1)S(1)}, bf16[256,256]{1,0:T(8,128)(2,1)S(1)}, u32[]{:S(2)}, u32[]{:S(2)}) collective-permute-start(bf16[256,256]{1,0:T(8,128)(2,1)S(1)} %collective-permute-done.12.refs_4_), channel_id=1, source_target_pairs={{0,4},{4,0},{8,12},{12,8},{16,20},{20,16},{24,28},{28,24},{1,5},{5... | collective-permute-start | bytes 393224 | tf_op jit(solution)/shard_map/ppermute | solution.py:240
  43.3 7.3 %collective-permute-start.37 = (bf16[256,256]{1,0:T(8,128)(2,1)S(1)}, bf16[256,256]{1,0:T(8,128)(2,1)S(1)}, u32[]{:S(2)}, u32[]{:S(2)}) collective-permute-start(bf16[256,256]{1,0:T(8,128)(2,1)S(1)} %sum_parts.1.refs_0_), channel_id=1, source_target_pairs={{0,24},{4,28},{8,16},{12,20},{16,8},{20,12},{24,0},{28,4},{1,25},{... | collective-permute-start | bytes 393224 | tf_op jit(solution)/shard_map/ppermute | solution.py:240
  44.8 8.2 %collective-permute-start.35 = (bf16[256,256]{1,0:T(8,128)(2,1)S(1)}, bf16[256,256]{1,0:T(8,128)(2,1)S(1)}, u32[]{:S(2)}, u32[]{:S(2)}) collective-permute-start(bf16[256,256]{1,0:T(8,128)(2,1)S(1)} %sum_parts.1.refs_0_), channel_id=1, source_target_pairs={{0,16},{4,20},{8,24},{12,28},{16,0},{20,4},{24,8},{28,12},{1,17},{... | collective-permute-start | bytes 393224 | tf_op jit(solution)/shard_map/ppermute | solution.py:240
  45.5 7.5 %collective-permute-start.33 = (bf16[256,256]{1,0:T(8,128)(2,1)S(1)}, bf16[256,256]{1,0:T(8,128)(2,1)S(1)}, u32[]{:S(2)}, u32[]{:S(2)}) collective-permute-start(bf16[256,256]{1,0:T(8,128)(2,1)S(1)} %sum_parts.1.refs_0_), channel_id=1, source_target_pairs={{0,8},{4,12},{8,0},{12,4},{16,24},{20,28},{24,16},{28,20},{1,9},{5... | collective-permute-start | bytes 393224 | tf_op jit(solution)/shard_map/ppermute | solution.py:240
  46.9 8.0 %collective-permute-start.11 = (bf16[256,256]{1,0:T(8,128)(2,1)S(1)}, bf16[256,256]{1,0:T(8,128)(2,1)S(1)}, u32[]{:S(2)}, u32[]{:S(2)}) collective-permute-start(bf16[256,256]{1,0:T(8,128)(2,1)S(1)} %collective-permute-done.10.refs_2_), channel_id=1, source_target_pairs={{0,4},{4,0},{8,12},{12,8},{16,20},{20,16},{24,28},{28,24},{1,5},{5... | collective-permute-start | bytes 393224 | tf_op jit(solution)/shard_map/ppermute | solution.py:240
  46.9 10.5 %collective-permute-start.32 = (bf16[256,256]{1,0:T(8,128)(2,1)S(1)}, bf16[256,256]{1,0:T(8,128)(2,1)S(1)}, u32[]{:S(2)}, u32[]{:S(2)}) collective-permute-start(bf16[256,256]{1,0:T(8,128)(2,1)S(1)} %sum_parts.1.refs_0_), channel_id=1, source_target_pairs={{0,4},{4,0},{8,12},{12,8},{16,20},{20,16},{24,28},{28,24},{1,5},{5... | collective-permute-start | bytes 393224 | tf_op jit(solution)/shard_map/ppermute | solution.py:240
  50.6 10.1 %collective-permute-start.38 = (bf16[256,256]{1,0:T(8,128)(2,1)S(1)}, bf16[256,256]{1,0:T(8,128)(2,1)S(1)}, u32[]{:S(2)}, u32[]{:S(2)}) collective-permute-start(bf16[256,256]{1,0:T(8,128)(2,1)S(1)} %collective-permute-done.37.refs_6_), channel_id=1, source_target_pairs={{0,4},{4,0},{8,12},{12,8},{16,20},{20,16},{24,28},{28,24},{1,5},{5... | collective-permute-start | bytes 393224 | tf_op jit(solution)/shard_map/ppermute | solution.py:240
  53.0 7.8 %collective-permute-start.36 = (bf16[256,256]{1,0:T(8,128)(2,1)S(1)}, bf16[256,256]{1,0:T(8,128)(2,1)S(1)}, u32[]{:S(2)}, u32[]{:S(2)}) collective-permute-start(bf16[256,256]{1,0:T(8,128)(2,1)S(1)} %collective-permute-done.35.refs_4_), channel_id=1, source_target_pairs={{0,4},{4,0},{8,12},{12,8},{16,20},{20,16},{24,28},{28,24},{1,5},{5... | collective-permute-start | bytes 393224 | tf_op jit(solution)/shard_map/ppermute | solution.py:240
  53.1 8.3 %collective-permute-start.34 = (bf16[256,256]{1,0:T(8,128)(2,1)S(1)}, bf16[256,256]{1,0:T(8,128)(2,1)S(1)}, u32[]{:S(2)}, u32[]{:S(2)}) collective-permute-start(bf16[256,256]{1,0:T(8,128)(2,1)S(1)} %collective-permute-done.33.refs_2_), channel_id=1, source_target_pairs={{0,4},{4,0},{8,12},{12,8},{16,20},{20,16},{24,28},{28,24},{1,5},{5... | collective-permute-start | bytes 393224 | tf_op jit(solution)/shard_map/ppermute | solution.py:240
  54.9 11.6 %collective-permute-start.26 = (bf16[128,256]{1,0:T(8,128)(2,1)S(1)}, bf16[128,256]{1,0:T(8,128)(2,1)S(1)}, u32[]{:S(2)}, u32[]{:S(2)}) collective-permute-start(bf16[128,256]{1,0:T(8,128)(2,1)S(1)} %get-tuple-element.28), channel_id=1, source_target_pairs={{0,1},{1,0},{2,3},{3,2},{4,5},{5,4},{6,7},{7,6},{8,9},{9,8},{10,11... | collective-permute-start | bytes 196616 | tf_op jit(solution)/shard_map/ppermute | solution.py:240
  57.5 9.2 %collective-permute-start.27 = (bf16[128,256]{1,0:T(8,128)(2,1)S(1)}, bf16[128,256]{1,0:T(8,128)(2,1)S(1)}, u32[]{:S(2)}, u32[]{:S(2)}) collective-permute-start(bf16[128,256]{1,0:T(8,128)(2,1)S(1)} %get-tuple-element.29), channel_id=1, source_target_pairs={{0,2},{1,3},{2,0},{3,1},{4,6},{5,7},{6,4},{7,5},{8,10},{9,11},{10,... | collective-permute-start | bytes 196616 | tf_op jit(solution)/shard_map/ppermute | solution.py:240
  60.7 6.8 %collective-permute-start.28 = (bf16[128,256]{1,0:T(8,128)(2,1)S(1)}, bf16[128,256]{1,0:T(8,128)(2,1)S(1)}, u32[]{:S(2)}, u32[]{:S(2)}) collective-permute-start(bf16[128,256]{1,0:T(8,128)(2,1)S(1)} %get-tuple-element.30), channel_id=1, source_target_pairs={{0,3},{1,2},{2,1},{3,0},{4,7},{5,6},{6,5},{7,4},{8,11},{9,10},{10,... | collective-permute-start | bytes 196616 | tf_op jit(solution)/shard_map/ppermute | solution.py:240
  60.8 11.4 %collective-permute-start.16 = (bf16[128,256]{1,0:T(8,128)(2,1)S(1)}, bf16[128,256]{1,0:T(8,128)(2,1)S(1)}, u32[]{:S(2)}, u32[]{:S(2)}) collective-permute-start(bf16[128,256]{1,0:T(8,128)(2,1)S(1)} %get-tuple-element.24), channel_id=1, source_target_pairs={{0,1},{1,0},{2,3},{3,2},{4,5},{5,4},{6,7},{7,6},{8,9},{9,8},{10,11... | collective-permute-start | bytes 196616 | tf_op jit(solution)/shard_map/ppermute | solution.py:240
  61.4 10.8 %collective-permute-start.17 = (bf16[128,256]{1,0:T(8,128)(2,1)S(1)}, bf16[128,256]{1,0:T(8,128)(2,1)S(1)}, u32[]{:S(2)}, u32[]{:S(2)}) collective-permute-start(bf16[128,256]{1,0:T(8,128)(2,1)S(1)} %get-tuple-element.25), channel_id=1, source_target_pairs={{0,2},{1,3},{2,0},{3,1},{4,6},{5,7},{6,4},{7,5},{8,10},{9,11},{10,... | collective-permute-start | bytes 196616 | tf_op jit(solution)/shard_map/ppermute | solution.py:240
  66.5 6.1 %collective-permute-start.18 = (bf16[128,256]{1,0:T(8,128)(2,1)S(1)}, bf16[128,256]{1,0:T(8,128)(2,1)S(1)}, u32[]{:S(2)}, u32[]{:S(2)}) collective-permute-start(bf16[128,256]{1,0:T(8,128)(2,1)S(1)} %get-tuple-element.26), channel_id=1, source_target_pairs={{0,3},{1,2},{2,1},{3,0},{4,7},{5,6},{6,5},{7,4},{8,11},{9,10},{10,... | collective-permute-start | bytes 196616 | tf_op jit(solution)/shard_map/ppermute | solution.py:240
  66.7 6.0 %collective-permute-start.39 = (bf16[128,256]{1,0:T(8,128)(2,1)S(1)}, bf16[128,256]{1,0:T(8,128)(2,1)S(1)}, u32[]{:S(2)}, u32[]{:S(2)}) collective-permute-start(bf16[128,256]{1,0:T(8,128)(2,1)S(1)} %get-tuple-element.36), channel_id=1, source_target_pairs={{0,1},{1,0},{2,3},{3,2},{4,5},{5,4},{6,7},{7,6},{8,9},{9,8},{10,11... | collective-permute-start | bytes 196616 | tf_op jit(solution)/shard_map/ppermute | solution.py:240
  67.5 8.8 %collective-permute-start.40 = (bf16[128,256]{1,0:T(8,128)(2,1)S(1)}, bf16[128,256]{1,0:T(8,128)(2,1)S(1)}, u32[]{:S(2)}, u32[]{:S(2)}) collective-permute-start(bf16[128,256]{1,0:T(8,128)(2,1)S(1)} %get-tuple-element.37), channel_id=1, source_target_pairs={{0,2},{1,3},{2,0},{3,1},{4,6},{5,7},{6,4},{7,5},{8,10},{9,11},{10,... | collective-permute-start | bytes 196616 | tf_op jit(solution)/shard_map/ppermute | solution.py:240
  72.2 6.1 %collective-permute-start.41 = (bf16[128,256]{1,0:T(8,128)(2,1)S(1)}, bf16[128,256]{1,0:T(8,128)(2,1)S(1)}, u32[]{:S(2)}, u32[]{:S(2)}) collective-permute-start(bf16[128,256]{1,0:T(8,128)(2,1)S(1)} %get-tuple-element.38), channel_id=1, source_target_pairs={{0,3},{1,2},{2,1},{3,0},{4,7},{5,6},{6,5},{7,4},{8,11},{9,10},{10,... | collective-permute-start | bytes 196616 | tf_op jit(solution)/shard_map/ppermute | solution.py:240

commit v3 on v2

v3 whole, which is shorter than its diff:
```python
import functools
import math

import jax
import jax.numpy as jnp
from jax import lax
from jax.experimental import pallas as pl
from jax.experimental.pallas import tpu as pltpu
from jax.sharding import PartitionSpec as P

masked_fill = -1e30
MOST_DOC = 4
TOGETHER = 2
AT_ONCE = {1: (4, 2, 1), 2: (2, 1), 3: (1,), 4: (1,)}
VMEM_LIMIT = 24 * 1024 * 1024

NT = (((1,), (1,)), ((), ()))
NN = (((1,), (0,)), ((), ()))
TN = (((0,), (0,)), ((), ()))


def dot(a, b, dims):
    return lax.dot_general(a, b, dims, preferred_element_type=jnp.float32)


def smem():
    return pl.BlockSpec(memory_space=pltpu.SMEM)


def vmem():
    return pl.BlockSpec(memory_space=pltpu.VMEM)


def kernel_params():
    return pltpu.CompilerParams(vmem_limit_bytes=VMEM_LIMIT)


def swap(x, axis, rel):
    return lax.ppermute(x, axis, [(i, i ^ rel) for i in range(lax.axis_size(axis))])


def routes(shards):
    bits = [1 << b for b in range(1, shards.bit_length() - 1)]
    return bits, bits[::-1]


def across(x, step):
    shards = lax.axis_size("seq")
    even, odd = routes(shards)
    pairs = [(i, i ^ (odd if i & 1 else even)[step]) for i in range(shards)]
    return lax.ppermute(x, "seq", pairs)


def from_chips(x):
    chunks = [x]
    for step in range(len(routes(lax.axis_size("seq"))[0])):
        chunks += [across(chunk, step) for chunk in chunks]
    return chunks


def with_other_core(chunks):
    return [part for chunk in chunks for part in (chunk, swap(chunk, "seq", 1))]


def origin(me, place, shards):
    def offset(order):
        return sum(bit for j, bit in enumerate(order) if (place >> 1) >> j & 1)

    even, odd = (offset(order) for order in routes(shards))
    core = me & 1
    if place & 1:
        return me ^ 1 ^ (odd + (even - odd) * core)
    return me ^ (even + (odd - even) * core)


def attention_kernel(shards, blocks, heads, hd, kv_at, q_at, scaling, last, *refs):
    meta = refs[0]
    kv_refs = refs[1 : 1 + shards]
    q_refs = refs[1 + shards : 1 + 2 * shards]
    refs = refs[1 + 2 * shards :]
    if last:
        dk_before, dv_before, dq_ref, dk_ref, dv_ref = refs[:5]
        refs = refs[5:]
    else:
        dq_ref, dk_ref, dv_ref = refs[:3]
        refs = refs[3:]
    keys, values, queries, grads, inverse, starts = refs
    me = meta[0]
    per_dev = blocks // shards
    span = keys.shape[0] // blocks
    qw = heads * hd

    def document(place):
        return meta[2 + blocks + place]

    def rows_at(first, count):
        return pl.ds(pl.multiple_of(first * span, span), count * span)

    for place in range(shards):
        device = origin(me, place, shards)
        for b in range(per_dev):
            storage = device * per_dev + b
            position = meta[2 + storage]
            inverse[position] = storage
            rows = rows_at(position, 1)
            here = slice(b * span, (b + 1) * span)
            keys[rows, :] = kv_refs[place][here, kv_at : kv_at + hd]
            values[rows, :] = kv_refs[place][here, kv_at + hd : kv_at + 2 * hd]
            queries[rows, :] = q_refs[place][here, q_at : q_at + qw]
            grads[rows, :] = q_refs[place][here, q_at + qw : q_at + 2 * qw]

    def note(state):
        first, counts = state[0], state[1:]
        size = jnp.int32(1)
        for ahead in range(1, MOST_DOC):
            at = jnp.minimum(first + ahead, blocks - 1)
            same = (first + ahead < blocks) & (document(at) == document(first))
            size = size + same.astype(jnp.int32)
        listed = counts[0]
        for n in range(2, MOST_DOC + 1):
            listed = jnp.where(size == n, counts[n - 1], listed)
        starts[(size - 1) * blocks + listed] = first
        counts = tuple(
            count + (size == n + 1).astype(jnp.int32) for n, count in enumerate(counts)
        )
        return (first + size,) + counts

    listed = lax.while_loop(
        lambda state: state[0] < blocks, note, (jnp.int32(0),) * (MOST_DOC + 1)
    )[1:]

    def stacked(ref, first, count):
        return jnp.concatenate(
            [ref[rows_at(first, count), h * hd : (h + 1) * hd] for h in range(heads)], axis=0
        )

    def masked(scores, before, count):
        square = (count * span, heads * count * span)
        key_at = lax.broadcasted_iota(jnp.int32, square, 0)
        query_at = lax.rem(lax.broadcasted_iota(jnp.int32, square, 1), count * span)
        diagonal = jnp.where(key_at <= query_at, scores[before * span :], masked_fill)
        if not before:
            return diagonal
        return jnp.concatenate([scores[: before * span], diagonal], axis=0)

    def step(firsts, size):
        parts = [
            (first, before, min(TOGETHER, size - before))
            for first in firsts
            for before in range(0, size, TOGETHER)
        ]
        q_cats = [stacked(queries, first + before, count) for first, before, count in parts]
        g_cats = [stacked(grads, first + before, count) for first, before, count in parts]
        key_wins = [keys[rows_at(first, before + count), :] for first, before, count in parts]
        value_wins = [values[rows_at(first, before + count), :] for first, before, count in parts]
        scores = [dot(key_win, q_cat, NT) for key_win, q_cat in zip(key_wins, q_cats)]
        dprobs = [dot(value_win, g_cat, NT) for value_win, g_cat in zip(value_wins, g_cats)]
        scores = [masked(s, before, count) for s, (_, before, count) in zip(scores, parts)]
        peaks = [jnp.max(s, axis=0, keepdims=True) for s in scores]
        weights = [
            jnp.exp2((s - peak) * (scaling * math.log2(math.e)))
            for s, peak in zip(scores, peaks)
        ]
        shares = [1.0 / jnp.sum(w, axis=0, keepdims=True) for w in weights]
        probs = [w * share for w, share in zip(weights, shares)]
        probs_b = [p.astype(jnp.bfloat16) for p in probs]
        deltas = [
            jnp.sum(p.astype(jnp.float32) * dp, axis=0, keepdims=True)
            for p, dp in zip(probs_b, dprobs)
        ]
        dscores = [
            (p * (dp - delta)).astype(jnp.bfloat16)
            for p, dp, delta in zip(probs, dprobs, deltas)
        ]
        dks = [dot(ds, q_cat, NN) for ds, q_cat in zip(dscores, q_cats)]
        dvs = [dot(p, g_cat, NN) for p, g_cat in zip(probs_b, g_cats)]
        dqs = [
            (dot(ds, key_win, TN) * scaling).astype(jnp.bfloat16)
            for ds, key_win in zip(dscores, key_wins)
        ]
        for dq, (first, before, count) in zip(dqs, parts):
            for t in range(count):
                at = rows_at(inverse[first + before + t], 1)
                for h in range(heads):
                    start = (h * count + t) * span
                    dq_ref[at, h * hd : (h + 1) * hd] = dq[start : start + span]
        for first in firsts:
            for j in range(size):
                reach = [
                    i
                    for i, (start, before, count) in enumerate(parts)
                    if start is first and before + count > j
                ]
                rows = slice(j * span, (j + 1) * span)
                dk = sum(dks[i][rows] for i in reach) * scaling
                dv = sum(dvs[i][rows] for i in reach)
                at = rows_at(inverse[first + j], 1)
                if last:
                    dk, dv = dk + dk_before[at, :], dv + dv_before[at, :]
                dk_ref[at, :] = dk.astype(dk_ref.dtype)
                dv_ref[at, :] = dv.astype(dv_ref.dtype)

    for size in range(MOST_DOC, 0, -1):
        done = jnp.int32(0)
        for together in AT_ONCE[size]:
            times = (listed[size - 1] - done) // together

            def some(k, carry, size=size, together=together, done=done):
                at = (size - 1) * blocks + done + k * together
                step([starts[at + d] for d in range(together)], size)
                return carry

            lax.fori_loop(0, times, some, jnp.int32(0))
            done = done + times * together


def attention(meta, blocks, hd, heads, kv_chunks, kv_at, q_chunks, q_at, before, last):
    shards = len(kv_chunks)
    length = kv_chunks[0].shape[0] * shards
    qw = heads * hd
    sums = jnp.bfloat16 if last else jnp.float32
    return pl.pallas_call(
        functools.partial(
            attention_kernel, shards, blocks, heads, hd, kv_at, q_at, hd**-0.5, last
        ),
        out_shape=(
            jax.ShapeDtypeStruct((length, qw), jnp.bfloat16),
            jax.ShapeDtypeStruct((length, hd), sums),
            jax.ShapeDtypeStruct((length, hd), sums),
        ),
        in_specs=[smem()] + [vmem()] * (2 * shards + len(before)),
        out_specs=(vmem(),) * 3,
        scratch_shapes=[
            pltpu.VMEM((length, hd), jnp.bfloat16),
            pltpu.VMEM((length, hd), jnp.bfloat16),
            pltpu.VMEM((length, qw), jnp.bfloat16),
            pltpu.VMEM((length, qw), jnp.bfloat16),
            pltpu.SMEM((blocks,), jnp.int32),
            pltpu.SMEM((MOST_DOC * blocks,), jnp.int32),
        ],
        compiler_params=kernel_params(),
        cost_estimate=pl.CostEstimate(
            flops=10 * 2 * length * span_of(length, blocks) * qw,
            bytes_accessed=24 * length * qw,
            transcendentals=2 * length * span_of(length, blocks) * heads,
        ),
        name="attention",
    )(meta, *kv_chunks, *q_chunks, *before)


def span_of(length, blocks):
    return length // blocks


def weight_kernel(owners, parts, meta, slab_ref, *refs):
    rows_refs = refs[:parts]
    own_ref = refs[parts]
    sends = refs[parts + 1 : parts + owners]
    total = refs[-1]
    my_dp = meta[1]
    first = 0
    for ref in rows_refs:
        width = ref.shape[1]
        total[:, first : first + width] = dot(slab_ref[...], ref[...], TN)
        first += width
    piece = total.shape[0] // owners
    for rel in range(owners):
        rows = pl.ds(pl.multiple_of((my_dp ^ rel) * piece, piece), piece)
        if rel == 0:
            own_ref[...] = total[rows, :]
        else:
            sends[rel - 1][...] = total[rows, :].astype(jnp.bfloat16)


def weight_part(meta, slab, grads, owners):
    length, features = slab.shape
    columns = sum(part.shape[1] for part in grads)
    piece = features // owners
    return pl.pallas_call(
        functools.partial(weight_kernel, owners, len(grads)),
        out_shape=(jax.ShapeDtypeStruct((piece, columns), jnp.float32),)
        + (jax.ShapeDtypeStruct((piece, columns), jnp.bfloat16),) * (owners - 1),
        in_specs=[smem()] + [vmem()] * (1 + len(grads)),
        out_specs=(vmem(),) * owners,
        scratch_shapes=[pltpu.VMEM((features, columns), jnp.float32)],
        compiler_params=kernel_params(),
        cost_estimate=pl.CostEstimate(
            flops=2 * length * features * columns,
            bytes_accessed=2 * length * (features + columns),
            transcendentals=0,
        ),
        name="weight_part",
    )(meta, slab, *grads)


def final_kernel(groups, owners, *refs):
    out_ref = refs[-1]
    first = 0
    for g in range(groups):
        own = refs[g * owners]
        total = own[...]
        for rel in range(1, owners):
            total = total + refs[g * owners + rel][...].astype(jnp.float32)
        for columns, width in out_columns(g, groups, own.shape[1], out_ref.shape[1]):
            out_ref[:, columns : columns + width] = total[:, first : first + width]
            first += width
        first = 0


def out_columns(group, groups, width, whole):
    return [(0, width)] if group == 0 else [(whole - width, width)]


def final_sum(parts):
    groups, owners = len(parts), len(parts[0])
    flat = [array for group in parts for array in group]
    columns = sum(group[0].shape[1] for group in parts)
    return pl.pallas_call(
        functools.partial(final_kernel, groups, owners),
        out_shape=jax.ShapeDtypeStruct((flat[0].shape[0], columns), jnp.float32),
        in_specs=[vmem()] * len(flat),
        out_specs=vmem(),
        compiler_params=kernel_params(),
        name="final_sum",
    )(*flat)


def ordered(first, later):
    return lax.optimization_barrier((first, later))


def body(layer_input, query_proj, key_proj, value_proj, out_grad, block_pos, doc_ids):
    dp = lax.axis_size("dp")
    blocks = block_pos.shape[1]
    hd = key_proj.shape[2]
    qw = query_proj.shape[2]
    half = qw // 2
    heads = half // hd
    me = jnp.stack([lax.axis_index("seq"), lax.axis_index("dp")]).astype(jnp.int32)
    meta = jnp.concatenate([me, block_pos[0], doc_ids[0]])
    slab = layer_input[0]

    first = jnp.concatenate(
        [key_proj[0], value_proj[0], query_proj[0, :, :half], out_grad[0, :, :half]], axis=1
    )
    first_sent = [across(first, step) for step in range(2)]
    first_sent[0], (queries, grads, meta) = ordered(
        first_sent[0], (query_proj[0], out_grad[0], meta)
    )
    first_sent.append(across(first_sent[0], 1))
    second = jnp.concatenate([queries[:, half:], grads[:, half:]], axis=1)
    second_sent = [across(second, step) for step in range(2)]
    first_sent, second_sent = ordered(first_sent, second_sent)
    second_sent.append(across(second_sent[0], 1))
    first_chunks = with_other_core([first] + first_sent)

    exchange = dp <= 8 and dp & (dp - 1) == 0
    owners = dp if exchange else 1

    def over_dp(terms):
        return [terms[0]] + [swap(term, "dp", i + 1) for i, term in enumerate(terms[1:])]

    early, *sums = attention(
        meta, blocks, hd, heads, first_chunks, 0, first_chunks, 2 * hd, [], False
    )
    second_sent, early = ordered(second_sent, early)
    second_chunks = with_other_core([second] + second_sent)
    early_terms = over_dp(weight_part(meta, slab, [early], owners))
    late, dk, dv = attention(
        meta, blocks, hd, heads, first_chunks, 0, second_chunks, 0, sums, True
    )
    early_terms, late = ordered(early_terms, late)
    late_terms = over_dp(weight_part(meta, slab, [late, dk, dv], owners))
    groups = (early_terms, late_terms)
    if exchange:
        return final_sum(groups)
    return lax.psum_scatter(
        jnp.concatenate([terms[0] for terms in groups], axis=1),
        "dp",
        scatter_dimension=0,
        tiled=True,
    )


def solution(mesh):
    placed = (
        P("dp", None, "seq"),
        P("dp", "seq", None),
        P("dp", "seq", None),
        P("dp", "seq", None),
        P("dp", "seq", None),
        P("dp", None),
        P("dp", None),
    )
    return jax.shard_map(
        body, mesh=mesh, in_specs=placed, out_specs=P(("seq", "dp"), None), check_vma=False
    )
```

time: 78.9 us -> 68.4 us (0.87)
  starting transfers between devices: 38 us -> 21.9 us
  Pallas kernels: 9.48 us -> 18.4 us
  waiting for transfers between devices: 27.1 us -> 23.2 us
    ppermute x42 -> x14, starting transfers between devices: 38 us -> 11.2 us  [swap(): lax.ppermute(x, axis, [(i, i ^ rel) for i in range(lax.axis_size(axis))])]
    ppermute x42 -> x14, waiting for transfers between devices: 27.1 us -> 9.12 us  [swap(): lax.ppermute(x, axis, [(i, i ^ rel) for i in range(lax.axis_size(axis))])]
    ppermute x0 -> x6, waiting for transfers between devices: none -> 14.1 us  [across(): return lax.ppermute(x, 'seq', pairs)]
    ppermute x0 -> x6, starting transfers between devices: none -> 10.7 us  [across(): return lax.ppermute(x, 'seq', pairs)]
    pallas_call x1 -> x2, Pallas kernels: 4.47 us -> 13.8 us  [attention(): pl.pallas_call(functools.partial(attention_kernel, shards, blocks, heads,...]
    unnamed x10 -> x2, local copies, waits for them, and re-layouts: 3.21 us -> 0.01 us
    slice x1 -> x2, local copies, waits for them, and re-layouts: 0.02 us -> 1.83 us  [body(): second = jnp.concatenate([queries[:, half:], grads[:, half:]], axis=1)]
    squeeze x0 -> x1, local copies, waits for them, and re-layouts: none -> 0.98 us  [body(): out_grad[0, :, :half]]
  transfers between devices with their start and end apart: 42 -> 20, of which waited for: 18 -> 4; matrix products, arithmetic and copies ran while one was open for 0% -> 4% of each run, Pallas kernels for 5% -> 22%
where the time goes in v3:
time: 68.4 us; the launch traced here: 68.1 us
  waiting for transfers between devices  23.2 us (34%)
  starting transfers between devices  21.9 us (32%)
  Pallas kernels  18.4 us (27%)
  local copies, waits for them, and re-layouts  2.82 us (4%)
  other arithmetic  1.67 us (2%)
    ppermute x6, waiting for transfers between devices, across(): return lax.ppermute(x, 'seq', pairs)  14.1 us
    pallas_call x2, Pallas kernels, attention(): pl.pallas_call(functools.partial(attention_kernel, shards, blocks, heads,...  13.8 us
    ppermute x14, starting transfers between devices, swap(): lax.ppermute(x, axis, [(i, i ^ rel) for i in range(lax.axis_size(axis))])  11.2 us
    ppermute x6, starting transfers between devices, across(): return lax.ppermute(x, 'seq', pairs)  10.7 us
    ppermute x14, waiting for transfers between devices, swap(): lax.ppermute(x, axis, [(i, i ^ rel) for i in range(lax.axis_size(axis))])  9.12 us
    pallas_call x2, Pallas kernels, weight_part(): pl.pallas_call(functools.partial(weight_kernel, owners, len(grads)), out_...  3.76 us
    slice x2, local copies, waits for them, and re-layouts, body(): second = jnp.concatenate([queries[:, half:], grads[:, half:]], axis=1)  1.83 us
  transfers between devices with their start and end apart: 20, of which 4 were waited for; matrix products, arithmetic and copies ran while one was open for 4% of the time, Pallas kernels for 22%

profile of v3, /device:TPU:0, one launch (start us, length us, event | category | flops | bytes accessed | tf_op | source)
XLA Modules:
  0.0 68.1 jit_solution(6049354448286094476)
XLA Ops:
  0.0 1.0 %slice_bitcast_fusion = (bf16[256,256]{1,0:T(8,128)(2,1)S(1)}, bf16[256,256]{1,0:T(8,128)(2,1)S(1)}) fusion(bf16[1,256,512]{2,1,0:T(8,128)(2,1)} %param.11, bf16[1,256,512]{2,1,0:T(8,128)(2,1)} %param.8), kind=kLoop, calls=%fused_computation.2 | loop fusion | bytes 524288 | tf_op jit(solution)/shard_map/squeeze | solution.py:344
  1.0 0.9 %pad_maximum_fusion.refs_1_.refs_9_ = bf16[256,768]{1,0:T(8,128)(2,1)S(1)} fusion(bf16[256,256]{1,0:T(8,128)(2,1)S(1)} %get-tuple-element.69, bf16[256,256]{1,0:T(8,128)(2,1)S(1)} %get-tuple-element.70, bf16[256,128]{1,0:T(8,128)(2,1)} %bitcast.17, bf16[256,128]{1,0:T(8,128)(2,1)} %bitcast.18), kind=kLoop, calls=%fused_computation | loop fusion | flops 1572864 | bytes 786432 | tf_op jit(solution)/shard_map/concatenate | solution.py:343
  1.9 3.0 %collective-permute-start = (bf16[256,768]{1,0:T(8,128)(2,1)S(1)}, bf16[256,768]{1,0:T(8,128)(2,1)S(1)}, u32[]{:S(2)}, u32[]{:S(2)}) collective-permute-start(bf16[256,768]{1,0:T(8,128)(2,1)S(1)} %pad_maximum_fusion.refs_1_.refs_9_), channel_id=1, source_target_pairs={{0,8},{4,20},{8,0},{12,28},{16,24},{20,4},{24,16},{28,12},{1,9},{5... | collective-permute-start | bytes 1179656 | tf_op jit(solution)/shard_map/ppermute | solution.py:51
  4.9 1.5 %collective-permute-start.1 = (bf16[256,768]{1,0:T(8,128)(2,1)S(1)}, bf16[256,768]{1,0:T(8,128)(2,1)S(1)}, u32[]{:S(2)}, u32[]{:S(2)}) collective-permute-start(bf16[256,768]{1,0:T(8,128)(2,1)S(1)} %pad_maximum_fusion.refs_1_.refs_9_), channel_id=1, source_target_pairs={{0,16},{4,12},{8,24},{12,4},{16,0},{20,28},{24,8},{28,20},{1,17},{... | collective-permute-start | bytes 1179656 | tf_op jit(solution)/shard_map/ppermute | solution.py:51
  6.4 0.7 %pad_add_fusion.refs_0_.meta = s32[34]{0:T(128)S(1)} fusion(s32[16]{0:T(128)} %bitcast.19, s32[16]{0:T(128)} %bitcast.20, s32[1]{0:T(128)} %bitcast.7, s32[1]{0:T(128)} %bitcast.6), kind=kLoop, calls=%fused_computation.4 | loop fusion | flops 102 | bytes 272 | tf_op jit(solution)/shard_map/concatenate | solution.py:340
  7.2 7.1 %collective-permute-done.refs_3_.refs_11_ = bf16[256,768]{1,0:T(8,128)(2,1)S(1)} collective-permute-done((bf16[256,768]{1,0:T(8,128)(2,1)S(1)}, bf16[256,768]{1,0:T(8,128)(2,1)S(1)}, u32[]{:S(2)}, u32[]{:S(2)}) %collective-permute-start) | collective-permute-done | bytes 393248 | tf_op jit(solution)/shard_map/ppermute | solution.py:51
  14.3 1.6 %collective-permute-start.2 = (bf16[256,768]{1,0:T(8,128)(2,1)S(1)}, bf16[256,768]{1,0:T(8,128)(2,1)S(1)}, u32[]{:S(2)}, u32[]{:S(2)}) collective-permute-start(bf16[256,768]{1,0:T(8,128)(2,1)S(1)} %collective-permute-done.refs_3_.refs_11_), channel_id=1, source_target_pairs={{0,16},{4,12},{8,24},{12,4},{16,0},{20,28},{24,8},{28,20},{1,17},{... | collective-permute-start | bytes 1179656 | tf_op jit(solution)/shard_map/ppermute | solution.py:51
  15.9 0.9 %slice.14 = bf16[256,256]{1,0:T(8,128)(2,1)S(1)} slice(bf16[256,512]{1,0:T(8,128)(2,1)} %bitcast.15), slice={[0:256], [256:512]} | slice | bytes 262144 | tf_op jit(solution)/shard_map/slice | solution.py:351
  16.8 0.9 %slice.15 = bf16[256,256]{1,0:T(8,128)(2,1)S(1)} slice(bf16[256,512]{1,0:T(8,128)(2,1)} %bitcast.16), slice={[0:256], [256:512]} | slice | bytes 262144 | tf_op jit(solution)/shard_map/slice | solution.py:351
  17.7 0.0 copy-start
  17.7 0.5 collective-permute-start.4
  18.3 2.5 %collective-permute-start.3 = (bf16[256,512]{1,0:T(8,128)(2,1)S(1)}, bf16[256,512]{1,0:T(8,128)(2,1)S(1)}, u32[]{:S(2)}, u32[]{:S(2)}) collective-permute-start(bf16[256,512]{1,0:T(8,128)(2,1)S(1)} %pad_maximum_fusion.1.refs_9_), channel_id=1, source_target_pairs={{0,8},{4,20},{8,0},{12,28},{16,24},{20,4},{24,16},{28,12},{1,9},{5... | collective-permute-start | bytes 786440 | tf_op jit(solution)/shard_map/ppermute | solution.py:51
  20.8 0.0 collective-permute-start.6
  20.8 0.0 collective-permute-done.1.refs_5_.refs_13_
  20.8 6.9 %collective-permute-done.4.refs_13_ = bf16[256,512]{1,0:T(8,128)(2,1)S(1)} collective-permute-done((bf16[256,512]{1,0:T(8,128)(2,1)S(1)}, bf16[256,512]{1,0:T(8,128)(2,1)S(1)}, u32[]{:S(2)}, u32[]{:S(2)}) %collective-permute-start.4) | collective-permute-done | bytes 262176 | tf_op jit(solution)/shard_map/ppermute | solution.py:51
  27.7 0.0 collective-permute-done.3.refs_11_
  27.7 0.0 collective-permute-done.2.refs_7_.refs_15_
  27.7 0.0 collective-permute-start.7
  27.7 0.5 collective-permute-start.8
  28.2 0.1 collective-permute-start.9
  28.3 1.6 %collective-permute-start.5 = (bf16[256,512]{1,0:T(8,128)(2,1)S(1)}, bf16[256,512]{1,0:T(8,128)(2,1)S(1)}, u32[]{:S(2)}, u32[]{:S(2)}) collective-permute-start(bf16[256,512]{1,0:T(8,128)(2,1)S(1)} %collective-permute-done.3.refs_11_), channel_id=1, source_target_pairs={{0,16},{4,12},{8,24},{12,4},{16,0},{20,28},{24,8},{28,20},{1,17},{... | collective-permute-start | bytes 786440 | tf_op jit(solution)/shard_map/ppermute | solution.py:51
  29.9 0.0 collective-permute-done.6.refs_2_.refs_10_
  29.9 1.1 %collective-permute-start.13 = (bf16[256,512]{1,0:T(8,128)(2,1)S(1)}, bf16[256,512]{1,0:T(8,128)(2,1)S(1)}, u32[]{:S(2)}, u32[]{:S(2)}) collective-permute-start(bf16[256,512]{1,0:T(8,128)(2,1)S(1)} %pad_maximum_fusion.1.refs_9_), channel_id=1, source_target_pairs={{0,4},{4,0},{8,12},{12,8},{16,20},{20,16},{24,28},{28,24},{1,5},{5... | collective-permute-start | bytes 786440 | tf_op jit(solution)/shard_map/ppermute | solution.py:39
  30.9 0.0 collective-permute-done.7.refs_4_.refs_12_
  30.9 0.0 collective-permute-done.8.refs_6_.refs_14_
  30.9 0.0 collective-permute-done.9.refs_8_.refs_16_
  30.9 6.8 %attention.2 = (bf16[2048,256]{1,0:T(8,128)(2,1)S(1)}, f32[2048,128]{1,0:T(8,128)S(1)}, f32[2048,128]{1,0:T(8,128)S(1)}) custom-call(s32[34]{0:T(128)S(1)} %pad_add_fusion.refs_0_.meta, bf16[256,768]{1,0:T(8,128)(2,1)S(1)} %pad_maximum_fusion.refs_1_.refs_9_, bf16[256,768]{1,0:T(8,128)(2,1)S(1)} %collective-permute-done.6.refs_2_.refs_10_, ...), custom_call_target="tpu_custom_call" | custom-call | flops 1342177280 | bytes 12582912 | tf_op jit(solution)/shard_map/attention/pallas_call | solution.py:222
  37.8 0.0 collective-permute-done.5.refs_15_
  37.8 0.1 collective-permute-start.14
  37.9 0.5 collective-permute-start.15
  38.4 0.1 collective-permute-start.16
  38.4 0.0 copy-done
  38.4 1.3 %weight_part.2 = (f32[128,256]{1,0:T(8,128)S(1)}, bf16[128,256]{1,0:T(8,128)(2,1)S(1)}, bf16[128,256]{1,0:T(8,128)(2,1)S(1)}, bf16[128,256]{1,0:T(8,128)(2,1)S(1)}) custom-call(s32[34]{0:T(128)S(1)} %pad_add_fusion.refs_0_.meta, bf16[2048,512]{1,0:T(8,128)(2,1)S(1)} %bitcast.13, bf16[2048,256]{1,0:T(8,128)(2,1)S(1)} %get-tuple-element.47.refs_0_), custom_call_target="tpu_custom_call" | custom-call | flops 536870912 | bytes 3145728 | tf_op jit(solution)/shard_map/weight_part/pallas_call | solution.py:279
  39.8 1.5 %collective-permute-start.10 = (bf16[128,256]{1,0:T(8,128)(2,1)S(1)}, bf16[128,256]{1,0:T(8,128)(2,1)S(1)}, u32[]{:S(2)}, u32[]{:S(2)}) collective-permute-start(bf16[128,256]{1,0:T(8,128)(2,1)S(1)} %get-tuple-element.49), channel_id=1, source_target_pairs={{0,1},{1,0},{2,3},{3,2},{4,5},{5,4},{6,7},{7,6},{8,9},{9,8},{10,11... | collective-permute-start | bytes 196616 | tf_op jit(solution)/shard_map/ppermute | solution.py:39
  41.3 0.0 collective-permute-done.13.refs_10_
  41.3 2.6 %collective-permute-start.11 = (bf16[128,256]{1,0:T(8,128)(2,1)S(1)}, bf16[128,256]{1,0:T(8,128)(2,1)S(1)}, u32[]{:S(2)}, u32[]{:S(2)}) collective-permute-start(bf16[128,256]{1,0:T(8,128)(2,1)S(1)} %get-tuple-element.50), channel_id=1, source_target_pairs={{0,2},{1,3},{2,0},{3,1},{4,6},{5,7},{6,4},{7,5},{8,10},{9,11},{10,... | collective-permute-start | bytes 196616 | tf_op jit(solution)/shard_map/ppermute | solution.py:39
  43.9 0.0 collective-permute-done.14.refs_12_
  43.9 0.4 collective-permute-start.12
  44.2 0.0 collective-permute-done.15.refs_14_
  44.2 0.0 collective-permute-done.16.refs_16_
  44.2 7.0 %attention.3 = (bf16[2048,256]{1,0:T(8,128)(2,1)S(1)}, bf16[2048,128]{1,0:T(8,128)(2,1)S(1)}, bf16[2048,128]{1,0:T(8,128)(2,1)S(1)}) custom-call(s32[34]{0:T(128)S(1)} %pad_add_fusion.refs_0_.meta, bf16[256,768]{1,0:T(8,128)(2,1)S(1)} %pad_maximum_fusion.refs_1_.refs_9_, bf16[256,768]{1,0:T(8,128)(2,1)S(1)} %collective-permute-done.6.refs_2_.refs_10_, ...), custom_call_target="tpu_custom_call" | custom-call | flops 1342177280 | bytes 12582912 | tf_op jit(solution)/shard_map/attention/pallas_call | solution.py:222
  51.3 0.0 collective-permute-done.10.refs_1_
  51.3 0.0 collective-permute-done.11.refs_2_
  51.3 0.0 collective-permute-done.12.refs_3_
  51.3 2.4 %weight_part.3 = (f32[128,512]{1,0:T(8,128)S(1)}, bf16[128,512]{1,0:T(8,128)(2,1)S(1)}, bf16[128,512]{1,0:T(8,128)(2,1)S(1)}, bf16[128,512]{1,0:T(8,128)(2,1)S(1)}) custom-call(s32[34]{0:T(128)S(1)} %pad_add_fusion.refs_0_.meta, bf16[2048,512]{1,0:T(8,128)(2,1)S(1)} %bitcast.14, bf16[2048,256]{1,0:T(8,128)(2,1)S(1)} %get-tuple-element.62.refs_0_, ...), custom_call_target="tpu_custom_call" | custom-call | flops 1073741824 | bytes 4194304 | tf_op jit(solution)/shard_map/weight_part/pallas_call | solution.py:279
  53.7 0.2 collective-permute-start.17
  53.9 3.5 %collective-permute-start.18 = (bf16[128,512]{1,0:T(8,128)(2,1)S(1)}, bf16[128,512]{1,0:T(8,128)(2,1)S(1)}, u32[]{:S(2)}, u32[]{:S(2)}) collective-permute-start(bf16[128,512]{1,0:T(8,128)(2,1)S(1)} %get-tuple-element.67), channel_id=1, source_target_pairs={{0,2},{1,3},{2,0},{3,1},{4,6},{5,7},{6,4},{7,5},{8,10},{9,11},{10,... | collective-permute-start | bytes 393224 | tf_op jit(solution)/shard_map/ppermute | solution.py:39
  57.4 0.8 %collective-permute-start.19 = (bf16[128,512]{1,0:T(8,128)(2,1)S(1)}, bf16[128,512]{1,0:T(8,128)(2,1)S(1)}, u32[]{:S(2)}, u32[]{:S(2)}) collective-permute-start(bf16[128,512]{1,0:T(8,128)(2,1)S(1)} %get-tuple-element.68), channel_id=1, source_target_pairs={{0,3},{1,2},{2,1},{3,0},{4,7},{5,6},{6,5},{7,4},{8,11},{9,10},{10,... | collective-permute-start | bytes 393224 | tf_op jit(solution)/shard_map/ppermute | solution.py:39
  58.2 2.6 %collective-permute-done.17.refs_5_ = bf16[128,512]{1,0:T(8,128)(2,1)S(1)} collective-permute-done((bf16[128,512]{1,0:T(8,128)(2,1)S(1)}, bf16[128,512]{1,0:T(8,128)(2,1)S(1)}, u32[]{:S(2)}, u32[]{:S(2)}) %collective-permute-start.17) | collective-permute-done | bytes 131104 | tf_op jit(solution)/shard_map/ppermute | solution.py:39
  60.8 6.5 %collective-permute-done.18.refs_6_ = bf16[128,512]{1,0:T(8,128)(2,1)S(1)} collective-permute-done((bf16[128,512]{1,0:T(8,128)(2,1)S(1)}, bf16[128,512]{1,0:T(8,128)(2,1)S(1)}, u32[]{:S(2)}, u32[]{:S(2)}) %collective-permute-start.18) | collective-permute-done | bytes 131104 | tf_op jit(solution)/shard_map/ppermute | solution.py:39
  67.3 0.0 collective-permute-done.19.refs_7_
  67.3 0.8 %final_sum.1 = f32[128,768]{1,0:T(8,128)} custom-call(f32[128,256]{1,0:T(8,128)S(1)} %get-tuple-element.58.refs_0_, bf16[128,256]{1,0:T(8,128)(2,1)S(1)} %collective-permute-done.10.refs_1_, bf16[128,256]{1,0:T(8,128)(2,1)S(1)} %collective-permute-done.11.refs_2_, bf16[128,256]{1,0:T(8,128)(2,1)S(1)} %collective-permute-done.12.refs_3_, ...), custom_call_target="tpu_custom_call" | custom-call | tf_op jit(solution)/shard_map/final_sum/pallas_call | solution.py:318
  (1 shorter events, 0.0 us)
Async XLA Ops:
  1.9 12.4 %collective-permute-start = (bf16[256,768]{1,0:T(8,128)(2,1)S(1)}, bf16[256,768]{1,0:T(8,128)(2,1)S(1)}, u32[]{:S(2)}, u32[]{:S(2)}) collective-permute-start(bf16[256,768]{1,0:T(8,128)(2,1)S(1)} %pad_maximum_fusion.refs_1_.refs_9_), channel_id=1, source_target_pairs={{0,8},{4,20},{8,0},{12,28},{16,24},{20,4},{24,16},{28,12},{1,9},{5... | collective-permute-start | bytes 1179656 | tf_op jit(solution)/shard_map/ppermute | solution.py:51
  4.9 15.9 %collective-permute-start.1 = (bf16[256,768]{1,0:T(8,128)(2,1)S(1)}, bf16[256,768]{1,0:T(8,128)(2,1)S(1)}, u32[]{:S(2)}, u32[]{:S(2)}) collective-permute-start(bf16[256,768]{1,0:T(8,128)(2,1)S(1)} %pad_maximum_fusion.refs_1_.refs_9_), channel_id=1, source_target_pairs={{0,16},{4,12},{8,24},{12,4},{16,0},{20,28},{24,8},{28,20},{1,17},{... | collective-permute-start | bytes 1179656 | tf_op jit(solution)/shard_map/ppermute | solution.py:51
  14.3 13.4 %collective-permute-start.2 = (bf16[256,768]{1,0:T(8,128)(2,1)S(1)}, bf16[256,768]{1,0:T(8,128)(2,1)S(1)}, u32[]{:S(2)}, u32[]{:S(2)}) collective-permute-start(bf16[256,768]{1,0:T(8,128)(2,1)S(1)} %collective-permute-done.refs_3_.refs_11_), channel_id=1, source_target_pairs={{0,16},{4,12},{8,24},{12,4},{16,0},{20,28},{24,8},{28,20},{1,17},{... | collective-permute-start | bytes 1179656 | tf_op jit(solution)/shard_map/ppermute | solution.py:51
  17.7 20.7 %copy-start = (bf16[1,2048,512]{2,1,0:T(8,128)(2,1)S(1)}, bf16[1,2048,512]{2,1,0:T(8,128)(2,1)}, u32[]{:S(2)}) copy-start(bf16[1,2048,512]{2,1,0:T(8,128)(2,1)} %param.7) | copy-start | bytes 6291460
  17.7 10.0 %collective-permute-start.4 = (bf16[256,512]{1,0:T(8,128)(2,1)S(1)}, bf16[256,512]{1,0:T(8,128)(2,1)S(1)}, u32[]{:S(2)}, u32[]{:S(2)}) collective-permute-start(bf16[256,512]{1,0:T(8,128)(2,1)S(1)} %pad_maximum_fusion.1.refs_9_), channel_id=1, source_target_pairs={{0,16},{4,12},{8,24},{12,4},{16,0},{20,28},{24,8},{28,20},{1,17},{... | collective-permute-start | bytes 786440 | tf_op jit(solution)/shard_map/ppermute | solution.py:51
  18.3 9.4 %collective-permute-start.3 = (bf16[256,512]{1,0:T(8,128)(2,1)S(1)}, bf16[256,512]{1,0:T(8,128)(2,1)S(1)}, u32[]{:S(2)}, u32[]{:S(2)}) collective-permute-start(bf16[256,512]{1,0:T(8,128)(2,1)S(1)} %pad_maximum_fusion.1.refs_9_), channel_id=1, source_target_pairs={{0,8},{4,20},{8,0},{12,28},{16,24},{20,4},{24,16},{28,12},{1,9},{5... | collective-permute-start | bytes 786440 | tf_op jit(solution)/shard_map/ppermute | solution.py:51
  20.8 9.1 %collective-permute-start.6 = (bf16[256,768]{1,0:T(8,128)(2,1)S(1)}, bf16[256,768]{1,0:T(8,128)(2,1)S(1)}, u32[]{:S(2)}, u32[]{:S(2)}) collective-permute-start(bf16[256,768]{1,0:T(8,128)(2,1)S(1)} %pad_maximum_fusion.refs_1_.refs_9_), channel_id=1, source_target_pairs={{0,4},{4,0},{8,12},{12,8},{16,20},{20,16},{24,28},{28,24},{1,5},{5... | collective-permute-start | bytes 1179656 | tf_op jit(solution)/shard_map/ppermute | solution.py:39
  27.7 3.2 %collective-permute-start.7 = (bf16[256,768]{1,0:T(8,128)(2,1)S(1)}, bf16[256,768]{1,0:T(8,128)(2,1)S(1)}, u32[]{:S(2)}, u32[]{:S(2)}) collective-permute-start(bf16[256,768]{1,0:T(8,128)(2,1)S(1)} %collective-permute-done.refs_3_.refs_11_), channel_id=1, source_target_pairs={{0,4},{4,0},{8,12},{12,8},{16,20},{20,16},{24,28},{28,24},{1,5},{5... | collective-permute-start | bytes 1179656 | tf_op jit(solution)/shard_map/ppermute | solution.py:39
  27.7 3.2 %collective-permute-start.8 = (bf16[256,768]{1,0:T(8,128)(2,1)S(1)}, bf16[256,768]{1,0:T(8,128)(2,1)S(1)}, u32[]{:S(2)}, u32[]{:S(2)}) collective-permute-start(bf16[256,768]{1,0:T(8,128)(2,1)S(1)} %collective-permute-done.1.refs_5_.refs_13_), channel_id=1, source_target_pairs={{0,4},{4,0},{8,12},{12,8},{16,20},{20,16},{24,28},{28,24},{1,5},{5... | collective-permute-start | bytes 1179656 | tf_op jit(solution)/shard_map/ppermute | solution.py:39
  28.2 2.7 %collective-permute-start.9 = (bf16[256,768]{1,0:T(8,128)(2,1)S(1)}, bf16[256,768]{1,0:T(8,128)(2,1)S(1)}, u32[]{:S(2)}, u32[]{:S(2)}) collective-permute-start(bf16[256,768]{1,0:T(8,128)(2,1)S(1)} %collective-permute-done.2.refs_7_.refs_15_), channel_id=1, source_target_pairs={{0,4},{4,0},{8,12},{12,8},{16,20},{20,16},{24,28},{28,24},{1,5},{5... | collective-permute-start | bytes 1179656 | tf_op jit(solution)/shard_map/ppermute | solution.py:39
  28.3 9.5 %collective-permute-start.5 = (bf16[256,512]{1,0:T(8,128)(2,1)S(1)}, bf16[256,512]{1,0:T(8,128)(2,1)S(1)}, u32[]{:S(2)}, u32[]{:S(2)}) collective-permute-start(bf16[256,512]{1,0:T(8,128)(2,1)S(1)} %collective-permute-done.3.refs_11_), channel_id=1, source_target_pairs={{0,16},{4,12},{8,24},{12,4},{16,0},{20,28},{24,8},{28,20},{1,17},{... | collective-permute-start | bytes 786440 | tf_op jit(solution)/shard_map/ppermute | solution.py:51
  29.9 11.4 %collective-permute-start.13 = (bf16[256,512]{1,0:T(8,128)(2,1)S(1)}, bf16[256,512]{1,0:T(8,128)(2,1)S(1)}, u32[]{:S(2)}, u32[]{:S(2)}) collective-permute-start(bf16[256,512]{1,0:T(8,128)(2,1)S(1)} %pad_maximum_fusion.1.refs_9_), channel_id=1, source_target_pairs={{0,4},{4,0},{8,12},{12,8},{16,20},{20,16},{24,28},{28,24},{1,5},{5... | collective-permute-start | bytes 786440 | tf_op jit(solution)/shard_map/ppermute | solution.py:39
  37.8 6.1 %collective-permute-start.14 = (bf16[256,512]{1,0:T(8,128)(2,1)S(1)}, bf16[256,512]{1,0:T(8,128)(2,1)S(1)}, u32[]{:S(2)}, u32[]{:S(2)}) collective-permute-start(bf16[256,512]{1,0:T(8,128)(2,1)S(1)} %collective-permute-done.3.refs_11_), channel_id=1, source_target_pairs={{0,4},{4,0},{8,12},{12,8},{16,20},{20,16},{24,28},{28,24},{1,5},{5... | collective-permute-start | bytes 786440 | tf_op jit(solution)/shard_map/ppermute | solution.py:39
  37.9 6.4 %collective-permute-start.15 = (bf16[256,512]{1,0:T(8,128)(2,1)S(1)}, bf16[256,512]{1,0:T(8,128)(2,1)S(1)}, u32[]{:S(2)}, u32[]{:S(2)}) collective-permute-start(bf16[256,512]{1,0:T(8,128)(2,1)S(1)} %collective-permute-done.4.refs_13_), channel_id=1, source_target_pairs={{0,4},{4,0},{8,12},{12,8},{16,20},{20,16},{24,28},{28,24},{1,5},{5... | collective-permute-start | bytes 786440 | tf_op jit(solution)/shard_map/ppermute | solution.py:39
  38.4 5.9 %collective-permute-start.16 = (bf16[256,512]{1,0:T(8,128)(2,1)S(1)}, bf16[256,512]{1,0:T(8,128)(2,1)S(1)}, u32[]{:S(2)}, u32[]{:S(2)}) collective-permute-start(bf16[256,512]{1,0:T(8,128)(2,1)S(1)} %collective-permute-done.5.refs_15_), channel_id=1, source_target_pairs={{0,4},{4,0},{8,12},{12,8},{16,20},{20,16},{24,28},{28,24},{1,5},{5... | collective-permute-start | bytes 786440 | tf_op jit(solution)/shard_map/ppermute | solution.py:39
  39.8 11.5 %collective-permute-start.10 = (bf16[128,256]{1,0:T(8,128)(2,1)S(1)}, bf16[128,256]{1,0:T(8,128)(2,1)S(1)}, u32[]{:S(2)}, u32[]{:S(2)}) collective-permute-start(bf16[128,256]{1,0:T(8,128)(2,1)S(1)} %get-tuple-element.49), channel_id=1, source_target_pairs={{0,1},{1,0},{2,3},{3,2},{4,5},{5,4},{6,7},{7,6},{8,9},{9,8},{10,11... | collective-permute-start | bytes 196616 | tf_op jit(solution)/shard_map/ppermute | solution.py:39
  41.3 10.0 %collective-permute-start.11 = (bf16[128,256]{1,0:T(8,128)(2,1)S(1)}, bf16[128,256]{1,0:T(8,128)(2,1)S(1)}, u32[]{:S(2)}, u32[]{:S(2)}) collective-permute-start(bf16[128,256]{1,0:T(8,128)(2,1)S(1)} %get-tuple-element.50), channel_id=1, source_target_pairs={{0,2},{1,3},{2,0},{3,1},{4,6},{5,7},{6,4},{7,5},{8,10},{9,11},{10,... | collective-permute-start | bytes 196616 | tf_op jit(solution)/shard_map/ppermute | solution.py:39
  43.9 7.4 %collective-permute-start.12 = (bf16[128,256]{1,0:T(8,128)(2,1)S(1)}, bf16[128,256]{1,0:T(8,128)(2,1)S(1)}, u32[]{:S(2)}, u32[]{:S(2)}) collective-permute-start(bf16[128,256]{1,0:T(8,128)(2,1)S(1)} %get-tuple-element.51), channel_id=1, source_target_pairs={{0,3},{1,2},{2,1},{3,0},{4,7},{5,6},{6,5},{7,4},{8,11},{9,10},{10,... | collective-permute-start | bytes 196616 | tf_op jit(solution)/shard_map/ppermute | solution.py:39
  53.7 7.1 %collective-permute-start.17 = (bf16[128,512]{1,0:T(8,128)(2,1)S(1)}, bf16[128,512]{1,0:T(8,128)(2,1)S(1)}, u32[]{:S(2)}, u32[]{:S(2)}) collective-permute-start(bf16[128,512]{1,0:T(8,128)(2,1)S(1)} %get-tuple-element.66), channel_id=1, source_target_pairs={{0,1},{1,0},{2,3},{3,2},{4,5},{5,4},{6,7},{7,6},{8,9},{9,8},{10,11... | collective-permute-start | bytes 393224 | tf_op jit(solution)/shard_map/ppermute | solution.py:39
  53.9 13.3 %collective-permute-start.18 = (bf16[128,512]{1,0:T(8,128)(2,1)S(1)}, bf16[128,512]{1,0:T(8,128)(2,1)S(1)}, u32[]{:S(2)}, u32[]{:S(2)}) collective-permute-start(bf16[128,512]{1,0:T(8,128)(2,1)S(1)} %get-tuple-element.67), channel_id=1, source_target_pairs={{0,2},{1,3},{2,0},{3,1},{4,6},{5,7},{6,4},{7,5},{8,10},{9,11},{10,... | collective-permute-start | bytes 393224 | tf_op jit(solution)/shard_map/ppermute | solution.py:39
  57.4 9.9 %collective-permute-start.19 = (bf16[128,512]{1,0:T(8,128)(2,1)S(1)}, bf16[128,512]{1,0:T(8,128)(2,1)S(1)}, u32[]{:S(2)}, u32[]{:S(2)}) collective-permute-start(bf16[128,512]{1,0:T(8,128)(2,1)S(1)} %get-tuple-element.68), channel_id=1, source_target_pairs={{0,3},{1,2},{2,1},{3,0},{4,7},{5,6},{6,5},{7,4},{8,11},{9,10},{10,... | collective-permute-start | bytes 393224 | tf_op jit(solution)/shard_map/ppermute | solution.py:39

commit v4 on v3

--- a/solution.py
+++ b/solution.py
@@ -10,7 +10,7 @@
 
 masked_fill = -1e30
 MOST_DOC = 4
-TOGETHER = 2
+TOGETHER = 1
 AT_ONCE = {1: (4, 2, 1), 2: (2, 1), 3: (1,), 4: (1,)}
 VMEM_LIMIT = 24 * 1024 * 1024
 
@@ -73,18 +73,11 @@
     return me ^ (even + (odd - even) * core)
 
 
-def attention_kernel(shards, blocks, heads, hd, kv_at, q_at, scaling, last, *refs):
+def attention_kernel(shards, blocks, heads, hd, scaling, *refs):
     meta = refs[0]
-    kv_refs = refs[1 : 1 + shards]
-    q_refs = refs[1 + shards : 1 + 2 * shards]
-    refs = refs[1 + 2 * shards :]
-    if last:
-        dk_before, dv_before, dq_ref, dk_ref, dv_ref = refs[:5]
-        refs = refs[5:]
-    else:
-        dq_ref, dk_ref, dv_ref = refs[:3]
-        refs = refs[3:]
-    keys, values, queries, grads, inverse, starts = refs
+    chunks = refs[1 : 1 + shards]
+    dq_refs = refs[1 + shards : -8]
+    dk_ref, dv_ref, keys, values, queries, grads, inverse, starts = refs[-8:]
     me = meta[0]
     per_dev = blocks // shards
     span = keys.shape[0] // blocks
@@ -104,10 +97,10 @@
             inverse[position] = storage
             rows = rows_at(position, 1)
             here = slice(b * span, (b + 1) * span)
-            keys[rows, :] = kv_refs[place][here, kv_at : kv_at + hd]
-            values[rows, :] = kv_refs[place][here, kv_at + hd : kv_at + 2 * hd]
-            queries[rows, :] = q_refs[place][here, q_at : q_at + qw]
-            grads[rows, :] = q_refs[place][here, q_at + qw : q_at + 2 * qw]
+            at = 0
+            for whole in (keys, values, queries, grads):
+                whole[rows, :] = chunks[place][here, at : at + whole.shape[1]]
+                at += whole.shape[1]
 
     def note(state):
         first, counts = state[0], state[1:]
@@ -183,7 +176,9 @@
                 at = rows_at(inverse[first + before + t], 1)
                 for h in range(heads):
                     start = (h * count + t) * span
-                    dq_ref[at, h * hd : (h + 1) * hd] = dq[start : start + span]
+                    dq_ref = dq_refs[h * len(dq_refs) // heads]
+                    column = h * hd % dq_ref.shape[1]
+                    dq_ref[at, column : column + hd] = dq[start : start + span]
         for first in firsts:
             for j in range(size):
                 reach = [
@@ -195,8 +190,6 @@
                 dk = sum(dks[i][rows] for i in reach) * scaling
                 dv = sum(dvs[i][rows] for i in reach)
                 at = rows_at(inverse[first + j], 1)
-                if last:
-                    dk, dv = dk + dk_before[at, :], dv + dv_before[at, :]
                 dk_ref[at, :] = dk.astype(dk_ref.dtype)
                 dv_ref[at, :] = dv.astype(dv_ref.dtype)
 
@@ -214,22 +207,18 @@
             done = done + times * together
 
 
-def attention(meta, blocks, hd, heads, kv_chunks, kv_at, q_chunks, q_at, before, last):
-    shards = len(kv_chunks)
-    length = kv_chunks[0].shape[0] * shards
-    qw = heads * hd
-    sums = jnp.bfloat16 if last else jnp.float32
+def attention(meta, blocks, hd, chunks, groups):
+    shards = len(chunks)
+    tok, columns = chunks[0].shape
+    length = tok * shards
+    qw = (columns - 2 * hd) // 2
+    outs = (qw // groups,) * groups + (hd, hd)
+    pairs = length * length // blocks
     return pl.pallas_call(
-        functools.partial(
-            attention_kernel, shards, blocks, heads, hd, kv_at, q_at, hd**-0.5, last
-        ),
-        out_shape=(
-            jax.ShapeDtypeStruct((length, qw), jnp.bfloat16),
-            jax.ShapeDtypeStruct((length, hd), sums),
-            jax.ShapeDtypeStruct((length, hd), sums),
-        ),
-        in_specs=[smem()] + [vmem()] * (2 * shards + len(before)),
-        out_specs=(vmem(),) * 3,
+        functools.partial(attention_kernel, shards, blocks, qw // hd, hd, hd**-0.5),
+        out_shape=tuple(jax.ShapeDtypeStruct((length, width), jnp.bfloat16) for width in outs),
+        in_specs=[smem()] + [vmem()] * shards,
+        out_specs=(vmem(),) * len(outs),
         scratch_shapes=[
             pltpu.VMEM((length, hd), jnp.bfloat16),
             pltpu.VMEM((length, hd), jnp.bfloat16),
@@ -240,23 +229,17 @@
         ],
         compiler_params=kernel_params(),
         cost_estimate=pl.CostEstimate(
-            flops=10 * 2 * length * span_of(length, blocks) * qw,
-            bytes_accessed=24 * length * qw,
-            transcendentals=2 * length * span_of(length, blocks) * heads,
+            flops=20 * pairs * qw,
+            bytes_accessed=4 * length * columns,
+            transcendentals=2 * pairs * qw // hd,
         ),
         name="attention",
-    )(meta, *kv_chunks, *q_chunks, *before)
-
-
-def span_of(length, blocks):
-    return length // blocks
-
-
-def weight_kernel(owners, parts, meta, slab_ref, *refs):
+    )(meta, *chunks)
+
+
+def weight_kernel(owners, at_once, parts, meta, slab_ref, *refs):
     rows_refs = refs[:parts]
-    own_ref = refs[parts]
-    sends = refs[parts + 1 : parts + owners]
-    total = refs[-1]
+    kept, sent, total = refs[parts], refs[parts + 1 : -1], refs[-1]
     my_dp = meta[1]
     first = 0
     for ref in rows_refs:
@@ -266,22 +249,28 @@
     piece = total.shape[0] // owners
     for rel in range(owners):
         rows = pl.ds(pl.multiple_of((my_dp ^ rel) * piece, piece), piece)
-        if rel == 0:
-            own_ref[...] = total[rows, :]
+        to = slice((rel >> 1) * piece, ((rel >> 1) + 1) * piece)
+        if at_once and rel:
+            sent[rel - 1][...] = total[rows, :].astype(sent[rel - 1].dtype)
+        elif at_once:
+            kept[...] = total[rows, :]
+        elif rel & 1:
+            sent[0][to, :] = total[rows, :].astype(sent[0].dtype)
         else:
-            sends[rel - 1][...] = total[rows, :].astype(jnp.bfloat16)
-
-
-def weight_part(meta, slab, grads, owners):
+            kept[to, :] = total[rows, :]
+
+
+def weight_part(meta, slab, grads, owners, at_once):
     length, features = slab.shape
     columns = sum(part.shape[1] for part in grads)
-    piece = features // owners
+    rows = features // owners if at_once else features // 2
+    sends = owners - 1 if at_once else 1
     return pl.pallas_call(
-        functools.partial(weight_kernel, owners, len(grads)),
-        out_shape=(jax.ShapeDtypeStruct((piece, columns), jnp.float32),)
-        + (jax.ShapeDtypeStruct((piece, columns), jnp.bfloat16),) * (owners - 1),
+        functools.partial(weight_kernel, owners, at_once, len(grads)),
+        out_shape=(jax.ShapeDtypeStruct((rows, columns), jnp.float32),)
+        + (jax.ShapeDtypeStruct((rows, columns), jnp.bfloat16),) * sends,
         in_specs=[smem()] + [vmem()] * (1 + len(grads)),
-        out_specs=(vmem(),) * owners,
+        out_specs=(vmem(),) * (1 + sends),
         scratch_shapes=[pltpu.VMEM((features, columns), jnp.float32)],
         compiler_params=kernel_params(),
         cost_estimate=pl.CostEstimate(
@@ -293,30 +282,49 @@
     )(meta, slab, *grads)
 
 
-def final_kernel(groups, owners, *refs):
+def fold_kernel(piece, kept_ref, arrived_ref, kept, sent):
+    for j in range(kept_ref.shape[0] // piece):
+        rows = slice(j * piece, (j + 1) * piece)
+        total = kept_ref[rows, :] + arrived_ref[rows, :].astype(jnp.float32)
+        to = slice((j >> 1) * piece, ((j >> 1) + 1) * piece)
+        if j & 1:
+            sent[to, :] = total.astype(sent.dtype)
+        else:
+            kept[to, :] = total
+
+
+def fold(kept, arrived, piece):
+    rows, columns = kept.shape
+    return pl.pallas_call(
+        functools.partial(fold_kernel, piece),
+        out_shape=(
+            jax.ShapeDtypeStruct((rows // 2, columns), jnp.float32),
+            jax.ShapeDtypeStruct((rows // 2, columns), jnp.bfloat16),
+        ),
+        in_specs=[vmem()] * 2,
+        out_specs=(vmem(),) * 2,
+        compiler_params=kernel_params(),
+        name="fold",
+    )(kept, arrived)
+
+
+def final_kernel(sizes, *refs):
     out_ref = refs[-1]
-    first = 0
-    for g in range(groups):
-        own = refs[g * owners]
-        total = own[...]
-        for rel in range(1, owners):
-            total = total + refs[g * owners + rel][...].astype(jnp.float32)
-        for columns, width in out_columns(g, groups, own.shape[1], out_ref.shape[1]):
-            out_ref[:, columns : columns + width] = total[:, first : first + width]
-            first += width
-        first = 0
-
-
-def out_columns(group, groups, width, whole):
-    return [(0, width)] if group == 0 else [(whole - width, width)]
-
-
-def final_sum(parts):
-    groups, owners = len(parts), len(parts[0])
-    flat = [array for group in parts for array in group]
-    columns = sum(group[0].shape[1] for group in parts)
+    first = at = 0
+    for size in sizes:
+        total = refs[at][...]
+        for ref in refs[at + 1 : at + size]:
+            total = total + ref[...].astype(jnp.float32)
+        out_ref[:, first : first + total.shape[1]] = total
+        first += total.shape[1]
+        at += size
+
+
+def final_sum(groups):
+    flat = [array for group in groups for array in group]
+    columns = sum(group[0].shape[1] for group in groups)
     return pl.pallas_call(
-        functools.partial(final_kernel, groups, owners),
+        functools.partial(final_kernel, [len(group) for group in groups]),
         out_shape=jax.ShapeDtypeStruct((flat[0].shape[0], columns), jnp.float32),
         in_specs=[vmem()] * len(flat),
         out_specs=vmem(),
@@ -325,6 +333,14 @@
     )(*flat)
 
 
+def halved(terms, piece, bit):
+    while bit < lax.axis_size("dp"):
+        kept, sent = fold(*terms, piece)
+        terms = [kept, swap(sent, "dp", bit)]
+        bit *= 2
+    return terms
+
+
 def ordered(first, later):
     return lax.optimization_barrier((first, later))
 
@@ -333,53 +349,27 @@
     dp = lax.axis_size("dp")
     blocks = block_pos.shape[1]
     hd = key_proj.shape[2]
-    qw = query_proj.shape[2]
-    half = qw // 2
-    heads = half // hd
     me = jnp.stack([lax.axis_index("seq"), lax.axis_index("dp")]).astype(jnp.int32)
     meta = jnp.concatenate([me, block_pos[0], doc_ids[0]])
     slab = layer_input[0]
 
-    first = jnp.concatenate(
-        [key_proj[0], value_proj[0], query_proj[0, :, :half], out_grad[0, :, :half]], axis=1
-    )
-    first_sent = [across(first, step) for step in range(2)]
-    first_sent[0], (queries, grads, meta) = ordered(
-        first_sent[0], (query_proj[0], out_grad[0], meta)
-    )
-    first_sent.append(across(first_sent[0], 1))
-    second = jnp.concatenate([queries[:, half:], grads[:, half:]], axis=1)
-    second_sent = [across(second, step) for step in range(2)]
-    first_sent, second_sent = ordered(first_sent, second_sent)
-    second_sent.append(across(second_sent[0], 1))
-    first_chunks = with_other_core([first] + first_sent)
-
-    exchange = dp <= 8 and dp & (dp - 1) == 0
-    owners = dp if exchange else 1
-
-    def over_dp(terms):
-        return [terms[0]] + [swap(term, "dp", i + 1) for i, term in enumerate(terms[1:])]
-
-    early, *sums = attention(
-        meta, blocks, hd, heads, first_chunks, 0, first_chunks, 2 * hd, [], False
-    )
-    second_sent, early = ordered(second_sent, early)
-    second_chunks = with_other_core([second] + second_sent)
-    early_terms = over_dp(weight_part(meta, slab, [early], owners))
-    late, dk, dv = attention(
-        meta, blocks, hd, heads, first_chunks, 0, second_chunks, 0, sums, True
-    )
-    early_terms, late = ordered(early_terms, late)
-    late_terms = over_dp(weight_part(meta, slab, [late, dk, dv], owners))
-    groups = (early_terms, late_terms)
-    if exchange:
-        return final_sum(groups)
-    return lax.psum_scatter(
-        jnp.concatenate([terms[0] for terms in groups], axis=1),
-        "dp",
-        scatter_dimension=0,
-        tiled=True,
-    )
+    own = jnp.concatenate([key_proj[0], value_proj[0], query_proj[0], out_grad[0]], axis=1)
+    sent = [across(own, step) for step in range(2)]
+    sent[0], meta = ordered(sent[0], meta)
+    sent.append(across(sent[0], 1))
+    chunks = with_other_core([own] + sent)
+    *dqs, dk, dv = attention(meta, blocks, hd, chunks, 2)
+
+    halving = 1 < dp <= 8 and dp & (dp - 1) == 0
+    grads = [[dk, dv]] + [[dq] for dq in dqs]
+    owners = dp if halving else 1
+    terms = [weight_part(meta, slab, grad, owners, not halving) for grad in grads]
+    terms = terms[1:] + terms[:1]
+    if not halving:
+        whole = jnp.concatenate([kept for kept, in terms], axis=1)
+        return lax.psum_scatter(whole, "dp", scatter_dimension=0, tiled=True)
+    terms = [[kept, swap(part, "dp", 1)] for kept, part in terms]
+    return final_sum([halved(term, slab.shape[1] // dp, 2) for term in terms])
 
 
 def solution(mesh):

time: 68.4 us -> 64.4 us (0.942)
  waiting for transfers between devices: 23.2 us -> 29 us
  Pallas kernels: 18.4 us -> 14.7 us
  local copies, waits for them, and re-layouts: 2.82 us -> 0.01 us
  starting transfers between devices: 21.9 us -> 19.2 us
    ppermute x6 -> x3, waiting for transfers between devices: 14.1 us -> 21.9 us  [across(): return lax.ppermute(x, 'seq', pairs)]
    ppermute x6 -> x3, starting transfers between devices: 10.7 us -> 6.09 us  [across(): return lax.ppermute(x, 'seq', pairs)]
    pallas_call x5 -> x8, Pallas kernels: 18.4 us -> 14.7 us  [the longest x1 9.36 us: attention(): pl.pallas_call(functools.partial(attention_kernel, shards, blocks, qw //...]
    ppermute x14 -> x10, waiting for transfers between devices: 9.12 us -> 7.09 us  [swap(): lax.ppermute(x, axis, [(i, i ^ rel) for i in range(lax.axis_size(axis))])]
    ppermute x14 -> x10, starting transfers between devices: 11.2 us -> 13.2 us  [swap(): lax.ppermute(x, axis, [(i, i ^ rel) for i in range(lax.axis_size(axis))])]
    slice x2 -> x0, local copies, waits for them, and re-layouts: 1.83 us -> none  [body(): second = jnp.concatenate([queries[:, half:], grads[:, half:]], axis=1)]
    squeeze x1 -> x0, local copies, waits for them, and re-layouts: 0.98 us -> none  [body(): out_grad[0, :, :half]]
  transfers between devices with their start and end apart: 20 -> 13, of which waited for: 4 -> 6; matrix products, arithmetic and copies ran while one was open for 4% -> 0% of each run, Pallas kernels for 22% -> 5%
where the time goes in v4:
time: 64.4 us; the launch traced here: 64.3 us
  waiting for transfers between devices  29 us (45%)
  starting transfers between devices  19.2 us (30%)
  Pallas kernels  14.7 us (23%)
  other arithmetic  1.18 us (2%)
    ppermute x3, waiting for transfers between devices, across(): return lax.ppermute(x, 'seq', pairs)  21.9 us
    ppermute x10, starting transfers between devices, swap(): lax.ppermute(x, axis, [(i, i ^ rel) for i in range(lax.axis_size(axis))])  13.2 us
    pallas_call x1, Pallas kernels, attention(): pl.pallas_call(functools.partial(attention_kernel, shards, blocks, qw //...  9.36 us
    ppermute x10, waiting for transfers between devices, swap(): lax.ppermute(x, axis, [(i, i ^ rel) for i in range(lax.axis_size(axis))])  7.09 us
    ppermute x3, starting transfers between devices, across(): return lax.ppermute(x, 'seq', pairs)  6.09 us
    pallas_call x3, Pallas kernels, weight_part(): pl.pallas_call(functools.partial(weight_kernel, owners, at_once, len(grad...  4.51 us
  transfers between devices with their start and end apart: 13, of which 6 were waited for; matrix products, arithmetic and copies ran while one was open for 0% of the time, Pallas kernels for 5%

profile of v4, /device:TPU:0, one launch (start us, length us, event | category | flops | bytes accessed | tf_op | source)
XLA Modules:
  0.0 64.3 jit_solution(2434228724038602447)
XLA Ops:
  0.0 0.0 copy-start.1
  0.0 0.0 copy-start.2
  0.0 1.1 %pad_maximum_fusion.refs_1_ = bf16[256,1280]{1,0:T(8,128)(2,1)S(1)} fusion(bf16[256,512]{1,0:T(8,128)(2,1)} %bitcast.12, bf16[256,512]{1,0:T(8,128)(2,1)} %bitcast.13, bf16[256,128]{1,0:T(8,128)(2,1)} %bitcast.14, bf16[256,128]{1,0:T(8,128)(2,1)} %bitcast.15), kind=kLoop, calls=%fused_computation | loop fusion | flops 2621440 | bytes 1310720 | tf_op jit(solution)/shard_map/concatenate | solution.py:356
  1.1 3.0 %collective-permute-start = (bf16[256,1280]{1,0:T(8,128)(2,1)S(1)}, bf16[256,1280]{1,0:T(8,128)(2,1)S(1)}, u32[]{:S(2)}, u32[]{:S(2)}) collective-permute-start(bf16[256,1280]{1,0:T(8,128)(2,1)S(1)} %pad_maximum_fusion.refs_1_), channel_id=1, source_target_pairs={{0,8},{4,20},{8,0},{12,28},{16,24},{20,4},{24,16},{28,12},{1,9},{5... | collective-permute-start | bytes 1966088 | tf_op jit(solution)/shard_map/ppermute | solution.py:51
  4.1 1.5 %collective-permute-start.3 = (bf16[256,1280]{1,0:T(8,128)(2,1)S(1)}, bf16[256,1280]{1,0:T(8,128)(2,1)S(1)}, u32[]{:S(2)}, u32[]{:S(2)}) collective-permute-start(bf16[256,1280]{1,0:T(8,128)(2,1)S(1)} %pad_maximum_fusion.refs_1_), channel_id=1, source_target_pairs={{0,16},{4,12},{8,24},{12,4},{16,0},{20,28},{24,8},{28,20},{1,17},{... | collective-permute-start | bytes 1966088 | tf_op jit(solution)/shard_map/ppermute | solution.py:51
  5.6 0.0 copy-done.1
  5.6 0.0 copy-done.2
  5.6 0.1 pad_add_fusion.refs_0_.meta
  5.7 0.0 copy-start
  5.7 13.4 %collective-permute-done.refs_3_ = bf16[256,1280]{1,0:T(8,128)(2,1)S(1)} collective-permute-done((bf16[256,1280]{1,0:T(8,128)(2,1)S(1)}, bf16[256,1280]{1,0:T(8,128)(2,1)S(1)}, u32[]{:S(2)}, u32[]{:S(2)}) %collective-permute-start) | collective-permute-done | bytes 655392 | tf_op jit(solution)/shard_map/ppermute | solution.py:51
  19.1 1.6 %collective-permute-start.5 = (bf16[256,1280]{1,0:T(8,128)(2,1)S(1)}, bf16[256,1280]{1,0:T(8,128)(2,1)S(1)}, u32[]{:S(2)}, u32[]{:S(2)}) collective-permute-start(bf16[256,1280]{1,0:T(8,128)(2,1)S(1)} %collective-permute-done.refs_3_), channel_id=1, source_target_pairs={{0,16},{4,12},{8,24},{12,4},{16,0},{20,28},{24,8},{28,20},{1,17},{... | collective-permute-start | bytes 1966088 | tf_op jit(solution)/shard_map/ppermute | solution.py:51
  20.7 0.0 collective-permute-start.1
  20.7 0.5 collective-permute-start.2
  21.2 0.0 collective-permute-done.3.refs_5_
  21.2 0.0 collective-permute-start.4
  21.2 8.5 %collective-permute-done.5.refs_7_ = bf16[256,1280]{1,0:T(8,128)(2,1)S(1)} collective-permute-done((bf16[256,1280]{1,0:T(8,128)(2,1)S(1)}, bf16[256,1280]{1,0:T(8,128)(2,1)S(1)}, u32[]{:S(2)}, u32[]{:S(2)}) %collective-permute-start.5) | collective-permute-done | bytes 655392 | tf_op jit(solution)/shard_map/ppermute | solution.py:51
  29.7 0.0 collective-permute-start.6
  29.7 0.0 collective-permute-done.1.refs_2_
  29.7 0.0 collective-permute-done.4.refs_6_
  29.7 0.0 collective-permute-done.2.refs_4_
  29.7 2.1 %collective-permute-done.6.refs_8_ = bf16[256,1280]{1,0:T(8,128)(2,1)S(1)} collective-permute-done((bf16[256,1280]{1,0:T(8,128)(2,1)S(1)}, bf16[256,1280]{1,0:T(8,128)(2,1)S(1)}, u32[]{:S(2)}, u32[]{:S(2)}) %collective-permute-start.6) | collective-permute-done | bytes 655392 | tf_op jit(solution)/shard_map/ppermute | solution.py:39
  31.8 9.4 %attention.1 = (bf16[2048,256]{1,0:T(8,128)(2,1)S(1)}, bf16[2048,256]{1,0:T(8,128)(2,1)S(1)}, bf16[2048,128]{1,0:T(8,128)(2,1)S(1)}, bf16[2048,128]{1,0:T(8,128)(2,1)S(1)}) custom-call(s32[34]{0:T(128)S(1)} %pad_add_fusion.refs_0_.meta, bf16[256,1280]{1,0:T(8,128)(2,1)S(1)} %pad_maximum_fusion.refs_1_, bf16[256,1280]{1,0:T(8,128)(2,1)S(1)} %collective-permute-done.1.refs_2_, ...), custom_call_target="tpu_custom_call" | custom-call | flops 2684354560 | bytes 10485760 | tf_op jit(solution)/shard_map/attention/pallas_call | solution.py:217
  41.2 0.0 copy-done
  41.2 1.3 %weight_part.3 = (f32[256,256]{1,0:T(8,128)S(1)}, bf16[256,256]{1,0:T(8,128)(2,1)S(1)}) custom-call(s32[34]{0:T(128)S(1)} %pad_add_fusion.refs_0_.meta, bf16[2048,512]{1,0:T(8,128)(2,1)S(1)} %bitcast.9, bf16[2048,256]{1,0:T(8,128)(2,1)S(1)} %get-tuple-element.25.refs_0_), custom_call_target="tpu_custom_call" | custom-call | flops 536870912 | bytes 3145728 | tf_op jit(solution)/shard_map/weight_part/pallas_call | solution.py:268
  42.5 2.6 %collective-permute-start.7 = (bf16[256,256]{1,0:T(8,128)(2,1)S(1)}, bf16[256,256]{1,0:T(8,128)(2,1)S(1)}, u32[]{:S(2)}, u32[]{:S(2)}) collective-permute-start(bf16[256,256]{1,0:T(8,128)(2,1)S(1)} %get-tuple-element.27), channel_id=1, source_target_pairs={{0,1},{1,0},{2,3},{3,2},{4,5},{5,4},{6,7},{7,6},{8,9},{9,8},{10,11... | collective-permute-start | bytes 393224 | tf_op jit(solution)/shard_map/ppermute | solution.py:39
  45.2 1.3 %weight_part.4 = (f32[256,256]{1,0:T(8,128)S(1)}, bf16[256,256]{1,0:T(8,128)(2,1)S(1)}) custom-call(s32[34]{0:T(128)S(1)} %pad_add_fusion.refs_0_.meta, bf16[2048,512]{1,0:T(8,128)(2,1)S(1)} %bitcast.10, bf16[2048,256]{1,0:T(8,128)(2,1)S(1)} %get-tuple-element.30.refs_0_), custom_call_target="tpu_custom_call" | custom-call | flops 536870912 | bytes 3145728 | tf_op jit(solution)/shard_map/weight_part/pallas_call | solution.py:268
  46.5 0.1 collective-permute-start.9
  46.6 1.9 %weight_part.5 = (f32[256,256]{1,0:T(8,128)S(1)}, bf16[256,256]{1,0:T(8,128)(2,1)S(1)}) custom-call(s32[34]{0:T(128)S(1)} %pad_add_fusion.refs_0_.meta, bf16[2048,512]{1,0:T(8,128)(2,1)S(1)} %bitcast.11, bf16[2048,128]{1,0:T(8,128)(2,1)S(1)} %get-tuple-element.35.refs_0_, bf16[2048,128]{1,0:T(8,128)(2,1)S(1)} %get-tuple-element.36.refs_1_), custom_call_target="tpu_custom_call" | custom-call | flops 536870912 | bytes 3145728 | tf_op jit(solution)/shard_map/weight_part/pallas_call | solution.py:268
  48.5 2.1 %collective-permute-start.11 = (bf16[256,256]{1,0:T(8,128)(2,1)S(1)}, bf16[256,256]{1,0:T(8,128)(2,1)S(1)}, u32[]{:S(2)}, u32[]{:S(2)}) collective-permute-start(bf16[256,256]{1,0:T(8,128)(2,1)S(1)} %get-tuple-element.38), channel_id=1, source_target_pairs={{0,1},{1,0},{2,3},{3,2},{4,5},{5,4},{6,7},{7,6},{8,9},{9,8},{10,11... | collective-permute-start | bytes 393224 | tf_op jit(solution)/shard_map/ppermute | solution.py:39
  50.5 0.0 collective-permute-done.7.arrived_ref
  50.6 3.0 %collective-permute-start.8 = (bf16[128,256]{1,0:T(8,128)(2,1)S(1)}, bf16[128,256]{1,0:T(8,128)(2,1)S(1)}, u32[]{:S(2)}, u32[]{:S(2)}) collective-permute-start(bf16[128,256]{1,0:T(8,128)(2,1)S(1)} %get-tuple-element.29), channel_id=1, source_target_pairs={{0,2},{1,3},{2,0},{3,1},{4,6},{5,7},{6,4},{7,5},{8,10},{9,11},{10,... | collective-permute-start | bytes 196616 | tf_op jit(solution)/shard_map/ppermute | solution.py:39
  53.6 0.0 collective-permute-done.9.arrived_ref
  53.7 2.2 %collective-permute-start.10 = (bf16[128,256]{1,0:T(8,128)(2,1)S(1)}, bf16[128,256]{1,0:T(8,128)(2,1)S(1)}, u32[]{:S(2)}, u32[]{:S(2)}) collective-permute-start(bf16[128,256]{1,0:T(8,128)(2,1)S(1)} %get-tuple-element.34), channel_id=1, source_target_pairs={{0,2},{1,3},{2,0},{3,1},{4,6},{5,7},{6,4},{7,5},{8,10},{9,11},{10,... | collective-permute-start | bytes 196616 | tf_op jit(solution)/shard_map/ppermute | solution.py:39
  55.9 0.2 collective-permute-done.11.arrived_ref
  56.1 2.6 %collective-permute-start.12 = (bf16[128,256]{1,0:T(8,128)(2,1)S(1)}, bf16[128,256]{1,0:T(8,128)(2,1)S(1)}, u32[]{:S(2)}, u32[]{:S(2)}) collective-permute-start(bf16[128,256]{1,0:T(8,128)(2,1)S(1)} %get-tuple-element.40), channel_id=1, source_target_pairs={{0,2},{1,3},{2,0},{3,1},{4,6},{5,7},{6,4},{7,5},{8,10},{9,11},{10,... | collective-permute-start | bytes 196616 | tf_op jit(solution)/shard_map/ppermute | solution.py:39
  58.7 0.0 collective-permute-done.8.refs_1_
  58.7 3.4 %collective-permute-done.10.refs_3_ = bf16[128,256]{1,0:T(8,128)(2,1)S(1)} collective-permute-done((bf16[128,256]{1,0:T(8,128)(2,1)S(1)}, bf16[128,256]{1,0:T(8,128)(2,1)S(1)}, u32[]{:S(2)}, u32[]{:S(2)}) %collective-permute-start.10) | collective-permute-done | bytes 65568 | tf_op jit(solution)/shard_map/ppermute | solution.py:39
  62.1 1.4 %collective-permute-done.12.refs_5_ = bf16[128,256]{1,0:T(8,128)(2,1)S(1)} collective-permute-done((bf16[128,256]{1,0:T(8,128)(2,1)S(1)}, bf16[128,256]{1,0:T(8,128)(2,1)S(1)}, u32[]{:S(2)}, u32[]{:S(2)}) %collective-permute-start.12) | collective-permute-done | bytes 65568 | tf_op jit(solution)/shard_map/ppermute | solution.py:39
  63.5 0.8 %final_sum.1 = f32[128,768]{1,0:T(8,128)} custom-call(f32[128,256]{1,0:T(8,128)S(1)} %get-tuple-element.28.refs_0_, bf16[128,256]{1,0:T(8,128)(2,1)S(1)} %collective-permute-done.8.refs_1_, f32[128,256]{1,0:T(8,128)S(1)} %get-tuple-element.33.refs_2_, bf16[128,256]{1,0:T(8,128)(2,1)S(1)} %collective-permute-done.10.refs_3_, ...), custom_call_target="tpu_custom_call" | custom-call | tf_op jit(solution)/shard_map/final_sum/pallas_call | solution.py:326
  (3 shorter events, 0.1 us)
Async XLA Ops:
  0.0 5.6 %copy-start.1 = (s32[1,16]{1,0:T(1,128)S(1)}, s32[1,16]{1,0:T(1,128)}, u32[]{:S(2)}) copy-start(s32[1,16]{1,0:T(1,128)} %param.13) | copy-start | bytes 196
  0.0 5.6 %copy-start.2 = (s32[1,16]{1,0:T(1,128)S(1)}, s32[1,16]{1,0:T(1,128)}, u32[]{:S(2)}) copy-start(s32[1,16]{1,0:T(1,128)} %param.12) | copy-start | bytes 196
  1.1 18.0 %collective-permute-start = (bf16[256,1280]{1,0:T(8,128)(2,1)S(1)}, bf16[256,1280]{1,0:T(8,128)(2,1)S(1)}, u32[]{:S(2)}, u32[]{:S(2)}) collective-permute-start(bf16[256,1280]{1,0:T(8,128)(2,1)S(1)} %pad_maximum_fusion.refs_1_), channel_id=1, source_target_pairs={{0,8},{4,20},{8,0},{12,28},{16,24},{20,4},{24,16},{28,12},{1,9},{5... | collective-permute-start | bytes 1966088 | tf_op jit(solution)/shard_map/ppermute | solution.py:51
  4.1 17.1 %collective-permute-start.3 = (bf16[256,1280]{1,0:T(8,128)(2,1)S(1)}, bf16[256,1280]{1,0:T(8,128)(2,1)S(1)}, u32[]{:S(2)}, u32[]{:S(2)}) collective-permute-start(bf16[256,1280]{1,0:T(8,128)(2,1)S(1)} %pad_maximum_fusion.refs_1_), channel_id=1, source_target_pairs={{0,16},{4,12},{8,24},{12,4},{16,0},{20,28},{24,8},{28,20},{1,17},{... | collective-permute-start | bytes 1966088 | tf_op jit(solution)/shard_map/ppermute | solution.py:51
  5.7 35.5 %copy-start = (bf16[1,2048,512]{2,1,0:T(8,128)(2,1)S(1)}, bf16[1,2048,512]{2,1,0:T(8,128)(2,1)}, u32[]{:S(2)}) copy-start(bf16[1,2048,512]{2,1,0:T(8,128)(2,1)} %param.7) | copy-start | bytes 6291460
  19.1 10.6 %collective-permute-start.5 = (bf16[256,1280]{1,0:T(8,128)(2,1)S(1)}, bf16[256,1280]{1,0:T(8,128)(2,1)S(1)}, u32[]{:S(2)}, u32[]{:S(2)}) collective-permute-start(bf16[256,1280]{1,0:T(8,128)(2,1)S(1)} %collective-permute-done.refs_3_), channel_id=1, source_target_pairs={{0,16},{4,12},{8,24},{12,4},{16,0},{20,28},{24,8},{28,20},{1,17},{... | collective-permute-start | bytes 1966088 | tf_op jit(solution)/shard_map/ppermute | solution.py:51
  20.7 9.0 %collective-permute-start.1 = (bf16[256,1280]{1,0:T(8,128)(2,1)S(1)}, bf16[256,1280]{1,0:T(8,128)(2,1)S(1)}, u32[]{:S(2)}, u32[]{:S(2)}) collective-permute-start(bf16[256,1280]{1,0:T(8,128)(2,1)S(1)} %pad_maximum_fusion.refs_1_), channel_id=1, source_target_pairs={{0,4},{4,0},{8,12},{12,8},{16,20},{20,16},{24,28},{28,24},{1,5},{5... | collective-permute-start | bytes 1966088 | tf_op jit(solution)/shard_map/ppermute | solution.py:39
  20.7 9.0 %collective-permute-start.2 = (bf16[256,1280]{1,0:T(8,128)(2,1)S(1)}, bf16[256,1280]{1,0:T(8,128)(2,1)S(1)}, u32[]{:S(2)}, u32[]{:S(2)}) collective-permute-start(bf16[256,1280]{1,0:T(8,128)(2,1)S(1)} %collective-permute-done.refs_3_), channel_id=1, source_target_pairs={{0,4},{4,0},{8,12},{12,8},{16,20},{20,16},{24,28},{28,24},{1,5},{5... | collective-permute-start | bytes 1966088 | tf_op jit(solution)/shard_map/ppermute | solution.py:39
  21.2 8.5 %collective-permute-start.4 = (bf16[256,1280]{1,0:T(8,128)(2,1)S(1)}, bf16[256,1280]{1,0:T(8,128)(2,1)S(1)}, u32[]{:S(2)}, u32[]{:S(2)}) collective-permute-start(bf16[256,1280]{1,0:T(8,128)(2,1)S(1)} %collective-permute-done.3.refs_5_), channel_id=1, source_target_pairs={{0,4},{4,0},{8,12},{12,8},{16,20},{20,16},{24,28},{28,24},{1,5},{5... | collective-permute-start | bytes 1966088 | tf_op jit(solution)/shard_map/ppermute | solution.py:39
  29.7 2.1 %collective-permute-start.6 = (bf16[256,1280]{1,0:T(8,128)(2,1)S(1)}, bf16[256,1280]{1,0:T(8,128)(2,1)S(1)}, u32[]{:S(2)}, u32[]{:S(2)}) collective-permute-start(bf16[256,1280]{1,0:T(8,128)(2,1)S(1)} %collective-permute-done.5.refs_7_), channel_id=1, source_target_pairs={{0,4},{4,0},{8,12},{12,8},{16,20},{20,16},{24,28},{28,24},{1,5},{5... | collective-permute-start | bytes 1966088 | tf_op jit(solution)/shard_map/ppermute | solution.py:39
  42.5 8.0 %collective-permute-start.7 = (bf16[256,256]{1,0:T(8,128)(2,1)S(1)}, bf16[256,256]{1,0:T(8,128)(2,1)S(1)}, u32[]{:S(2)}, u32[]{:S(2)}) collective-permute-start(bf16[256,256]{1,0:T(8,128)(2,1)S(1)} %get-tuple-element.27), channel_id=1, source_target_pairs={{0,1},{1,0},{2,3},{3,2},{4,5},{5,4},{6,7},{7,6},{8,9},{9,8},{10,11... | collective-permute-start | bytes 393224 | tf_op jit(solution)/shard_map/ppermute | solution.py:39
  46.5 7.1 %collective-permute-start.9 = (bf16[256,256]{1,0:T(8,128)(2,1)S(1)}, bf16[256,256]{1,0:T(8,128)(2,1)S(1)}, u32[]{:S(2)}, u32[]{:S(2)}) collective-permute-start(bf16[256,256]{1,0:T(8,128)(2,1)S(1)} %get-tuple-element.32), channel_id=1, source_target_pairs={{0,1},{1,0},{2,3},{3,2},{4,5},{5,4},{6,7},{7,6},{8,9},{9,8},{10,11... | collective-permute-start | bytes 393224 | tf_op jit(solution)/shard_map/ppermute | solution.py:39
  48.5 7.6 %collective-permute-start.11 = (bf16[256,256]{1,0:T(8,128)(2,1)S(1)}, bf16[256,256]{1,0:T(8,128)(2,1)S(1)}, u32[]{:S(2)}, u32[]{:S(2)}) collective-permute-start(bf16[256,256]{1,0:T(8,128)(2,1)S(1)} %get-tuple-element.38), channel_id=1, source_target_pairs={{0,1},{1,0},{2,3},{3,2},{4,5},{5,4},{6,7},{7,6},{8,9},{9,8},{10,11... | collective-permute-start | bytes 393224 | tf_op jit(solution)/shard_map/ppermute | solution.py:39
  50.6 8.1 %collective-permute-start.8 = (bf16[128,256]{1,0:T(8,128)(2,1)S(1)}, bf16[128,256]{1,0:T(8,128)(2,1)S(1)}, u32[]{:S(2)}, u32[]{:S(2)}) collective-permute-start(bf16[128,256]{1,0:T(8,128)(2,1)S(1)} %get-tuple-element.29), channel_id=1, source_target_pairs={{0,2},{1,3},{2,0},{3,1},{4,6},{5,7},{6,4},{7,5},{8,10},{9,11},{10,... | collective-permute-start | bytes 196616 | tf_op jit(solution)/shard_map/ppermute | solution.py:39
  53.7 8.4 %collective-permute-start.10 = (bf16[128,256]{1,0:T(8,128)(2,1)S(1)}, bf16[128,256]{1,0:T(8,128)(2,1)S(1)}, u32[]{:S(2)}, u32[]{:S(2)}) collective-permute-start(bf16[128,256]{1,0:T(8,128)(2,1)S(1)} %get-tuple-element.34), channel_id=1, source_target_pairs={{0,2},{1,3},{2,0},{3,1},{4,6},{5,7},{6,4},{7,5},{8,10},{9,11},{10,... | collective-permute-start | bytes 196616 | tf_op jit(solution)/shard_map/ppermute | solution.py:39
  56.1 7.4 %collective-permute-start.12 = (bf16[128,256]{1,0:T(8,128)(2,1)S(1)}, bf16[128,256]{1,0:T(8,128)(2,1)S(1)}, u32[]{:S(2)}, u32[]{:S(2)}) collective-permute-start(bf16[128,256]{1,0:T(8,128)(2,1)S(1)} %get-tuple-element.40), channel_id=1, source_target_pairs={{0,2},{1,3},{2,0},{3,1},{4,6},{5,7},{6,4},{7,5},{8,10},{9,11},{10,... | collective-permute-start | bytes 196616 | tf_op jit(solution)/shard_map/ppermute | solution.py:39

commit v5 on v4

--- a/solution.py
+++ b/solution.py
@@ -73,10 +73,26 @@
     return me ^ (even + (odd - even) * core)
 
 
+def hold_kernel(x_ref, out_ref):
+    out_ref[...] = x_ref[...]
+
+
+def held(x):
+    return pl.pallas_call(
+        hold_kernel,
+        out_shape=jax.ShapeDtypeStruct(x.shape, x.dtype),
+        in_specs=[vmem()],
+        out_specs=vmem(),
+        compiler_params=kernel_params(),
+        name="held",
+    )(x)
+
+
 def attention_kernel(shards, blocks, heads, hd, scaling, *refs):
     meta = refs[0]
     chunks = refs[1 : 1 + shards]
-    dq_refs = refs[1 + shards : -8]
+    grad_chunks = refs[1 + shards : 1 + 2 * shards]
+    dq_refs = refs[1 + 2 * shards : -8]
     dk_ref, dv_ref, keys, values, queries, grads, inverse, starts = refs[-8:]
     me = meta[0]
     per_dev = blocks // shards
@@ -98,7 +114,8 @@
             rows = rows_at(position, 1)
             here = slice(b * span, (b + 1) * span)
             at = 0
-            for whole in (keys, values, queries, grads):
+            grads[rows, :] = grad_chunks[place][here, :]
+            for whole in (keys, values, queries):
                 whole[rows, :] = chunks[place][here, at : at + whole.shape[1]]
                 at += whole.shape[1]
 
@@ -208,16 +225,16 @@
 
 
 def attention(meta, blocks, hd, chunks, groups):
-    shards = len(chunks)
+    shards = len(chunks) // 2
     tok, columns = chunks[0].shape
     length = tok * shards
-    qw = (columns - 2 * hd) // 2
+    qw = columns - 2 * hd
     outs = (qw // groups,) * groups + (hd, hd)
     pairs = length * length // blocks
     return pl.pallas_call(
         functools.partial(attention_kernel, shards, blocks, qw // hd, hd, hd**-0.5),
         out_shape=tuple(jax.ShapeDtypeStruct((length, width), jnp.bfloat16) for width in outs),
-        in_specs=[smem()] + [vmem()] * shards,
+        in_specs=[smem()] + [vmem()] * (2 * shards),
         out_specs=(vmem(),) * len(outs),
         scratch_shapes=[
             pltpu.VMEM((length, hd), jnp.bfloat16),
@@ -353,11 +370,19 @@
     meta = jnp.concatenate([me, block_pos[0], doc_ids[0]])
     slab = layer_input[0]
 
-    own = jnp.concatenate([key_proj[0], value_proj[0], query_proj[0], out_grad[0]], axis=1)
-    sent = [across(own, step) for step in range(2)]
-    sent[0], meta = ordered(sent[0], meta)
-    sent.append(across(sent[0], 1))
-    chunks = with_other_core([own] + sent)
+    own_grad = out_grad[0]
+    own = jnp.concatenate([key_proj[0], value_proj[0], query_proj[0]], axis=1)
+    grad_sent = across(own_grad, 0)
+    sent = across(own, 0)
+    grad_sent, (own_grad, own, meta) = ordered(grad_sent, (own_grad, own, meta))
+    grad_chunks = [own_grad, grad_sent, across(own_grad, 1), across(grad_sent, 1)]
+    chunks = [own, sent, across(own, 1), across(sent, 1)]
+    early_grads = with_other_core([held(own_grad)] + grad_chunks[1:3])
+    early = with_other_core(chunks[:3])
+    (grad_chunks, chunks), (early_grads, early) = ordered(
+        (grad_chunks, chunks), (early_grads, early)
+    )
+    chunks = early + with_other_core(chunks[3:]) + early_grads + with_other_core(grad_chunks[3:])
     *dqs, dk, dv = attention(meta, blocks, hd, chunks, 2)
 
     halving = 1 < dp <= 8 and dp & (dp - 1) == 0

time: 64.4 us -> 60.8 us (0.944)
  waiting for transfers between devices: 29 us -> 19 us
  starting transfers between devices: 19.2 us -> 23.7 us
  local copies, waits for them, and re-layouts: 0.01 us -> 0.96 us
    ppermute x3 -> x6, waiting for transfers between devices: 21.9 us -> 10 us  [across(): return lax.ppermute(x, 'seq', pairs)]
    ppermute x3 -> x6, starting transfers between devices: 6.09 us -> 9.36 us  [across(): return lax.ppermute(x, 'seq', pairs)]
    ppermute x10 -> x14, waiting for transfers between devices: 7.09 us -> 8.93 us  [swap(): lax.ppermute(x, axis, [(i, i ^ rel) for i in range(lax.axis_size(axis))])]
    ppermute x10 -> x14, starting transfers between devices: 13.2 us -> 14.4 us  [swap(): lax.ppermute(x, axis, [(i, i ^ rel) for i in range(lax.axis_size(axis))])]
    unnamed x6 -> x4, local copies, waits for them, and re-layouts: 0.01 us -> 0.96 us
    concatenate x1, other arithmetic: 0.08 us -> 0.75 us  [body(): meta = jnp.concatenate([me, block_pos[0], doc_ids[0]])]
  transfers between devices with their start and end apart: 13 -> 20, of which waited for: 6 -> 9; matrix products, arithmetic and copies ran while one was open for 0% -> 3% of each run, Pallas kernels for 5% -> 5%
where the time goes in v5:
time: 60.8 us
  starting transfers between devices  23.7 us (39%)
  waiting for transfers between devices  19 us (31%)
  Pallas kernels  15.3 us (25%)
  other arithmetic  1.77 us (3%)
  local copies, waits for them, and re-layouts  0.96 us (2%)
    ppermute x14, starting transfers between devices, swap(): lax.ppermute(x, axis, [(i, i ^ rel) for i in range(lax.axis_size(axis))])  14.4 us
    ppermute x6, waiting for transfers between devices, across(): return lax.ppermute(x, 'seq', pairs)  10 us
    pallas_call x1, Pallas kernels, attention(): pl.pallas_call(functools.partial(attention_kernel, shards, blocks, qw //...  9.87 us
    ppermute x6, starting transfers between devices, across(): return lax.ppermute(x, 'seq', pairs)  9.36 us
    ppermute x14, waiting for transfers between devices, swap(): lax.ppermute(x, axis, [(i, i ^ rel) for i in range(lax.axis_size(axis))])  8.93 us
    pallas_call x3, Pallas kernels, weight_part(): pl.pallas_call(functools.partial(weight_kernel, owners, at_once, len(grad...  4.51 us
  transfers between devices with their start and end apart: 20, of which 9 were waited for; matrix products, arithmetic and copies ran while one was open for 3% of the time, Pallas kernels for 5%

profile of v5, /device:TPU:0, one launch (start us, length us, event | category | flops | bytes accessed | tf_op | source)
XLA Modules:
  0.0 60.8 jit_solution(818675623709950057)
XLA Ops:
  0.0 2.9 %collective-permute-start = (bf16[256,512]{1,0:T(8,128)(2,1)}, bf16[256,512]{1,0:T(8,128)(2,1)S(1)}, u32[]{:S(2)}, u32[]{:S(2)}) collective-permute-start(bf16[256,512]{1,0:T(8,128)(2,1)} %bitcast.12), channel_id=1, source_target_pairs={{0,8},{4,20},{8,0},{12,28},{16,24},{20,4},{24,16},{28,12},{1,9},{5... | collective-permute-start | bytes 786440 | tf_op jit(solution)/shard_map/ppermute | solution.py:51
  2.9 1.0 %pad_maximum_fusion.refs_1_ = bf16[256,768]{1,0:T(8,128)(2,1)S(1)} fusion(bf16[256,512]{1,0:T(8,128)(2,1)} %bitcast.15, bf16[256,128]{1,0:T(8,128)(2,1)} %bitcast.16, bf16[256,128]{1,0:T(8,128)(2,1)} %bitcast.17), kind=kLoop, calls=%fused_computation | loop fusion | flops 1179648 | bytes 786432 | tf_op jit(solution)/shard_map/concatenate | solution.py:374
  4.0 0.1 collective-permute-start.3
  4.0 0.8 %pad_add_fusion.refs_0_.meta = s32[34]{0:T(128)S(1)} fusion(s32[16]{0:T(128)} %bitcast.18, s32[16]{0:T(128)} %bitcast.19, s32[1]{0:T(128)} %bitcast.5, s32[1]{0:T(128)} %bitcast.4), kind=kLoop, calls=%fused_computation.1 | loop fusion | flops 102 | bytes 272 | tf_op jit(solution)/shard_map/concatenate | solution.py:370
  4.8 2.7 %collective-permute-done.refs_11_ = bf16[256,512]{1,0:T(8,128)(2,1)S(1)} collective-permute-done((bf16[256,512]{1,0:T(8,128)(2,1)}, bf16[256,512]{1,0:T(8,128)(2,1)S(1)}, u32[]{:S(2)}, u32[]{:S(2)}) %collective-permute-start) | collective-permute-done | bytes 262176 | tf_op jit(solution)/shard_map/ppermute | solution.py:51
  7.5 2.1 %collective-permute-start.4 = (bf16[256,768]{1,0:T(8,128)(2,1)S(1)}, bf16[256,768]{1,0:T(8,128)(2,1)S(1)}, u32[]{:S(2)}, u32[]{:S(2)}) collective-permute-start(bf16[256,768]{1,0:T(8,128)(2,1)S(1)} %pad_maximum_fusion.refs_1_), channel_id=1, source_target_pairs={{0,16},{4,12},{8,24},{12,4},{16,0},{20,28},{24,8},{28,20},{1,17},{... | collective-permute-start | bytes 1179656 | tf_op jit(solution)/shard_map/ppermute | solution.py:51
  9.6 0.0 copy-start.1
  9.6 0.9 %copy-done.1 = bf16[1,256,512]{2,1,0:T(8,128)(2,1)S(1)} copy-done((bf16[1,256,512]{2,1,0:T(8,128)(2,1)S(1)}, bf16[1,256,512]{2,1,0:T(8,128)(2,1)}, u32[]{:S(2)}) %copy-start.1) | copy-done | bytes 262168
  10.5 0.0 copy-start
  10.5 0.1 collective-permute-start.6
  10.6 0.2 collective-permute-start.1
  10.8 1.5 %collective-permute-start.7 = (bf16[256,512]{1,0:T(8,128)(2,1)S(1)}, bf16[256,512]{1,0:T(8,128)(2,1)S(1)}, u32[]{:S(2)}, u32[]{:S(2)}) collective-permute-start(bf16[256,512]{1,0:T(8,128)(2,1)S(1)} %collective-permute-done.refs_11_), channel_id=1, source_target_pairs={{0,4},{4,0},{8,12},{12,8},{16,20},{20,16},{24,28},{28,24},{1,5},{5... | collective-permute-start | bytes 786440 | tf_op jit(solution)/shard_map/ppermute | solution.py:39
  12.3 1.8 %collective-permute-done.3.refs_3_ = bf16[256,768]{1,0:T(8,128)(2,1)S(1)} collective-permute-done((bf16[256,768]{1,0:T(8,128)(2,1)S(1)}, bf16[256,768]{1,0:T(8,128)(2,1)S(1)}, u32[]{:S(2)}, u32[]{:S(2)}) %collective-permute-start.3) | collective-permute-done | bytes 393248 | tf_op jit(solution)/shard_map/ppermute | solution.py:51
  14.2 2.2 %collective-permute-start.2 = (bf16[256,512]{1,0:T(8,128)(2,1)S(1)}, bf16[256,512]{1,0:T(8,128)(2,1)S(1)}, u32[]{:S(2)}, u32[]{:S(2)}) collective-permute-start(bf16[256,512]{1,0:T(8,128)(2,1)S(1)} %collective-permute-done.refs_11_), channel_id=1, source_target_pairs={{0,16},{4,12},{8,24},{12,4},{16,0},{20,28},{24,8},{28,20},{1,17},{... | collective-permute-start | bytes 786440 | tf_op jit(solution)/shard_map/ppermute | solution.py:51
  16.3 0.0 collective-permute-done.6.refs_10_
  16.3 0.0 collective-permute-start.9
  16.3 1.8 %collective-permute-done.1.refs_13_ = bf16[256,512]{1,0:T(8,128)(2,1)S(1)} collective-permute-done((bf16[256,512]{1,0:T(8,128)(2,1)S(1)}, bf16[256,512]{1,0:T(8,128)(2,1)S(1)}, u32[]{:S(2)}, u32[]{:S(2)}) %collective-permute-start.1) | collective-permute-done | bytes 262176 | tf_op jit(solution)/shard_map/ppermute | solution.py:51
  18.1 0.8 %collective-permute-start.10 = (bf16[256,768]{1,0:T(8,128)(2,1)S(1)}, bf16[256,768]{1,0:T(8,128)(2,1)S(1)}, u32[]{:S(2)}, u32[]{:S(2)}) collective-permute-start(bf16[256,768]{1,0:T(8,128)(2,1)S(1)} %collective-permute-done.3.refs_3_), channel_id=1, source_target_pairs={{0,4},{4,0},{8,12},{12,8},{16,20},{20,16},{24,28},{28,24},{1,5},{5... | collective-permute-start | bytes 1179656 | tf_op jit(solution)/shard_map/ppermute | solution.py:39
  18.9 0.0 collective-permute-done.7.refs_12_
  18.9 2.0 %collective-permute-start.5 = (bf16[256,768]{1,0:T(8,128)(2,1)S(1)}, bf16[256,768]{1,0:T(8,128)(2,1)S(1)}, u32[]{:S(2)}, u32[]{:S(2)}) collective-permute-start(bf16[256,768]{1,0:T(8,128)(2,1)S(1)} %collective-permute-done.3.refs_3_), channel_id=1, source_target_pairs={{0,16},{4,12},{8,24},{12,4},{16,0},{20,28},{24,8},{28,20},{1,17},{... | collective-permute-start | bytes 1179656 | tf_op jit(solution)/shard_map/ppermute | solution.py:51
  20.9 0.0 collective-permute-done.4.refs_5_
  20.9 0.0 collective-permute-start.11
  20.9 0.0 collective-permute-done.2.refs_15_
  20.9 0.5 collective-permute-start.8
  21.5 0.0 collective-permute-done.9.refs_2_
  21.5 1.5 %collective-permute-done.8.refs_14_ = bf16[256,512]{1,0:T(8,128)(2,1)S(1)} collective-permute-done((bf16[256,512]{1,0:T(8,128)(2,1)S(1)}, bf16[256,512]{1,0:T(8,128)(2,1)S(1)}, u32[]{:S(2)}, u32[]{:S(2)}) %collective-permute-start.8) | collective-permute-done | bytes 262176 | tf_op jit(solution)/shard_map/ppermute | solution.py:39
  23.0 0.0 collective-permute-done.10.refs_4_
  23.0 3.7 %collective-permute-done.5.refs_7_ = bf16[256,768]{1,0:T(8,128)(2,1)S(1)} collective-permute-done((bf16[256,768]{1,0:T(8,128)(2,1)S(1)}, bf16[256,768]{1,0:T(8,128)(2,1)S(1)}, u32[]{:S(2)}, u32[]{:S(2)}) %collective-permute-start.5) | collective-permute-done | bytes 393248 | tf_op jit(solution)/shard_map/ppermute | solution.py:51
  26.7 0.0 collective-permute-done.11.refs_6_
  26.7 0.0 collective-permute-start.12
  26.7 0.5 collective-permute-start.13
  27.2 1.6 %collective-permute-done.13.refs_16_ = bf16[256,512]{1,0:T(8,128)(2,1)S(1)} collective-permute-done((bf16[256,512]{1,0:T(8,128)(2,1)S(1)}, bf16[256,512]{1,0:T(8,128)(2,1)S(1)}, u32[]{:S(2)}, u32[]{:S(2)}) %collective-permute-start.13) | collective-permute-done | bytes 262176 | tf_op jit(solution)/shard_map/ppermute | solution.py:39
  28.8 0.0 collective-permute-done.12.refs_8_
  28.8 9.9 %attention.1 = (bf16[2048,256]{1,0:T(8,128)(2,1)S(1)}, bf16[2048,256]{1,0:T(8,128)(2,1)S(1)}, bf16[2048,128]{1,0:T(8,128)(2,1)S(1)}, bf16[2048,128]{1,0:T(8,128)(2,1)S(1)}) custom-call(s32[34]{0:T(128)S(1)} %pad_add_fusion.refs_0_.meta, bf16[256,768]{1,0:T(8,128)(2,1)S(1)} %pad_maximum_fusion.refs_1_, bf16[256,768]{1,0:T(8,128)(2,1)S(1)} %collective-permute-done.9.refs_2_, ...), custom_call_target="tpu_custom_call" | custom-call | flops 2684354560 | bytes 6291456 | tf_op jit(solution)/shard_map/attention/pallas_call | solution.py:234
  38.7 0.0 copy-done
  38.7 1.3 %weight_part.3 = (f32[256,256]{1,0:T(8,128)S(1)}, bf16[256,256]{1,0:T(8,128)(2,1)S(1)}) custom-call(s32[34]{0:T(128)S(1)} %pad_add_fusion.refs_0_.meta, bf16[2048,512]{1,0:T(8,128)(2,1)S(1)} %bitcast.9, bf16[2048,256]{1,0:T(8,128)(2,1)S(1)} %get-tuple-element.57.refs_0_), custom_call_target="tpu_custom_call" | custom-call | flops 536870912 | bytes 3145728 | tf_op jit(solution)/shard_map/weight_part/pallas_call | solution.py:285
  40.1 2.1 %collective-permute-start.14 = (bf16[256,256]{1,0:T(8,128)(2,1)S(1)}, bf16[256,256]{1,0:T(8,128)(2,1)S(1)}, u32[]{:S(2)}, u32[]{:S(2)}) collective-permute-start(bf16[256,256]{1,0:T(8,128)(2,1)S(1)} %get-tuple-element.59), channel_id=1, source_target_pairs={{0,1},{1,0},{2,3},{3,2},{4,5},{5,4},{6,7},{7,6},{8,9},{9,8},{10,11... | collective-permute-start | bytes 393224 | tf_op jit(solution)/shard_map/ppermute | solution.py:39
  42.1 1.3 %weight_part.4 = (f32[256,256]{1,0:T(8,128)S(1)}, bf16[256,256]{1,0:T(8,128)(2,1)S(1)}) custom-call(s32[34]{0:T(128)S(1)} %pad_add_fusion.refs_0_.meta, bf16[2048,512]{1,0:T(8,128)(2,1)S(1)} %bitcast.10, bf16[2048,256]{1,0:T(8,128)(2,1)S(1)} %get-tuple-element.62.refs_0_), custom_call_target="tpu_custom_call" | custom-call | flops 536870912 | bytes 3145728 | tf_op jit(solution)/shard_map/weight_part/pallas_call | solution.py:285
  43.5 0.1 collective-permute-start.16
  43.5 1.9 %weight_part.5 = (f32[256,256]{1,0:T(8,128)S(1)}, bf16[256,256]{1,0:T(8,128)(2,1)S(1)}) custom-call(s32[34]{0:T(128)S(1)} %pad_add_fusion.refs_0_.meta, bf16[2048,512]{1,0:T(8,128)(2,1)S(1)} %bitcast.11, bf16[2048,128]{1,0:T(8,128)(2,1)S(1)} %get-tuple-element.67.refs_0_, bf16[2048,128]{1,0:T(8,128)(2,1)S(1)} %get-tuple-element.68.refs_1_), custom_call_target="tpu_custom_call" | custom-call | flops 536870912 | bytes 3145728 | tf_op jit(solution)/shard_map/weight_part/pallas_call | solution.py:285
  45.4 2.1 %collective-permute-start.18 = (bf16[256,256]{1,0:T(8,128)(2,1)S(1)}, bf16[256,256]{1,0:T(8,128)(2,1)S(1)}, u32[]{:S(2)}, u32[]{:S(2)}) collective-permute-start(bf16[256,256]{1,0:T(8,128)(2,1)S(1)} %get-tuple-element.70), channel_id=1, source_target_pairs={{0,1},{1,0},{2,3},{3,2},{4,5},{5,4},{6,7},{7,6},{8,9},{9,8},{10,11... | collective-permute-start | bytes 393224 | tf_op jit(solution)/shard_map/ppermute | solution.py:39
  47.5 0.0 collective-permute-done.14.arrived_ref
  47.5 2.6 %collective-permute-start.15 = (bf16[128,256]{1,0:T(8,128)(2,1)S(1)}, bf16[128,256]{1,0:T(8,128)(2,1)S(1)}, u32[]{:S(2)}, u32[]{:S(2)}) collective-permute-start(bf16[128,256]{1,0:T(8,128)(2,1)S(1)} %get-tuple-element.61), channel_id=1, source_target_pairs={{0,2},{1,3},{2,0},{3,1},{4,6},{5,7},{6,4},{7,5},{8,10},{9,11},{10,... | collective-permute-start | bytes 196616 | tf_op jit(solution)/shard_map/ppermute | solution.py:39
  50.2 0.0 collective-permute-done.16.arrived_ref
  50.2 2.2 %collective-permute-start.17 = (bf16[128,256]{1,0:T(8,128)(2,1)S(1)}, bf16[128,256]{1,0:T(8,128)(2,1)S(1)}, u32[]{:S(2)}, u32[]{:S(2)}) collective-permute-start(bf16[128,256]{1,0:T(8,128)(2,1)S(1)} %get-tuple-element.66), channel_id=1, source_target_pairs={{0,2},{1,3},{2,0},{3,1},{4,6},{5,7},{6,4},{7,5},{8,10},{9,11},{10,... | collective-permute-start | bytes 196616 | tf_op jit(solution)/shard_map/ppermute | solution.py:39
  52.4 0.9 %collective-permute-done.18.arrived_ref = bf16[256,256]{1,0:T(8,128)(2,1)S(1)} collective-permute-done((bf16[256,256]{1,0:T(8,128)(2,1)S(1)}, bf16[256,256]{1,0:T(8,128)(2,1)S(1)}, u32[]{:S(2)}, u32[]{:S(2)}) %collective-permute-start.18) | collective-permute-done | bytes 131104 | tf_op jit(solution)/shard_map/ppermute | solution.py:39
  53.3 1.8 %collective-permute-start.19 = (bf16[128,256]{1,0:T(8,128)(2,1)S(1)}, bf16[128,256]{1,0:T(8,128)(2,1)S(1)}, u32[]{:S(2)}, u32[]{:S(2)}) collective-permute-start(bf16[128,256]{1,0:T(8,128)(2,1)S(1)} %get-tuple-element.72), channel_id=1, source_target_pairs={{0,2},{1,3},{2,0},{3,1},{4,6},{5,7},{6,4},{7,5},{8,10},{9,11},{10,... | collective-permute-start | bytes 196616 | tf_op jit(solution)/shard_map/ppermute | solution.py:39
  55.2 0.0 collective-permute-done.15.refs_1_
  55.2 3.4 %collective-permute-done.17.refs_3_ = bf16[128,256]{1,0:T(8,128)(2,1)S(1)} collective-permute-done((bf16[128,256]{1,0:T(8,128)(2,1)S(1)}, bf16[128,256]{1,0:T(8,128)(2,1)S(1)}, u32[]{:S(2)}, u32[]{:S(2)}) %collective-permute-start.17) | collective-permute-done | bytes 65568 | tf_op jit(solution)/shard_map/ppermute | solution.py:39
  58.6 1.4 %collective-permute-done.19.refs_5_ = bf16[128,256]{1,0:T(8,128)(2,1)S(1)} collective-permute-done((bf16[128,256]{1,0:T(8,128)(2,1)S(1)}, bf16[128,256]{1,0:T(8,128)(2,1)S(1)}, u32[]{:S(2)}, u32[]{:S(2)}) %collective-permute-start.19) | collective-permute-done | bytes 65568 | tf_op jit(solution)/shard_map/ppermute | solution.py:39
  60.0 0.8 %final_sum.1 = f32[128,768]{1,0:T(8,128)} custom-call(f32[128,256]{1,0:T(8,128)S(1)} %get-tuple-element.60.refs_0_, bf16[128,256]{1,0:T(8,128)(2,1)S(1)} %collective-permute-done.15.refs_1_, f32[128,256]{1,0:T(8,128)S(1)} %get-tuple-element.65.refs_2_, bf16[128,256]{1,0:T(8,128)(2,1)S(1)} %collective-permute-done.17.refs_3_, ...), custom_call_target="tpu_custom_call" | custom-call | tf_op jit(solution)/shard_map/final_sum/pallas_call | solution.py:343
  (4 shorter events, 0.1 us)
Async XLA Ops:
  0.0 7.5 %collective-permute-start = (bf16[256,512]{1,0:T(8,128)(2,1)}, bf16[256,512]{1,0:T(8,128)(2,1)S(1)}, u32[]{:S(2)}, u32[]{:S(2)}) collective-permute-start(bf16[256,512]{1,0:T(8,128)(2,1)} %bitcast.12), channel_id=1, source_target_pairs={{0,8},{4,20},{8,0},{12,28},{16,24},{20,4},{24,16},{28,12},{1,9},{5... | collective-permute-start | bytes 786440 | tf_op jit(solution)/shard_map/ppermute | solution.py:51
  4.0 10.2 %collective-permute-start.3 = (bf16[256,768]{1,0:T(8,128)(2,1)S(1)}, bf16[256,768]{1,0:T(8,128)(2,1)S(1)}, u32[]{:S(2)}, u32[]{:S(2)}) collective-permute-start(bf16[256,768]{1,0:T(8,128)(2,1)S(1)} %pad_maximum_fusion.refs_1_), channel_id=1, source_target_pairs={{0,8},{4,20},{8,0},{12,28},{16,24},{20,4},{24,16},{28,12},{1,9},{5... | collective-permute-start | bytes 1179656 | tf_op jit(solution)/shard_map/ppermute | solution.py:51
  7.5 13.4 %collective-permute-start.4 = (bf16[256,768]{1,0:T(8,128)(2,1)S(1)}, bf16[256,768]{1,0:T(8,128)(2,1)S(1)}, u32[]{:S(2)}, u32[]{:S(2)}) collective-permute-start(bf16[256,768]{1,0:T(8,128)(2,1)S(1)} %pad_maximum_fusion.refs_1_), channel_id=1, source_target_pairs={{0,16},{4,12},{8,24},{12,4},{16,0},{20,28},{24,8},{28,20},{1,17},{... | collective-permute-start | bytes 1179656 | tf_op jit(solution)/shard_map/ppermute | solution.py:51
  9.6 0.9 %copy-start.1 = (bf16[1,256,512]{2,1,0:T(8,128)(2,1)S(1)}, bf16[1,256,512]{2,1,0:T(8,128)(2,1)}, u32[]{:S(2)}) copy-start(bf16[1,256,512]{2,1,0:T(8,128)(2,1)} %param.11) | copy-start | bytes 786436
  10.5 28.2 %copy-start = (bf16[1,2048,512]{2,1,0:T(8,128)(2,1)S(1)}, bf16[1,2048,512]{2,1,0:T(8,128)(2,1)}, u32[]{:S(2)}) copy-start(bf16[1,2048,512]{2,1,0:T(8,128)(2,1)} %param.7) | copy-start | bytes 6291460
  10.5 5.8 %collective-permute-start.6 = (bf16[256,512]{1,0:T(8,128)(2,1)S(1)}, bf16[256,512]{1,0:T(8,128)(2,1)S(1)}, u32[]{:S(2)}, u32[]{:S(2)}) collective-permute-start(bf16[256,512]{1,0:T(8,128)(2,1)S(1)} %held.1.refs_9_), channel_id=1, source_target_pairs={{0,4},{4,0},{8,12},{12,8},{16,20},{20,16},{24,28},{28,24},{1,5},{5... | collective-permute-start | bytes 786440 | tf_op jit(solution)/shard_map/ppermute | solution.py:39
  10.6 7.5 %collective-permute-start.1 = (bf16[256,512]{1,0:T(8,128)(2,1)S(1)}, bf16[256,512]{1,0:T(8,128)(2,1)S(1)}, u32[]{:S(2)}, u32[]{:S(2)}) collective-permute-start(bf16[256,512]{1,0:T(8,128)(2,1)S(1)} %bitcast.14), channel_id=1, source_target_pairs={{0,16},{4,12},{8,24},{12,4},{16,0},{20,28},{24,8},{28,20},{1,17},{... | collective-permute-start | bytes 786440 | tf_op jit(solution)/shard_map/ppermute | solution.py:51
  10.8 8.2 %collective-permute-start.7 = (bf16[256,512]{1,0:T(8,128)(2,1)S(1)}, bf16[256,512]{1,0:T(8,128)(2,1)S(1)}, u32[]{:S(2)}, u32[]{:S(2)}) collective-permute-start(bf16[256,512]{1,0:T(8,128)(2,1)S(1)} %collective-permute-done.refs_11_), channel_id=1, source_target_pairs={{0,4},{4,0},{8,12},{12,8},{16,20},{20,16},{24,28},{28,24},{1,5},{5... | collective-permute-start | bytes 786440 | tf_op jit(solution)/shard_map/ppermute | solution.py:39
  14.2 6.8 %collective-permute-start.2 = (bf16[256,512]{1,0:T(8,128)(2,1)S(1)}, bf16[256,512]{1,0:T(8,128)(2,1)S(1)}, u32[]{:S(2)}, u32[]{:S(2)}) collective-permute-start(bf16[256,512]{1,0:T(8,128)(2,1)S(1)} %collective-permute-done.refs_11_), channel_id=1, source_target_pairs={{0,16},{4,12},{8,24},{12,4},{16,0},{20,28},{24,8},{28,20},{1,17},{... | collective-permute-start | bytes 786440 | tf_op jit(solution)/shard_map/ppermute | solution.py:51
  16.3 5.1 %collective-permute-start.9 = (bf16[256,768]{1,0:T(8,128)(2,1)S(1)}, bf16[256,768]{1,0:T(8,128)(2,1)S(1)}, u32[]{:S(2)}, u32[]{:S(2)}) collective-permute-start(bf16[256,768]{1,0:T(8,128)(2,1)S(1)} %pad_maximum_fusion.refs_1_), channel_id=1, source_target_pairs={{0,4},{4,0},{8,12},{12,8},{16,20},{20,16},{24,28},{28,24},{1,5},{5... | collective-permute-start | bytes 1179656 | tf_op jit(solution)/shard_map/ppermute | solution.py:39
  18.1 4.9 %collective-permute-start.10 = (bf16[256,768]{1,0:T(8,128)(2,1)S(1)}, bf16[256,768]{1,0:T(8,128)(2,1)S(1)}, u32[]{:S(2)}, u32[]{:S(2)}) collective-permute-start(bf16[256,768]{1,0:T(8,128)(2,1)S(1)} %collective-permute-done.3.refs_3_), channel_id=1, source_target_pairs={{0,4},{4,0},{8,12},{12,8},{16,20},{20,16},{24,28},{28,24},{1,5},{5... | collective-permute-start | bytes 1179656 | tf_op jit(solution)/shard_map/ppermute | solution.py:39
  18.9 7.8 %collective-permute-start.5 = (bf16[256,768]{1,0:T(8,128)(2,1)S(1)}, bf16[256,768]{1,0:T(8,128)(2,1)S(1)}, u32[]{:S(2)}, u32[]{:S(2)}) collective-permute-start(bf16[256,768]{1,0:T(8,128)(2,1)S(1)} %collective-permute-done.3.refs_3_), channel_id=1, source_target_pairs={{0,16},{4,12},{8,24},{12,4},{16,0},{20,28},{24,8},{28,20},{1,17},{... | collective-permute-start | bytes 1179656 | tf_op jit(solution)/shard_map/ppermute | solution.py:51
  20.9 5.8 %collective-permute-start.11 = (bf16[256,768]{1,0:T(8,128)(2,1)S(1)}, bf16[256,768]{1,0:T(8,128)(2,1)S(1)}, u32[]{:S(2)}, u32[]{:S(2)}) collective-permute-start(bf16[256,768]{1,0:T(8,128)(2,1)S(1)} %collective-permute-done.4.refs_5_), channel_id=1, source_target_pairs={{0,4},{4,0},{8,12},{12,8},{16,20},{20,16},{24,28},{28,24},{1,5},{5... | collective-permute-start | bytes 1179656 | tf_op jit(solution)/shard_map/ppermute | solution.py:39
  20.9 2.1 %collective-permute-start.8 = (bf16[256,512]{1,0:T(8,128)(2,1)S(1)}, bf16[256,512]{1,0:T(8,128)(2,1)S(1)}, u32[]{:S(2)}, u32[]{:S(2)}) collective-permute-start(bf16[256,512]{1,0:T(8,128)(2,1)S(1)} %collective-permute-done.1.refs_13_), channel_id=1, source_target_pairs={{0,4},{4,0},{8,12},{12,8},{16,20},{20,16},{24,28},{28,24},{1,5},{5... | collective-permute-start | bytes 786440 | tf_op jit(solution)/shard_map/ppermute | solution.py:39
  26.7 2.1 %collective-permute-start.12 = (bf16[256,768]{1,0:T(8,128)(2,1)S(1)}, bf16[256,768]{1,0:T(8,128)(2,1)S(1)}, u32[]{:S(2)}, u32[]{:S(2)}) collective-permute-start(bf16[256,768]{1,0:T(8,128)(2,1)S(1)} %collective-permute-done.5.refs_7_), channel_id=1, source_target_pairs={{0,4},{4,0},{8,12},{12,8},{16,20},{20,16},{24,28},{28,24},{1,5},{5... | collective-permute-start | bytes 1179656 | tf_op jit(solution)/shard_map/ppermute | solution.py:39
  26.7 2.1 %collective-permute-start.13 = (bf16[256,512]{1,0:T(8,128)(2,1)S(1)}, bf16[256,512]{1,0:T(8,128)(2,1)S(1)}, u32[]{:S(2)}, u32[]{:S(2)}) collective-permute-start(bf16[256,512]{1,0:T(8,128)(2,1)S(1)} %collective-permute-done.2.refs_15_), channel_id=1, source_target_pairs={{0,4},{4,0},{8,12},{12,8},{16,20},{20,16},{24,28},{28,24},{1,5},{5... | collective-permute-start | bytes 786440 | tf_op jit(solution)/shard_map/ppermute | solution.py:39
  40.1 7.4 %collective-permute-start.14 = (bf16[256,256]{1,0:T(8,128)(2,1)S(1)}, bf16[256,256]{1,0:T(8,128)(2,1)S(1)}, u32[]{:S(2)}, u32[]{:S(2)}) collective-permute-start(bf16[256,256]{1,0:T(8,128)(2,1)S(1)} %get-tuple-element.59), channel_id=1, source_target_pairs={{0,1},{1,0},{2,3},{3,2},{4,5},{5,4},{6,7},{7,6},{8,9},{9,8},{10,11... | collective-permute-start | bytes 393224 | tf_op jit(solution)/shard_map/ppermute | solution.py:39
  43.5 6.7 %collective-permute-start.16 = (bf16[256,256]{1,0:T(8,128)(2,1)S(1)}, bf16[256,256]{1,0:T(8,128)(2,1)S(1)}, u32[]{:S(2)}, u32[]{:S(2)}) collective-permute-start(bf16[256,256]{1,0:T(8,128)(2,1)S(1)} %get-tuple-element.64), channel_id=1, source_target_pairs={{0,1},{1,0},{2,3},{3,2},{4,5},{5,4},{6,7},{7,6},{8,9},{9,8},{10,11... | collective-permute-start | bytes 393224 | tf_op jit(solution)/shard_map/ppermute | solution.py:39
  45.4 7.9 %collective-permute-start.18 = (bf16[256,256]{1,0:T(8,128)(2,1)S(1)}, bf16[256,256]{1,0:T(8,128)(2,1)S(1)}, u32[]{:S(2)}, u32[]{:S(2)}) collective-permute-start(bf16[256,256]{1,0:T(8,128)(2,1)S(1)} %get-tuple-element.70), channel_id=1, source_target_pairs={{0,1},{1,0},{2,3},{3,2},{4,5},{5,4},{6,7},{7,6},{8,9},{9,8},{10,11... | collective-permute-start | bytes 393224 | tf_op jit(solution)/shard_map/ppermute | solution.py:39
  47.5 7.7 %collective-permute-start.15 = (bf16[128,256]{1,0:T(8,128)(2,1)S(1)}, bf16[128,256]{1,0:T(8,128)(2,1)S(1)}, u32[]{:S(2)}, u32[]{:S(2)}) collective-permute-start(bf16[128,256]{1,0:T(8,128)(2,1)S(1)} %get-tuple-element.61), channel_id=1, source_target_pairs={{0,2},{1,3},{2,0},{3,1},{4,6},{5,7},{6,4},{7,5},{8,10},{9,11},{10,... | collective-permute-start | bytes 196616 | tf_op jit(solution)/shard_map/ppermute | solution.py:39
  50.2 8.4 %collective-permute-start.17 = (bf16[128,256]{1,0:T(8,128)(2,1)S(1)}, bf16[128,256]{1,0:T(8,128)(2,1)S(1)}, u32[]{:S(2)}, u32[]{:S(2)}) collective-permute-start(bf16[128,256]{1,0:T(8,128)(2,1)S(1)} %get-tuple-element.66), channel_id=1, source_target_pairs={{0,2},{1,3},{2,0},{3,1},{4,6},{5,7},{6,4},{7,5},{8,10},{9,11},{10,... | collective-permute-start | bytes 196616 | tf_op jit(solution)/shard_map/ppermute | solution.py:39
  53.3 6.7 %collective-permute-start.19 = (bf16[128,256]{1,0:T(8,128)(2,1)S(1)}, bf16[128,256]{1,0:T(8,128)(2,1)S(1)}, u32[]{:S(2)}, u32[]{:S(2)}) collective-permute-start(bf16[128,256]{1,0:T(8,128)(2,1)S(1)} %get-tuple-element.72), channel_id=1, source_target_pairs={{0,2},{1,3},{2,0},{3,1},{4,6},{5,7},{6,4},{7,5},{8,10},{9,11},{10,... | collective-permute-start | bytes 196616 | tf_op jit(solution)/shard_map/ppermute | solution.py:39

commit v6 on v5

--- a/solution.py
+++ b/solution.py
@@ -12,7 +12,7 @@
 MOST_DOC = 4
 TOGETHER = 1
 AT_ONCE = {1: (4, 2, 1), 2: (2, 1), 3: (1,), 4: (1,)}
-VMEM_LIMIT = 24 * 1024 * 1024
+VMEM_LIMIT = 16 * 1024 * 1024
 
 NT = (((1,), (1,)), ((), ()))
 NN = (((1,), (0,)), ((), ()))
@@ -256,25 +256,22 @@
 
 def weight_kernel(owners, at_once, parts, meta, slab_ref, *refs):
     rows_refs = refs[:parts]
-    kept, sent, total = refs[parts], refs[parts + 1 : -1], refs[-1]
+    kept, sent = refs[parts], refs[parts + 1 :]
     my_dp = meta[1]
-    first = 0
-    for ref in rows_refs:
-        width = ref.shape[1]
-        total[:, first : first + width] = dot(slab_ref[...], ref[...], TN)
-        first += width
-    piece = total.shape[0] // owners
+    piece = slab_ref.shape[1] // owners
     for rel in range(owners):
-        rows = pl.ds(pl.multiple_of((my_dp ^ rel) * piece, piece), piece)
+        features = pl.ds(pl.multiple_of((my_dp ^ rel) * piece, piece), piece)
         to = slice((rel >> 1) * piece, ((rel >> 1) + 1) * piece)
-        if at_once and rel:
-            sent[rel - 1][...] = total[rows, :].astype(sent[rel - 1].dtype)
-        elif at_once:
-            kept[...] = total[rows, :]
-        elif rel & 1:
-            sent[0][to, :] = total[rows, :].astype(sent[0].dtype)
+        if at_once:
+            ref, to = (sent[rel - 1] if rel else kept), slice(0, piece)
         else:
-            kept[to, :] = total[rows, :]
+            ref = sent[0] if rel & 1 else kept
+        first = 0
+        for rows in rows_refs:
+            width = rows.shape[1]
+            total = dot(slab_ref[:, features], rows[...], TN)
+            ref[to, first : first + width] = total.astype(ref.dtype)
+            first += width
 
 
 def weight_part(meta, slab, grads, owners, at_once):
@@ -288,7 +285,6 @@
         + (jax.ShapeDtypeStruct((rows, columns), jnp.bfloat16),) * sends,
         in_specs=[smem()] + [vmem()] * (1 + len(grads)),
         out_specs=(vmem(),) * (1 + sends),
-        scratch_shapes=[pltpu.VMEM((features, columns), jnp.float32)],
         compiler_params=kernel_params(),
         cost_estimate=pl.CostEstimate(
             flops=2 * length * features * columns,

time: 60.8 us -> 60.9 us (level)
  no operation moved by 1% of the time
where the time goes in v6:
time: 60.9 us; the launch traced here: 60.7 us
  starting transfers between devices  24.2 us (40%)
  waiting for transfers between devices  18.9 us (31%)
  Pallas kernels  14.8 us (24%)
  other arithmetic  1.77 us (3%)
  local copies, waits for them, and re-layouts  0.96 us (2%)
    ppermute x14, starting transfers between devices, swap(): lax.ppermute(x, axis, [(i, i ^ rel) for i in range(lax.axis_size(axis))])  14.8 us
    ppermute x6, waiting for transfers between devices, across(): return lax.ppermute(x, 'seq', pairs)  10 us
    pallas_call x1, Pallas kernels, attention(): pl.pallas_call(functools.partial(attention_kernel, shards, blocks, qw //...  9.37 us
    ppermute x6, starting transfers between devices, across(): return lax.ppermute(x, 'seq', pairs)  9.36 us
    ppermute x14, waiting for transfers between devices, swap(): lax.ppermute(x, axis, [(i, i ^ rel) for i in range(lax.axis_size(axis))])  8.91 us
    pallas_call x3, Pallas kernels, weight_part(): pl.pallas_call(functools.partial(weight_kernel, owners, at_once, len(grad...  4.52 us
  transfers between devices with their start and end apart: 20, of which 9 were waited for; matrix products, arithmetic and copies ran while one was open for 3% of the time, Pallas kernels for 5%

profile of v6, /device:TPU:0, one launch (start us, length us, event | category | flops | bytes accessed | tf_op | source)
XLA Modules:
  0.0 60.7 jit_solution(12118895098384711026)
XLA Ops:
  0.0 2.9 %collective-permute-start = (bf16[256,512]{1,0:T(8,128)(2,1)}, bf16[256,512]{1,0:T(8,128)(2,1)S(1)}, u32[]{:S(2)}, u32[]{:S(2)}) collective-permute-start(bf16[256,512]{1,0:T(8,128)(2,1)} %bitcast.12), channel_id=1, source_target_pairs={{0,8},{4,20},{8,0},{12,28},{16,24},{20,4},{24,16},{28,12},{1,9},{5... | collective-permute-start | bytes 786440 | tf_op jit(solution)/shard_map/ppermute | solution.py:51
  2.9 1.0 %pad_maximum_fusion.refs_1_ = bf16[256,768]{1,0:T(8,128)(2,1)S(1)} fusion(bf16[256,512]{1,0:T(8,128)(2,1)} %bitcast.15, bf16[256,128]{1,0:T(8,128)(2,1)} %bitcast.16, bf16[256,128]{1,0:T(8,128)(2,1)} %bitcast.17), kind=kLoop, calls=%fused_computation | loop fusion | flops 1179648 | bytes 786432 | tf_op jit(solution)/shard_map/concatenate | solution.py:370
  4.0 0.1 collective-permute-start.3
  4.0 0.8 %pad_add_fusion.refs_0_.meta = s32[34]{0:T(128)S(1)} fusion(s32[16]{0:T(128)} %bitcast.18, s32[16]{0:T(128)} %bitcast.19, s32[1]{0:T(128)} %bitcast.5, s32[1]{0:T(128)} %bitcast.4), kind=kLoop, calls=%fused_computation.1 | loop fusion | flops 102 | bytes 272 | tf_op jit(solution)/shard_map/concatenate | solution.py:366
  4.8 2.7 %collective-permute-done.refs_11_ = bf16[256,512]{1,0:T(8,128)(2,1)S(1)} collective-permute-done((bf16[256,512]{1,0:T(8,128)(2,1)}, bf16[256,512]{1,0:T(8,128)(2,1)S(1)}, u32[]{:S(2)}, u32[]{:S(2)}) %collective-permute-start) | collective-permute-done | bytes 262176 | tf_op jit(solution)/shard_map/ppermute | solution.py:51
  7.5 2.1 %collective-permute-start.4 = (bf16[256,768]{1,0:T(8,128)(2,1)S(1)}, bf16[256,768]{1,0:T(8,128)(2,1)S(1)}, u32[]{:S(2)}, u32[]{:S(2)}) collective-permute-start(bf16[256,768]{1,0:T(8,128)(2,1)S(1)} %pad_maximum_fusion.refs_1_), channel_id=1, source_target_pairs={{0,16},{4,12},{8,24},{12,4},{16,0},{20,28},{24,8},{28,20},{1,17},{... | collective-permute-start | bytes 1179656 | tf_op jit(solution)/shard_map/ppermute | solution.py:51
  9.6 0.0 copy-start.1
  9.6 0.9 %copy-done.1 = bf16[1,256,512]{2,1,0:T(8,128)(2,1)S(1)} copy-done((bf16[1,256,512]{2,1,0:T(8,128)(2,1)S(1)}, bf16[1,256,512]{2,1,0:T(8,128)(2,1)}, u32[]{:S(2)}) %copy-start.1) | copy-done | bytes 262168
  10.5 0.0 copy-start
  10.5 0.1 collective-permute-start.6
  10.6 0.2 collective-permute-start.1
  10.8 1.5 %collective-permute-start.7 = (bf16[256,512]{1,0:T(8,128)(2,1)S(1)}, bf16[256,512]{1,0:T(8,128)(2,1)S(1)}, u32[]{:S(2)}, u32[]{:S(2)}) collective-permute-start(bf16[256,512]{1,0:T(8,128)(2,1)S(1)} %collective-permute-done.refs_11_), channel_id=1, source_target_pairs={{0,4},{4,0},{8,12},{12,8},{16,20},{20,16},{24,28},{28,24},{1,5},{5... | collective-permute-start | bytes 786440 | tf_op jit(solution)/shard_map/ppermute | solution.py:39
  12.3 1.8 %collective-permute-done.3.refs_3_ = bf16[256,768]{1,0:T(8,128)(2,1)S(1)} collective-permute-done((bf16[256,768]{1,0:T(8,128)(2,1)S(1)}, bf16[256,768]{1,0:T(8,128)(2,1)S(1)}, u32[]{:S(2)}, u32[]{:S(2)}) %collective-permute-start.3) | collective-permute-done | bytes 393248 | tf_op jit(solution)/shard_map/ppermute | solution.py:51
  14.2 2.2 %collective-permute-start.2 = (bf16[256,512]{1,0:T(8,128)(2,1)S(1)}, bf16[256,512]{1,0:T(8,128)(2,1)S(1)}, u32[]{:S(2)}, u32[]{:S(2)}) collective-permute-start(bf16[256,512]{1,0:T(8,128)(2,1)S(1)} %collective-permute-done.refs_11_), channel_id=1, source_target_pairs={{0,16},{4,12},{8,24},{12,4},{16,0},{20,28},{24,8},{28,20},{1,17},{... | collective-permute-start | bytes 786440 | tf_op jit(solution)/shard_map/ppermute | solution.py:51
  16.3 0.0 collective-permute-done.6.refs_10_
  16.3 0.0 collective-permute-start.9
  16.3 1.8 %collective-permute-done.1.refs_13_ = bf16[256,512]{1,0:T(8,128)(2,1)S(1)} collective-permute-done((bf16[256,512]{1,0:T(8,128)(2,1)S(1)}, bf16[256,512]{1,0:T(8,128)(2,1)S(1)}, u32[]{:S(2)}, u32[]{:S(2)}) %collective-permute-start.1) | collective-permute-done | bytes 262176 | tf_op jit(solution)/shard_map/ppermute | solution.py:51
  18.1 0.8 %collective-permute-start.10 = (bf16[256,768]{1,0:T(8,128)(2,1)S(1)}, bf16[256,768]{1,0:T(8,128)(2,1)S(1)}, u32[]{:S(2)}, u32[]{:S(2)}) collective-permute-start(bf16[256,768]{1,0:T(8,128)(2,1)S(1)} %collective-permute-done.3.refs_3_), channel_id=1, source_target_pairs={{0,4},{4,0},{8,12},{12,8},{16,20},{20,16},{24,28},{28,24},{1,5},{5... | collective-permute-start | bytes 1179656 | tf_op jit(solution)/shard_map/ppermute | solution.py:39
  18.9 0.0 collective-permute-done.7.refs_12_
  18.9 2.0 %collective-permute-start.5 = (bf16[256,768]{1,0:T(8,128)(2,1)S(1)}, bf16[256,768]{1,0:T(8,128)(2,1)S(1)}, u32[]{:S(2)}, u32[]{:S(2)}) collective-permute-start(bf16[256,768]{1,0:T(8,128)(2,1)S(1)} %collective-permute-done.3.refs_3_), channel_id=1, source_target_pairs={{0,16},{4,12},{8,24},{12,4},{16,0},{20,28},{24,8},{28,20},{1,17},{... | collective-permute-start | bytes 1179656 | tf_op jit(solution)/shard_map/ppermute | solution.py:51
  20.9 0.0 collective-permute-done.4.refs_5_
  20.9 0.0 collective-permute-start.11
  20.9 0.0 collective-permute-done.2.refs_15_
  20.9 0.5 collective-permute-start.8
  21.5 0.0 collective-permute-done.9.refs_2_
  21.5 1.5 %collective-permute-done.8.refs_14_ = bf16[256,512]{1,0:T(8,128)(2,1)S(1)} collective-permute-done((bf16[256,512]{1,0:T(8,128)(2,1)S(1)}, bf16[256,512]{1,0:T(8,128)(2,1)S(1)}, u32[]{:S(2)}, u32[]{:S(2)}) %collective-permute-start.8) | collective-permute-done | bytes 262176 | tf_op jit(solution)/shard_map/ppermute | solution.py:39
  23.0 0.0 collective-permute-done.10.refs_4_
  23.0 3.7 %collective-permute-done.5.refs_7_ = bf16[256,768]{1,0:T(8,128)(2,1)S(1)} collective-permute-done((bf16[256,768]{1,0:T(8,128)(2,1)S(1)}, bf16[256,768]{1,0:T(8,128)(2,1)S(1)}, u32[]{:S(2)}, u32[]{:S(2)}) %collective-permute-start.5) | collective-permute-done | bytes 393248 | tf_op jit(solution)/shard_map/ppermute | solution.py:51
  26.7 0.0 collective-permute-done.11.refs_6_
  26.7 0.0 collective-permute-start.12
  26.7 0.5 collective-permute-start.13
  27.2 1.6 %collective-permute-done.13.refs_16_ = bf16[256,512]{1,0:T(8,128)(2,1)S(1)} collective-permute-done((bf16[256,512]{1,0:T(8,128)(2,1)S(1)}, bf16[256,512]{1,0:T(8,128)(2,1)S(1)}, u32[]{:S(2)}, u32[]{:S(2)}) %collective-permute-start.13) | collective-permute-done | bytes 262176 | tf_op jit(solution)/shard_map/ppermute | solution.py:39
  28.8 0.0 collective-permute-done.12.refs_8_
  28.8 9.4 %attention.1 = (bf16[2048,256]{1,0:T(8,128)(2,1)S(1)}, bf16[2048,256]{1,0:T(8,128)(2,1)S(1)}, bf16[2048,128]{1,0:T(8,128)(2,1)S(1)}, bf16[2048,128]{1,0:T(8,128)(2,1)S(1)}) custom-call(s32[34]{0:T(128)S(1)} %pad_add_fusion.refs_0_.meta, bf16[256,768]{1,0:T(8,128)(2,1)S(1)} %pad_maximum_fusion.refs_1_, bf16[256,768]{1,0:T(8,128)(2,1)S(1)} %collective-permute-done.9.refs_2_, ...), custom_call_target="tpu_custom_call" | custom-call | flops 2684354560 | bytes 6291456 | tf_op jit(solution)/shard_map/attention/pallas_call | solution.py:234
  38.2 0.0 copy-done
  38.2 1.3 %weight_part.3 = (f32[256,256]{1,0:T(8,128)S(1)}, bf16[256,256]{1,0:T(8,128)(2,1)S(1)}) custom-call(s32[34]{0:T(128)S(1)} %pad_add_fusion.refs_0_.meta, bf16[2048,512]{1,0:T(8,128)(2,1)S(1)} %bitcast.9, bf16[2048,256]{1,0:T(8,128)(2,1)S(1)} %get-tuple-element.57.refs_0_), custom_call_target="tpu_custom_call" | custom-call | flops 536870912 | bytes 3145728 | tf_op jit(solution)/shard_map/weight_part/pallas_call | solution.py:282
  39.5 2.6 %collective-permute-start.14 = (bf16[256,256]{1,0:T(8,128)(2,1)S(1)}, bf16[256,256]{1,0:T(8,128)(2,1)S(1)}, u32[]{:S(2)}, u32[]{:S(2)}) collective-permute-start(bf16[256,256]{1,0:T(8,128)(2,1)S(1)} %get-tuple-element.59), channel_id=1, source_target_pairs={{0,1},{1,0},{2,3},{3,2},{4,5},{5,4},{6,7},{7,6},{8,9},{9,8},{10,11... | collective-permute-start | bytes 393224 | tf_op jit(solution)/shard_map/ppermute | solution.py:39
  42.1 1.3 %weight_part.4 = (f32[256,256]{1,0:T(8,128)S(1)}, bf16[256,256]{1,0:T(8,128)(2,1)S(1)}) custom-call(s32[34]{0:T(128)S(1)} %pad_add_fusion.refs_0_.meta, bf16[2048,512]{1,0:T(8,128)(2,1)S(1)} %bitcast.10, bf16[2048,256]{1,0:T(8,128)(2,1)S(1)} %get-tuple-element.62.refs_0_), custom_call_target="tpu_custom_call" | custom-call | flops 536870912 | bytes 3145728 | tf_op jit(solution)/shard_map/weight_part/pallas_call | solution.py:282
  43.4 0.1 collective-permute-start.16
  43.5 1.9 %weight_part.5 = (f32[256,256]{1,0:T(8,128)S(1)}, bf16[256,256]{1,0:T(8,128)(2,1)S(1)}) custom-call(s32[34]{0:T(128)S(1)} %pad_add_fusion.refs_0_.meta, bf16[2048,512]{1,0:T(8,128)(2,1)S(1)} %bitcast.11, bf16[2048,128]{1,0:T(8,128)(2,1)S(1)} %get-tuple-element.67.refs_0_, bf16[2048,128]{1,0:T(8,128)(2,1)S(1)} %get-tuple-element.68.refs_1_), custom_call_target="tpu_custom_call" | custom-call | flops 536870912 | bytes 3145728 | tf_op jit(solution)/shard_map/weight_part/pallas_call | solution.py:282
  45.4 2.1 %collective-permute-start.18 = (bf16[256,256]{1,0:T(8,128)(2,1)S(1)}, bf16[256,256]{1,0:T(8,128)(2,1)S(1)}, u32[]{:S(2)}, u32[]{:S(2)}) collective-permute-start(bf16[256,256]{1,0:T(8,128)(2,1)S(1)} %get-tuple-element.70), channel_id=1, source_target_pairs={{0,1},{1,0},{2,3},{3,2},{4,5},{5,4},{6,7},{7,6},{8,9},{9,8},{10,11... | collective-permute-start | bytes 393224 | tf_op jit(solution)/shard_map/ppermute | solution.py:39
  47.5 0.0 collective-permute-done.14.arrived_ref
  47.5 2.6 %collective-permute-start.15 = (bf16[128,256]{1,0:T(8,128)(2,1)S(1)}, bf16[128,256]{1,0:T(8,128)(2,1)S(1)}, u32[]{:S(2)}, u32[]{:S(2)}) collective-permute-start(bf16[128,256]{1,0:T(8,128)(2,1)S(1)} %get-tuple-element.61), channel_id=1, source_target_pairs={{0,2},{1,3},{2,0},{3,1},{4,6},{5,7},{6,4},{7,5},{8,10},{9,11},{10,... | collective-permute-start | bytes 196616 | tf_op jit(solution)/shard_map/ppermute | solution.py:39
  50.2 0.0 collective-permute-done.16.arrived_ref
  50.2 2.0 %collective-permute-start.17 = (bf16[128,256]{1,0:T(8,128)(2,1)S(1)}, bf16[128,256]{1,0:T(8,128)(2,1)S(1)}, u32[]{:S(2)}, u32[]{:S(2)}) collective-permute-start(bf16[128,256]{1,0:T(8,128)(2,1)S(1)} %get-tuple-element.66), channel_id=1, source_target_pairs={{0,2},{1,3},{2,0},{3,1},{4,6},{5,7},{6,4},{7,5},{8,10},{9,11},{10,... | collective-permute-start | bytes 196616 | tf_op jit(solution)/shard_map/ppermute | solution.py:39
  52.3 0.9 %collective-permute-done.18.arrived_ref = bf16[256,256]{1,0:T(8,128)(2,1)S(1)} collective-permute-done((bf16[256,256]{1,0:T(8,128)(2,1)S(1)}, bf16[256,256]{1,0:T(8,128)(2,1)S(1)}, u32[]{:S(2)}, u32[]{:S(2)}) %collective-permute-start.18) | collective-permute-done | bytes 131104 | tf_op jit(solution)/shard_map/ppermute | solution.py:39
  53.2 1.9 %collective-permute-start.19 = (bf16[128,256]{1,0:T(8,128)(2,1)S(1)}, bf16[128,256]{1,0:T(8,128)(2,1)S(1)}, u32[]{:S(2)}, u32[]{:S(2)}) collective-permute-start(bf16[128,256]{1,0:T(8,128)(2,1)S(1)} %get-tuple-element.72), channel_id=1, source_target_pairs={{0,2},{1,3},{2,0},{3,1},{4,6},{5,7},{6,4},{7,5},{8,10},{9,11},{10,... | collective-permute-start | bytes 196616 | tf_op jit(solution)/shard_map/ppermute | solution.py:39
  55.1 0.0 collective-permute-done.15.refs_1_
  55.1 3.4 %collective-permute-done.17.refs_3_ = bf16[128,256]{1,0:T(8,128)(2,1)S(1)} collective-permute-done((bf16[128,256]{1,0:T(8,128)(2,1)S(1)}, bf16[128,256]{1,0:T(8,128)(2,1)S(1)}, u32[]{:S(2)}, u32[]{:S(2)}) %collective-permute-start.17) | collective-permute-done | bytes 65568 | tf_op jit(solution)/shard_map/ppermute | solution.py:39
  58.5 1.4 %collective-permute-done.19.refs_5_ = bf16[128,256]{1,0:T(8,128)(2,1)S(1)} collective-permute-done((bf16[128,256]{1,0:T(8,128)(2,1)S(1)}, bf16[128,256]{1,0:T(8,128)(2,1)S(1)}, u32[]{:S(2)}, u32[]{:S(2)}) %collective-permute-start.19) | collective-permute-done | bytes 65568 | tf_op jit(solution)/shard_map/ppermute | solution.py:39
  59.9 0.8 %final_sum.1 = f32[128,768]{1,0:T(8,128)} custom-call(f32[128,256]{1,0:T(8,128)S(1)} %get-tuple-element.60.refs_0_, bf16[128,256]{1,0:T(8,128)(2,1)S(1)} %collective-permute-done.15.refs_1_, f32[128,256]{1,0:T(8,128)S(1)} %get-tuple-element.65.refs_2_, bf16[128,256]{1,0:T(8,128)(2,1)S(1)} %collective-permute-done.17.refs_3_, ...), custom_call_target="tpu_custom_call" | custom-call | tf_op jit(solution)/shard_map/final_sum/pallas_call | solution.py:339
  (4 shorter events, 0.1 us)
Async XLA Ops:
  0.0 7.5 %collective-permute-start = (bf16[256,512]{1,0:T(8,128)(2,1)}, bf16[256,512]{1,0:T(8,128)(2,1)S(1)}, u32[]{:S(2)}, u32[]{:S(2)}) collective-permute-start(bf16[256,512]{1,0:T(8,128)(2,1)} %bitcast.12), channel_id=1, source_target_pairs={{0,8},{4,20},{8,0},{12,28},{16,24},{20,4},{24,16},{28,12},{1,9},{5... | collective-permute-start | bytes 786440 | tf_op jit(solution)/shard_map/ppermute | solution.py:51
  4.0 10.2 %collective-permute-start.3 = (bf16[256,768]{1,0:T(8,128)(2,1)S(1)}, bf16[256,768]{1,0:T(8,128)(2,1)S(1)}, u32[]{:S(2)}, u32[]{:S(2)}) collective-permute-start(bf16[256,768]{1,0:T(8,128)(2,1)S(1)} %pad_maximum_fusion.refs_1_), channel_id=1, source_target_pairs={{0,8},{4,20},{8,0},{12,28},{16,24},{20,4},{24,16},{28,12},{1,9},{5... | collective-permute-start | bytes 1179656 | tf_op jit(solution)/shard_map/ppermute | solution.py:51
  7.5 13.4 %collective-permute-start.4 = (bf16[256,768]{1,0:T(8,128)(2,1)S(1)}, bf16[256,768]{1,0:T(8,128)(2,1)S(1)}, u32[]{:S(2)}, u32[]{:S(2)}) collective-permute-start(bf16[256,768]{1,0:T(8,128)(2,1)S(1)} %pad_maximum_fusion.refs_1_), channel_id=1, source_target_pairs={{0,16},{4,12},{8,24},{12,4},{16,0},{20,28},{24,8},{28,20},{1,17},{... | collective-permute-start | bytes 1179656 | tf_op jit(solution)/shard_map/ppermute | solution.py:51
  9.6 0.9 %copy-start.1 = (bf16[1,256,512]{2,1,0:T(8,128)(2,1)S(1)}, bf16[1,256,512]{2,1,0:T(8,128)(2,1)}, u32[]{:S(2)}) copy-start(bf16[1,256,512]{2,1,0:T(8,128)(2,1)} %param.11) | copy-start | bytes 786436
  10.5 27.7 %copy-start = (bf16[1,2048,512]{2,1,0:T(8,128)(2,1)S(1)}, bf16[1,2048,512]{2,1,0:T(8,128)(2,1)}, u32[]{:S(2)}) copy-start(bf16[1,2048,512]{2,1,0:T(8,128)(2,1)} %param.7) | copy-start | bytes 6291460
  10.5 5.8 %collective-permute-start.6 = (bf16[256,512]{1,0:T(8,128)(2,1)S(1)}, bf16[256,512]{1,0:T(8,128)(2,1)S(1)}, u32[]{:S(2)}, u32[]{:S(2)}) collective-permute-start(bf16[256,512]{1,0:T(8,128)(2,1)S(1)} %held.1.refs_9_), channel_id=1, source_target_pairs={{0,4},{4,0},{8,12},{12,8},{16,20},{20,16},{24,28},{28,24},{1,5},{5... | collective-permute-start | bytes 786440 | tf_op jit(solution)/shard_map/ppermute | solution.py:39
  10.6 7.5 %collective-permute-start.1 = (bf16[256,512]{1,0:T(8,128)(2,1)S(1)}, bf16[256,512]{1,0:T(8,128)(2,1)S(1)}, u32[]{:S(2)}, u32[]{:S(2)}) collective-permute-start(bf16[256,512]{1,0:T(8,128)(2,1)S(1)} %bitcast.14), channel_id=1, source_target_pairs={{0,16},{4,12},{8,24},{12,4},{16,0},{20,28},{24,8},{28,20},{1,17},{... | collective-permute-start | bytes 786440 | tf_op jit(solution)/shard_map/ppermute | solution.py:51
  10.8 8.2 %collective-permute-start.7 = (bf16[256,512]{1,0:T(8,128)(2,1)S(1)}, bf16[256,512]{1,0:T(8,128)(2,1)S(1)}, u32[]{:S(2)}, u32[]{:S(2)}) collective-permute-start(bf16[256,512]{1,0:T(8,128)(2,1)S(1)} %collective-permute-done.refs_11_), channel_id=1, source_target_pairs={{0,4},{4,0},{8,12},{12,8},{16,20},{20,16},{24,28},{28,24},{1,5},{5... | collective-permute-start | bytes 786440 | tf_op jit(solution)/shard_map/ppermute | solution.py:39
  14.2 6.8 %collective-permute-start.2 = (bf16[256,512]{1,0:T(8,128)(2,1)S(1)}, bf16[256,512]{1,0:T(8,128)(2,1)S(1)}, u32[]{:S(2)}, u32[]{:S(2)}) collective-permute-start(bf16[256,512]{1,0:T(8,128)(2,1)S(1)} %collective-permute-done.refs_11_), channel_id=1, source_target_pairs={{0,16},{4,12},{8,24},{12,4},{16,0},{20,28},{24,8},{28,20},{1,17},{... | collective-permute-start | bytes 786440 | tf_op jit(solution)/shard_map/ppermute | solution.py:51
  16.3 5.1 %collective-permute-start.9 = (bf16[256,768]{1,0:T(8,128)(2,1)S(1)}, bf16[256,768]{1,0:T(8,128)(2,1)S(1)}, u32[]{:S(2)}, u32[]{:S(2)}) collective-permute-start(bf16[256,768]{1,0:T(8,128)(2,1)S(1)} %pad_maximum_fusion.refs_1_), channel_id=1, source_target_pairs={{0,4},{4,0},{8,12},{12,8},{16,20},{20,16},{24,28},{28,24},{1,5},{5... | collective-permute-start | bytes 1179656 | tf_op jit(solution)/shard_map/ppermute | solution.py:39
  18.1 4.9 %collective-permute-start.10 = (bf16[256,768]{1,0:T(8,128)(2,1)S(1)}, bf16[256,768]{1,0:T(8,128)(2,1)S(1)}, u32[]{:S(2)}, u32[]{:S(2)}) collective-permute-start(bf16[256,768]{1,0:T(8,128)(2,1)S(1)} %collective-permute-done.3.refs_3_), channel_id=1, source_target_pairs={{0,4},{4,0},{8,12},{12,8},{16,20},{20,16},{24,28},{28,24},{1,5},{5... | collective-permute-start | bytes 1179656 | tf_op jit(solution)/shard_map/ppermute | solution.py:39
  18.9 7.8 %collective-permute-start.5 = (bf16[256,768]{1,0:T(8,128)(2,1)S(1)}, bf16[256,768]{1,0:T(8,128)(2,1)S(1)}, u32[]{:S(2)}, u32[]{:S(2)}) collective-permute-start(bf16[256,768]{1,0:T(8,128)(2,1)S(1)} %collective-permute-done.3.refs_3_), channel_id=1, source_target_pairs={{0,16},{4,12},{8,24},{12,4},{16,0},{20,28},{24,8},{28,20},{1,17},{... | collective-permute-start | bytes 1179656 | tf_op jit(solution)/shard_map/ppermute | solution.py:51
  20.9 5.8 %collective-permute-start.11 = (bf16[256,768]{1,0:T(8,128)(2,1)S(1)}, bf16[256,768]{1,0:T(8,128)(2,1)S(1)}, u32[]{:S(2)}, u32[]{:S(2)}) collective-permute-start(bf16[256,768]{1,0:T(8,128)(2,1)S(1)} %collective-permute-done.4.refs_5_), channel_id=1, source_target_pairs={{0,4},{4,0},{8,12},{12,8},{16,20},{20,16},{24,28},{28,24},{1,5},{5... | collective-permute-start | bytes 1179656 | tf_op jit(solution)/shard_map/ppermute | solution.py:39
  20.9 2.1 %collective-permute-start.8 = (bf16[256,512]{1,0:T(8,128)(2,1)S(1)}, bf16[256,512]{1,0:T(8,128)(2,1)S(1)}, u32[]{:S(2)}, u32[]{:S(2)}) collective-permute-start(bf16[256,512]{1,0:T(8,128)(2,1)S(1)} %collective-permute-done.1.refs_13_), channel_id=1, source_target_pairs={{0,4},{4,0},{8,12},{12,8},{16,20},{20,16},{24,28},{28,24},{1,5},{5... | collective-permute-start | bytes 786440 | tf_op jit(solution)/shard_map/ppermute | solution.py:39
  26.7 2.1 %collective-permute-start.12 = (bf16[256,768]{1,0:T(8,128)(2,1)S(1)}, bf16[256,768]{1,0:T(8,128)(2,1)S(1)}, u32[]{:S(2)}, u32[]{:S(2)}) collective-permute-start(bf16[256,768]{1,0:T(8,128)(2,1)S(1)} %collective-permute-done.5.refs_7_), channel_id=1, source_target_pairs={{0,4},{4,0},{8,12},{12,8},{16,20},{20,16},{24,28},{28,24},{1,5},{5... | collective-permute-start | bytes 1179656 | tf_op jit(solution)/shard_map/ppermute | solution.py:39
  26.7 2.1 %collective-permute-start.13 = (bf16[256,512]{1,0:T(8,128)(2,1)S(1)}, bf16[256,512]{1,0:T(8,128)(2,1)S(1)}, u32[]{:S(2)}, u32[]{:S(2)}) collective-permute-start(bf16[256,512]{1,0:T(8,128)(2,1)S(1)} %collective-permute-done.2.refs_15_), channel_id=1, source_target_pairs={{0,4},{4,0},{8,12},{12,8},{16,20},{20,16},{24,28},{28,24},{1,5},{5... | collective-permute-start | bytes 786440 | tf_op jit(solution)/shard_map/ppermute | solution.py:39
  39.5 8.0 %collective-permute-start.14 = (bf16[256,256]{1,0:T(8,128)(2,1)S(1)}, bf16[256,256]{1,0:T(8,128)(2,1)S(1)}, u32[]{:S(2)}, u32[]{:S(2)}) collective-permute-start(bf16[256,256]{1,0:T(8,128)(2,1)S(1)} %get-tuple-element.59), channel_id=1, source_target_pairs={{0,1},{1,0},{2,3},{3,2},{4,5},{5,4},{6,7},{7,6},{8,9},{9,8},{10,11... | collective-permute-start | bytes 393224 | tf_op jit(solution)/shard_map/ppermute | solution.py:39
  43.4 6.7 %collective-permute-start.16 = (bf16[256,256]{1,0:T(8,128)(2,1)S(1)}, bf16[256,256]{1,0:T(8,128)(2,1)S(1)}, u32[]{:S(2)}, u32[]{:S(2)}) collective-permute-start(bf16[256,256]{1,0:T(8,128)(2,1)S(1)} %get-tuple-element.64), channel_id=1, source_target_pairs={{0,1},{1,0},{2,3},{3,2},{4,5},{5,4},{6,7},{7,6},{8,9},{9,8},{10,11... | collective-permute-start | bytes 393224 | tf_op jit(solution)/shard_map/ppermute | solution.py:39
  45.4 7.7 %collective-permute-start.18 = (bf16[256,256]{1,0:T(8,128)(2,1)S(1)}, bf16[256,256]{1,0:T(8,128)(2,1)S(1)}, u32[]{:S(2)}, u32[]{:S(2)}) collective-permute-start(bf16[256,256]{1,0:T(8,128)(2,1)S(1)} %get-tuple-element.70), channel_id=1, source_target_pairs={{0,1},{1,0},{2,3},{3,2},{4,5},{5,4},{6,7},{7,6},{8,9},{9,8},{10,11... | collective-permute-start | bytes 393224 | tf_op jit(solution)/shard_map/ppermute | solution.py:39
  47.5 7.5 %collective-permute-start.15 = (bf16[128,256]{1,0:T(8,128)(2,1)S(1)}, bf16[128,256]{1,0:T(8,128)(2,1)S(1)}, u32[]{:S(2)}, u32[]{:S(2)}) collective-permute-start(bf16[128,256]{1,0:T(8,128)(2,1)S(1)} %get-tuple-element.61), channel_id=1, source_target_pairs={{0,2},{1,3},{2,0},{3,1},{4,6},{5,7},{6,4},{7,5},{8,10},{9,11},{10,... | collective-permute-start | bytes 196616 | tf_op jit(solution)/shard_map/ppermute | solution.py:39
  50.2 8.3 %collective-permute-start.17 = (bf16[128,256]{1,0:T(8,128)(2,1)S(1)}, bf16[128,256]{1,0:T(8,128)(2,1)S(1)}, u32[]{:S(2)}, u32[]{:S(2)}) collective-permute-start(bf16[128,256]{1,0:T(8,128)(2,1)S(1)} %get-tuple-element.66), channel_id=1, source_target_pairs={{0,2},{1,3},{2,0},{3,1},{4,6},{5,7},{6,4},{7,5},{8,10},{9,11},{10,... | collective-permute-start | bytes 196616 | tf_op jit(solution)/shard_map/ppermute | solution.py:39
  53.2 6.7 %collective-permute-start.19 = (bf16[128,256]{1,0:T(8,128)(2,1)S(1)}, bf16[128,256]{1,0:T(8,128)(2,1)S(1)}, u32[]{:S(2)}, u32[]{:S(2)}) collective-permute-start(bf16[128,256]{1,0:T(8,128)(2,1)S(1)} %get-tuple-element.72), channel_id=1, source_target_pairs={{0,2},{1,3},{2,0},{3,1},{4,6},{5,7},{6,4},{7,5},{8,10},{9,11},{10,... | collective-permute-start | bytes 196616 | tf_op jit(solution)/shard_map/ppermute | solution.py:39
